TPU v7x, 32 devices: a whole 2x2x4 slice. The times are simulated.
32 devices in a mesh: space: 8 (over y, x, core), var: 4 (over z).
Axes of the slice: x: 2, y: 2, z: 4, core: 2. Of those that a mesh axis runs over, the one named last changes fastest.
Arguments:
- var_tokens: bfloat16 [16, 1024, 1024], P('var', 'space'), may hold values from -6 to 6
- key_query: bfloat16 [1024, 16], replicated
- value_weight: bfloat16 [1024, 1024], replicated, may hold values from -0.1875 to 0.1875
- qkv_weight: bfloat16 [1024, 3, 1024], P(None, None, 'var')
- out_weight: bfloat16 [1024, 1024], P('var'), may hold values from -0.1875 to 0.1875
- up_weight: bfloat16 [1024, 4096], P(None, 'var'), may hold values from -0.1875 to 0.1875
- down_weight: bfloat16 [4096, 1024], P('var'), may hold values from -0.09375 to 0.09375
- norm_gain: bfloat16 [1024], replicated, may hold values from 0.25 to 1.75
Outputs:
- block_out: bfloat16 [1024, 1024], P(('space', 'var'))
All inputs are finite; a program needn't handle non-finite values.
Results may differ from a plain program's by a relative error of at most 0.018.
Values may be sent and summed in bfloat16 or wider, within the bound.
No kernel may reach another device: no remote copies, remote signals or barrier semaphores. Data moves between devices by JAX's collectives and lax.ppermute only.
A program may use at most 64 MiB of HBM per device.

v0:
```python
import jax
import jax.numpy as jnp
from jax import lax
from jax.sharding import PartitionSpec as P

H = 16


def per_device(
    var_tokens, key_query, value_weight, qkv_weight, out_weight, up_weight, down_weight, norm_gain
):
    f32 = jnp.float32
    bf16 = jnp.bfloat16
    groups = lax.axis_size("var")
    local_vars, seq_rows, feat_width = var_tokens.shape
    head_dim = feat_width // H
    local_heads = H // groups
    scores = jnp.einsum("vsd,dh->vsh", var_tokens, key_query, preferred_element_type=f32)
    values = jnp.einsum("vsd,de->vse", var_tokens, value_weight, preferred_element_type=f32).astype(
        bf16
    )
    values = values.reshape(local_vars, seq_rows, H, head_dim)
    top_score = lax.pmax(jnp.max(scores, axis=0), "var")
    exp_terms = jnp.exp(scores - top_score[None])
    weight_sum = jnp.sum(exp_terms, axis=0)
    numerator = jnp.einsum(
        "vsh,vshe->she", exp_terms.astype(bf16), values, preferred_element_type=f32
    )
    numerator = numerator.reshape(seq_rows, feat_width)
    numer_part, total_part = (
        lax.psum_scatter(numerator, "var", scatter_dimension=1, tiled=True),
        lax.psum_scatter(weight_sum, "var", scatter_dimension=1, tiled=True),
    )
    pooled = numer_part.reshape(seq_rows, local_heads, head_dim) / total_part[..., None]
    pooled = pooled.reshape(seq_rows, local_heads * head_dim).astype(bf16)
    all_features = lax.all_gather(pooled, "var", axis=1, tiled=True)
    pooled_f = all_features.astype(f32)
    mean_row = jnp.mean(pooled_f, axis=1, keepdims=True)
    centered = pooled_f - mean_row
    spread = jnp.mean(centered * centered, axis=1, keepdims=True)
    normed = (centered * lax.rsqrt(spread + 1e-05) * norm_gain.astype(f32)).astype(bf16)
    qkv = jnp.einsum("sd,dcj->scj", normed, qkv_weight, preferred_element_type=f32).astype(bf16)
    query_rows = qkv[:, 0].reshape(seq_rows, local_heads, head_dim)
    key_local = qkv[:, 1]
    value_local = qkv[:, 2]
    scale_attn = head_dim ** (-0.5)
    run_max = jnp.full((local_heads, seq_rows), -jnp.inf, f32)
    run_sum = jnp.zeros((local_heads, seq_rows), f32)
    run_acc = jnp.zeros((local_heads, seq_rows, head_dim), f32)
    key_block = lax.all_gather(key_local, "space", axis=0, tiled=True)
    value_block = lax.all_gather(value_local, "space", axis=0, tiled=True)
    key_rows = key_block.reshape(-1, local_heads, head_dim)
    value_rows = value_block.reshape(-1, local_heads, head_dim)
    logits = (
        jnp.einsum("shd,rhd->hsr", query_rows, key_rows, preferred_element_type=f32) * scale_attn
    )
    new_max = jnp.max(logits, axis=2)
    rescale = jnp.exp(run_max - new_max)
    exp_terms = jnp.exp(logits - new_max[..., None])
    new_sum = run_sum * rescale + jnp.sum(exp_terms, axis=2)
    update = jnp.einsum(
        "hsr,rhd->hsd", exp_terms.astype(bf16), value_rows, preferred_element_type=f32
    )
    final_acc = run_acc * rescale[..., None] + update
    attended = (
        (final_acc / new_sum[..., None])
        .transpose(1, 0, 2)
        .reshape(seq_rows, local_heads * head_dim)
        .astype(bf16)
    )
    hidden = jax.nn.gelu(
        jnp.dot(normed, up_weight, preferred_element_type=f32), approximate=True
    ).astype(bf16)
    rows_out = seq_rows // groups
    summed = lax.psum_scatter(
        (
            jnp.dot(attended, out_weight, preferred_element_type=f32)
            + jnp.dot(hidden, down_weight, preferred_element_type=f32)
        ).astype(jnp.bfloat16),
        "var",
        scatter_dimension=0,
        tiled=True,
    ).astype(jnp.float32)
    residual_rows = lax.dynamic_slice_in_dim(
        pooled_f, lax.axis_index("var") * rows_out, rows_out, 0
    )
    return (summed + residual_rows).astype(bf16)


def solution(mesh):
    placed = (
        P("var", "space", None),
        P(),
        P(),
        P(None, None, "var"),
        P("var", None),
        P(None, "var"),
        P("var", None),
        P(),
    )
    return jax.shard_map(
        per_device, mesh=mesh, in_specs=placed, out_specs=P(("space", "var"), None), check_vma=False
    )
```

profile of v0, /device:TPU:0, one launch (start us, length us, event | category | flops | bytes accessed | tf_op | source)
XLA Modules:
  0.0 123.2 jit_solution(10132563980585776142)
XLA Ops:
  6.5 0.0 copy-start
  6.5 0.0 reduce-scatter.3.cloned.1.call-start
  6.5 1.8 %fusion.41 = (f32[128,16]{0,1:T(8,128)S(1)}, f32[4,128,16]{1,2,0:T(8,128)S(1)}) fusion(bf16[4,128,1024]{2,1,0:T(8,128)(2,1)} %param.8, bf16[1024,16]{0,1:T(8,128)(2,1)} %param.9), kind=kOutput, calls=%fused_computation.55 | convolution fusion | flops 16783360 | bytes 1122304 | tf_op jit(solution)/shard_map/vsd,dh->vsh/dot_general | solution.py:18
  8.3 13.7 %pmax.7 = f32[128,16]{0,1:T(8,128)S(1)} all-reduce(f32[128,16]{0,1:T(8,128)S(1)} %get-tuple-element.10), channel_id=1, replica_groups=mesh['space'=8,'var'=4] {'var'}, use_global_device_ids=true, to_apply=%region_1.0 | all-reduce | flops 2048 | bytes 16384 | tf_op jit(solution)/shard_map/pmax | solution.py:23
  22.0 0.0 copy-done
  22.0 3.5 %fusion.4 = bf16[4,128,1024]{2,1,0:T(8,128)(2,1)} fusion(bf16[4,128,1024]{2,1,0:T(8,128)(2,1)} %param.8, bf16[1024,1024]{1,0:T(8,128)(2,1)S(1)} %copy-done), kind=kOutput, calls=%fused_computation.7 | convolution fusion | flops 1074266112 | bytes 4194304 | tf_op jit(solution)/shard_map/vsd,de->vse/dot_general | solution.py:19
  25.5 1.6 %copy.30 = bf16[4,128,1024]{1,2,0:T(8,128)(2,1)S(1)} copy(bf16[4,128,1024]{2,1,0:T(8,128)(2,1)} %fusion.4) | data formatting | bytes 2097152
  27.1 0.0 copy-start.4
  27.1 0.0 copy-start.3
  27.1 1.1 multiply_reduce_fusion
  28.2 2.0 %copy.19 = f32[128,1024]{1,0:T(8,128)} copy(f32[128,1024]{0,1:T(8,128)} %bitcast.53) | data formatting | bytes 1048576 | tf_op jit(solution)/shard_map/reshape | solution.py:29
  30.3 0.0 reduce-scatter.3.cloned.1.call-update
  30.3 0.0 reduce-scatter.5.cloned.1.call-start
  30.3 0.0 copy-done.4
  30.3 0.6 dynamic-slice
  31.6 8.5 %all-reduce = f32[128,16]{0,1:T(8,128)S(1)} all-reduce(f32[128,16]{0,1:T(8,128)S(1)} %get-tuple-element.8), channel_id=5, replica_groups=mesh['space'=8,'var'=4] {'var'}, use_global_device_ids=true, to_apply=%region_4.0.clone | all-reduce | flops 2048 | bytes 16384
  40.2 0.1 copy.20
  40.3 0.0 copy-done.3
  40.3 9.9 %reduce-scatter.3.cloned.1.call-done = f32[128,256]{1,0:T(8,128)} async-done(((f32[128,1024]{1,0:T(8,128)}), f32[128,256]{1,0:T(8,128)}) %reduce-scatter.3.cloned.1.call-update) | async-done | bytes 131088 | tf_op jit(solution)/shard_map/reduce_scatter | solution.py:31
  50.2 0.9 divide_convert_fusion
  51.1 14.1 %all_gather.9 = bf16[128,1024]{1,0:T(8,128)(2,1)S(1)} all-gather(bf16[128,256]{1,0:T(8,128)(2,1)S(1)} %divide_convert_fusion), channel_id=1, replica_groups=mesh['space'=8,'var'=4] {'var'}, dimensions={1}, use_global_device_ids=true | all-gather | bytes 327680 | tf_op jit(solution)/shard_map/all_gather | solution.py:36
  65.3 0.1 convert_reduce_fusion
  65.4 0.2 multiply_reduce_fusion.2
  65.6 1.8 %convolution_convert_fusion = bf16[128,3,256]{2,0,1:T(8,128)(2,1)S(1)} fusion(bf16[1024,3,256]{2,0,1:T(8,128)(2,1)} %param.11, bf16[128,1024]{1,0:T(8,128)(2,1)S(1)} %all_gather.9, f32[1024]{0:T(1024)S(1)} %convert_element_type.46, f32[128]{0:T(128)S(1)} %add_rsqrt_fusion, f32[128]{0:T(128)S(1)} %broadcast_multiply_fusion), kind=kOutput, calls=%fused_computation.10 | convolution fusion | flops 202080256 | bytes 2036736 | tf_op jit(solution)/shard_map/sd,dcj->scj/dot_general | solution.py:42
  67.5 10.0 %all-gather = bf16[1024,1,256]{2,0,1:T(8,128)(2,1)S(1)} all-gather(bf16[128,1,256]{2,0,1:T(8,128)(2,1)S(1)} %get-tuple-element.5), channel_id=2, replica_groups=mesh['space'=8,'var'=4] {'space'}, dimensions={0}, use_global_device_ids=true | all-gather | bytes 589824 | tf_op jit(solution)/shard_map/all_gather | solution.py:50
  77.5 0.2 copy.22
  77.7 0.1 copy.21
  77.8 0.6 multiply_reduce_fusion.1
  78.4 0.0 copy-start.1
  78.4 1.3 %copy-done.1 = f32[4,128,1024]{2,1,0:T(8,128)} copy-done((f32[4,128,1024]{2,1,0:T(8,128)}, f32[4,128,1024]{2,1,0:T(8,128)S(1)}, u32[]{:S(2)}) %copy-start.1) | copy-done | bytes 2097176
  79.7 0.5 fusion.2
  80.3 9.8 %all-gather.1 = bf16[1024,1,256]{2,0,1:T(8,128)(2,1)S(1)} all-gather(bf16[128,1,256]{2,0,1:T(8,128)(2,1)S(1)} %get-tuple-element.6), channel_id=3, replica_groups=mesh['space'=8,'var'=4] {'space'}, dimensions={0}, use_global_device_ids=true | all-gather | bytes 589824 | tf_op jit(solution)/shard_map/all_gather | solution.py:51
  90.1 0.0 copy-start.2
  90.1 1.0 copy.23
  91.1 2.3 %fusion.10 = bf16[128,4,64]{0,2,1:T(8,128)(2,1)S(1)} fusion(bf16[1024,4,64]{0,2,1:T(8,128)(2,1)} %bitcast.55, f32[4,128,1024]{2,1,0:T(8,128)} %copy-done.1, f32[4,128]{1,0:T(4,128)S(1)} %get-tuple-element.12, f32[128,4]{0,1:T(4,128)S(1)} %bitcast_add_fusion, f32[128,4]{0,1:T(4,128)S(1)} %multiply_bitcast_fusion), kind=kOutput, calls=%fused_computation.14 | convolution fusion | flops 68780032 | bytes 2693120 | tf_op jit(solution)/shard_map/hsr,rhd->hsd/dot_general | solution.py:61
  93.3 0.0 copy-done.2
  93.4 0.2 fusion.42
  93.6 3.8 %fusion.7 = bf16[128,1024]{1,0:T(8,128)(2,1)} fusion(f32[128,1024]{1,0:T(8,128)S(1)} %fusion.42, bf16[1024,1024]{1,0:T(8,128)(2,1)} %param.14, bf16[1024,1024]{1,0:T(8,128)(2,1)} %param.13, bf16[128,1024]{1,0:T(8,128)(2,1)S(1)} %all_gather.9, f32[1024]{0:T(1024)S(1)} %convert_element_type.46, f32[128]{0:T(128)S(1)} %add_rsqrt_fusion, ...), kind=kOutput, calls=%fused_computation.9 | convolution fusion | flops 538968064 | bytes 5248000 | tf_op jit(solution)/shard_map/dot_general | solution.py:78
  97.4 0.0 reduce-scatter.5.cloned.1.call-update
  97.5 17.3 %reduce-scatter.5.cloned.1.call-done = bf16[32,1024]{1,0:T(8,128)(2,1)} async-done(((bf16[128,1024]{1,0:T(8,128)(2,1)}), bf16[32,1024]{1,0:T(8,128)(2,1)}) %reduce-scatter.5.cloned.1.call-update) | async-done | bytes 65552 | tf_op jit(solution)/shard_map/reduce_scatter | solution.py:75
  114.8 1.5 %add_convert_fusion = bf16[32,1024]{1,0:T(8,128)(2,1)} fusion(f32[128,1024]{1,0:T(8,128)S(1)} %convert_element_type.45, s32[]{:T(128)S(6)} %select_n.3, bf16[32,1024]{1,0:T(8,128)(2,1)} %reduce-scatter.5.cloned.1.call-done), kind=kLoop, calls=%fused_computation.34 | loop fusion | flops 98304 | bytes 262148 | tf_op jit(solution)/shard_map/convert_element_type | solution.py:87
  (10 shorter events, 0.1 us)
Async XLA Ops:
  6.5 15.5 %copy-start = (bf16[1024,1024]{1,0:T(8,128)(2,1)S(1)}, bf16[1024,1024]{1,0:T(8,128)(2,1)}, u32[]{:S(2)}) copy-start(bf16[1024,1024]{1,0:T(8,128)(2,1)} %param.10) | copy-start | bytes 6291460
  6.5 43.7 %reduce-scatter.3.cloned.1.call-start = ((), (), s32[]{:S(2)}) async-start(), calls=%async_computation.2 | async-start | bytes 655360 | tf_op jit(solution)/shard_map/reduce_scatter | solution.py:31
  27.1 3.2 %copy-start.4 = (u32[32]{0:T(128)S(1)}, u32[32]{0:T(128)}, u32[]{:S(2)}) copy-start(u32[32]{0:T(128)} %constant.36) | copy-start | bytes 388
  27.1 13.2 %copy-start.3 = (bf16[1024]{0:T(1024)(128)(2,1)S(1)}, bf16[1024]{0:T(1024)(128)(2,1)}, u32[]{:S(2)}) copy-start(bf16[1024]{0:T(1024)(128)(2,1)} %param.15) | copy-start | bytes 6148
  30.3 84.5 %reduce-scatter.5.cloned.1.call-start = ((), (), s32[]{:S(2)}) async-start(), calls=%async_computation.3 | async-start | bytes 327680 | tf_op jit(solution)/shard_map/reduce_scatter | solution.py:75
  78.4 1.4 %copy-start.1 = (f32[4,128,1024]{2,1,0:T(8,128)}, f32[4,128,1024]{2,1,0:T(8,128)S(1)}, u32[]{:S(2)}) copy-start(f32[4,128,1024]{2,1,0:T(8,128)S(1)} %get-tuple-element.13) | copy-start | bytes 6291460
  90.1 3.3 %copy-start.2 = (bf16[256,1024]{1,0:T(8,128)(2,1)S(1)}, bf16[256,1024]{1,0:T(8,128)(2,1)}, u32[]{:S(2)}) copy-start(bf16[256,1024]{1,0:T(8,128)(2,1)} %param.12) | copy-start | bytes 1572868
Sparse Core Ops, SparseCore 0:
  30.4 19.7 reduce-scatter.2
  97.6 17.1 reduce-scatter.4
where the time goes:
time: 124 us; the launch traced here: 123 us
  blocking collectives  56.2 us (45%)
  waiting for transfers between devices  27.3 us (22%)
  between operations  14.2 us (11%)
  matrix products  14 us (11%)
  local copies, waits for them, and re-layouts  7.04 us (6%)
  other arithmetic  4.42 us (4%)
    reduce_scatter x1, waiting for transfers between devices, per_device(): lax.psum_scatter((jnp.dot(attended, out_weight, preferred_element_type=f3...  17.3 us
    all_gather x1, blocking collectives, per_device(): all_features = lax.all_gather(pooled, 'var', axis=1, tiled=True)  14.1 us
    pmax x1, blocking collectives, per_device(): top_score = lax.pmax(jnp.max(scores, axis=0), 'var')  13.7 us
    all_gather x1, blocking collectives, per_device(): key_block = lax.all_gather(key_local, 'space', axis=0, tiled=True)  10 us
    reduce_scatter x1, waiting for transfers between devices, per_device(): lax.psum_scatter(numerator, 'var', scatter_dimension=1, tiled=True)  9.93 us
    all_gather x1, blocking collectives, per_device(): value_block = lax.all_gather(value_local, 'space', axis=0, tiled=True)  9.8 us
    unnamed x1, blocking collectives  8.53 us
    dot_general x1, matrix products, per_device(): jnp.dot(hidden, down_weight, preferred_element_type=f32)  3.84 us
  transfers between devices with their start and end apart: 2, of which 2 were waited for; matrix products, arithmetic and copies ran while one was open for 1% of the time, Pallas kernels for 0%

commit v1 on v0

v1 whole, which is shorter than its diff:
```python
import functools

import jax
import jax.numpy as jnp
from jax import lax
from jax.experimental import pallas as pl
from jax.experimental.pallas import tpu as pltpu
from jax.sharding import PartitionSpec as P

H = 16
LANES = 128
EPS = 1e-05
f32 = jnp.float32
bf16 = jnp.bfloat16


def rows_of(refs):
    if len(refs) == 1:
        return refs[0][...]
    if refs[0].shape[0] % 16 == 0:
        return jnp.concatenate([r[...] for r in refs], axis=0)
    return jnp.concatenate([r[...].astype(f32) for r in refs], axis=0).astype(bf16)


def head_spread(first, last, width):
    lane = lax.broadcasted_iota(jnp.int32, (LANES, width), 0)
    column = lax.broadcasted_iota(jnp.int32, (LANES, width), 1)
    group = lane // H
    hit = (lane % H == column // (width // H)) & (group >= first) & (group < last)
    return hit.astype(bf16)


def split3(x):
    hi = x.astype(bf16).astype(f32)
    mid = (x - hi).astype(bf16).astype(f32)
    return hi, mid, x - hi - mid


def pool_kernel(me_ref, x_ref, kq_ref, wv_ref, *out_refs):
    n_vars, groups, rows, width = x_ref.shape
    me = me_ref[0]
    x = jnp.concatenate(
        [x_ref[v, me ^ k] for k in range(groups) for v in range(n_vars)], axis=0
    ) if rows % 16 == 0 else jnp.concatenate(
        [x_ref[v, me ^ k].astype(f32) for k in range(groups) for v in range(n_vars)], axis=0
    ).astype(bf16)
    kq = jnp.concatenate([kq_ref[...]] * (LANES // H), axis=0)
    scores = lax.dot_general(x, kq, (((1,), (1,)), ((), ())), preferred_element_type=f32)
    scores = scores.reshape(groups, n_vars, rows, LANES)
    top = jnp.max(scores, axis=1)
    terms = jnp.exp(scores - top[:, None])
    total = jnp.sum(terms, axis=1)
    share = (terms / total[:, None]).astype(bf16).reshape(groups * n_vars * rows, LANES)
    weights = jnp.dot(share, head_spread(0, 1, width), preferred_element_type=f32)
    values = jnp.dot(x, wv_ref[...], preferred_element_type=f32)
    mean = jnp.sum((weights * values).reshape(groups, n_vars, rows, width), axis=1)
    lane = lax.broadcasted_iota(jnp.int32, (rows, LANES), 1) // H
    for k in range(groups):
        stats = jnp.zeros((rows, LANES), f32)
        for j, part in enumerate(split3(top[k]) + split3(total[k])):
            stats = jnp.where(lane == j, part, stats)
        out_refs[k][:, :width] = mean[k].astype(bf16)
        out_refs[k][:, width:] = stats.astype(bf16)


def norm_kernel(gain_ref, *refs):
    parts, (normed_ref, pooled_ref) = refs[:-2], refs[-2:]
    rows, width = normed_ref.shape
    to_top = head_spread(0, 3, width)
    to_total = head_spread(3, 6, width)
    tops = [jnp.dot(p[:, width:], to_top, preferred_element_type=f32) for p in parts]
    totals = [jnp.dot(p[:, width:], to_total, preferred_element_type=f32) for p in parts]
    top = functools.reduce(jnp.maximum, tops)
    scales = [t * jnp.exp(m - top) for t, m in zip(totals, tops)]
    summed = functools.reduce(
        jnp.add, [s * p[:, :width].astype(f32) for s, p in zip(scales, parts)]
    )
    pooled = (summed / functools.reduce(jnp.add, scales)).astype(bf16)
    pooled_ref[...] = pooled
    pooled = pooled.astype(f32)
    centered = pooled - jnp.mean(pooled, axis=1, keepdims=True)
    spread = jnp.mean(centered * centered, axis=1, keepdims=True)
    normed_ref[...] = (centered * lax.rsqrt(spread + EPS) * gain_ref[...].astype(f32)).astype(bf16)


def qkv_kernel(w_ref, *refs):
    blocks, (q_ref, kv_ref) = refs[:-2], refs[-2:]
    x = rows_of(blocks)
    width = q_ref.shape[1]
    q_ref[...] = jnp.dot(x, w_ref[0], preferred_element_type=f32).astype(bf16)
    kv_ref[:, :width] = jnp.dot(x, w_ref[1], preferred_element_type=f32).astype(bf16)
    kv_ref[:, width:] = jnp.dot(x, w_ref[2], preferred_element_type=f32).astype(bf16)


def ffn_kernel(up_ref, down_ref, *refs):
    blocks, out_ref = refs[:-1], refs[-1]
    x = rows_of(blocks)
    hidden = jnp.dot(x, up_ref[...], preferred_element_type=f32)
    hidden = jax.nn.gelu(hidden, approximate=True).astype(bf16)
    out_ref[...] = jnp.dot(hidden, down_ref[...], preferred_element_type=f32)


def attend_kernel(heads, groups, q_ref, ffn_ref, wo_ref, *refs):
    blocks, out_refs = refs[:-groups], refs[-groups:]
    rows, width = q_ref.shape
    head_dim = width // heads
    q = q_ref[...].astype(f32) * head_dim ** (-0.5)
    owner = lax.broadcasted_iota(jnp.int32, (rows, width), 1) // head_dim
    stacked = jnp.concatenate([jnp.where(owner == h, q, 0.0) for h in range(heads)], axis=0)
    stacked = stacked.astype(bf16)
    keys = jnp.concatenate([b[:, :width] for b in blocks], axis=0)
    vals = jnp.concatenate([b[:, width:] for b in blocks], axis=0)
    logits = lax.dot_general(stacked, keys, (((1,), (1,)), ((), ())), preferred_element_type=f32)
    terms = jnp.exp(logits - jnp.max(logits, axis=1, keepdims=True))
    total = jnp.sum(terms, axis=1, keepdims=True)
    mixed = jnp.dot(terms.astype(bf16), vals, preferred_element_type=f32) / total
    attended = mixed[:rows]
    for h in range(1, heads):
        attended = jnp.where(owner == h, mixed[h * rows : (h + 1) * rows], attended)
    out = jnp.dot(attended.astype(bf16), wo_ref[...], preferred_element_type=f32) + ffn_ref[...]
    part = rows // groups
    for k in range(groups):
        out_refs[k][...] = out[k * part : (k + 1) * part].astype(bf16)


def add_kernel(*refs):
    out_ref = refs[-1]
    out_ref[...] = functools.reduce(jnp.add, [r[...].astype(f32) for r in refs[:-1]]).astype(bf16)


def call(kernel, out_shapes, *args, flops=0, smem=0, vmem=48):
    vmem_spec = pl.BlockSpec(memory_space=pltpu.VMEM)
    single = not isinstance(out_shapes, list)
    outs = [out_shapes] if single else out_shapes
    moved = sum(a.size * a.dtype.itemsize for a in (*args, *outs))
    result = pl.pallas_call(
        kernel,
        out_shape=outs,
        in_specs=[pl.BlockSpec(memory_space=pltpu.SMEM)] * smem + [vmem_spec] * (len(args) - smem),
        out_specs=[vmem_spec] * len(outs),
        compiler_params=pltpu.CompilerParams(vmem_limit_bytes=vmem << 20),
        cost_estimate=pl.CostEstimate(flops=flops, bytes_accessed=moved, transcendentals=0),
    )(*args)
    return result[0] if single else result


def exchange(parts, axis, size):
    return [parts[0]] + [
        lax.ppermute(parts[k], axis, [(i, i ^ k) for i in range(size)]) for k in range(1, size)
    ]


def gather_space(block, size):
    if size > 8:
        return [lax.all_gather(block, "space", axis=0, tiled=True)]
    blocks = exchange_chips(block, size)
    twin = [(i, i ^ 1) for i in range(size)]
    return blocks + [lax.ppermute(b, "space", twin) for b in blocks]


def exchange_chips(block, size):
    return [block] + [
        lax.ppermute(block, "space", [(i, i ^ k) for i in range(size)]) for k in range(2, size, 2)
    ]


def per_device(
    var_tokens, key_query, value_weight, qkv_weight, out_weight, up_weight, down_weight, norm_gain
):
    groups = lax.axis_size("var")
    spaces = lax.axis_size("space")
    n_vars, rows, width = var_tokens.shape
    part = rows // groups
    local = qkv_weight.shape[2]
    me = lax.axis_index("var").astype(jnp.int32).reshape(1)

    tokens = var_tokens.reshape(n_vars, groups, part, width)
    shape = jax.ShapeDtypeStruct
    sent = call(
        pool_kernel,
        [shape((part, width + LANES), bf16)] * groups,
        me, tokens, key_query.T, value_weight,
        flops=2 * n_vars * rows * width * width, smem=1,
    )
    got = exchange(sent, "var", groups)
    normed, pooled = call(
        norm_kernel, [shape((part, width), bf16)] * 2, norm_gain.reshape(1, width), *got
    )
    blocks = exchange([normed] * groups, "var", groups)
    q, kv = call(
        qkv_kernel,
        [shape((rows, local), bf16), shape((rows, 2 * local), bf16)],
        qkv_weight.transpose(1, 0, 2), *blocks,
        flops=6 * rows * width * local,
    )
    kv_blocks = gather_space(kv, spaces)
    hidden = up_weight.shape[1]
    ffn = call(
        ffn_kernel, shape((rows, width), f32), up_weight, down_weight, *blocks,
        flops=4 * rows * width * hidden,
    )
    sums = call(
        functools.partial(attend_kernel, H // groups, groups),
        [shape((part, width), bf16)] * groups,
        q, ffn, out_weight, *kv_blocks,
        flops=4 * rows * rows * spaces * local,
    )
    return call(add_kernel, shape((part, width), bf16), pooled, *exchange(sums, "var", groups))


def solution(mesh):
    placed = (
        P("var", "space", None),
        P(),
        P(),
        P(None, None, "var"),
        P("var", None),
        P(None, "var"),
        P("var", None),
        P(),
    )
    return jax.shard_map(
        per_device, mesh=mesh, in_specs=placed, out_specs=P(("space", "var"), None), check_vma=False
    )
```

time: 124 us -> 49.5 us (0.40)
  blocking collectives: 56.2 us -> 0 us
  starting transfers between devices: 0.04 us -> 18.2 us
  between operations: 14.2 us -> 0.1 us
  matrix products: 14 us -> 0 us
  waiting for transfers between devices: 27.3 us -> 19.4 us
  Pallas kernels: 0 us -> 6.47 us
  other arithmetic: 4.42 us -> 0 us
  local copies, waits for them, and re-layouts: 7.04 us -> 5.02 us
    all_gather x3 -> x0, blocking collectives: 33.9 us -> none  [the longest x1 14.1 us: per_device(): all_features = lax.all_gather(pooled, 'var', axis=1, tiled=True)]
    reduce_scatter x2 -> x0, waiting for transfers between devices: 27.2 us -> none  [the longest x1 17.3 us: per_device(): lax.psum_scatter((jnp.dot(attended, out_weight, preferred_element_type=f3...]
    ppermute x0 -> x16, waiting for transfers between devices: none -> 19.4 us  [the longest x9 14.5 us: exchange(): lax.ppermute(parts[k], axis, [(i, i ^ k) for i in range(size)])]
    ppermute x0 -> x16, starting transfers between devices: none -> 18.2 us  [the longest x9 14.6 us: exchange(): lax.ppermute(parts[k], axis, [(i, i ^ k) for i in range(size)])]
    dot_general x7 -> x0, matrix products: 14 us -> none  [the longest x1 3.84 us: per_device(): jnp.dot(hidden, down_weight, preferred_element_type=f32)]
    pmax x1 -> x0, blocking collectives: 13.7 us -> none  [per_device(): top_score = lax.pmax(jnp.max(scores, axis=0), 'var')]
    unnamed x1 -> x0, blocking collectives: 8.53 us -> none
    pallas_call x0 -> x6, Pallas kernels: none -> 6.47 us  [call(): pl.pallas_call(kernel, out_shape=outs, in_specs=[pl.BlockSpec(memory_spac...]
  transfers between devices with their start and end apart: 2 -> 16, of which waited for: 2 -> 10; matrix products, arithmetic and copies ran while one was open for 1% -> 0% of each run, Pallas kernels for 0% -> 2%
where the time goes in v1:
time: 49.5 us; the launch traced here: 49.2 us
  waiting for transfers between devices  19.4 us (39%)
  starting transfers between devices  18.2 us (37%)
  Pallas kernels  6.47 us (13%)
  local copies, waits for them, and re-layouts  5.02 us (10%)
    ppermute x9, starting transfers between devices, exchange(): lax.ppermute(parts[k], axis, [(i, i ^ k) for i in range(size)])  14.6 us
    ppermute x9, waiting for transfers between devices, exchange(): lax.ppermute(parts[k], axis, [(i, i ^ k) for i in range(size)])  14.5 us
    pallas_call x6, Pallas kernels, call(): pl.pallas_call(kernel, out_shape=outs, in_specs=[pl.BlockSpec(memory_spac...  6.47 us
    unnamed x16, local copies, waits for them, and re-layouts  5.01 us
    ppermute x3, waiting for transfers between devices, exchange_chips(): lax.ppermute(block, 'space', [(i, i ^ k) for i in range(size)])  4.42 us
    ppermute x3, starting transfers between devices, exchange_chips(): lax.ppermute(block, 'space', [(i, i ^ k) for i in range(size)])  3.55 us
  transfers between devices with their start and end apart: 16, of which 10 were waited for; matrix products, arithmetic and copies ran while one was open for 0% of the time, Pallas kernels for 2%

profile of v1, /device:TPU:0, one launch (start us, length us, event | category | flops | bytes accessed | tf_op | source)
XLA Modules:
  0.0 49.2 jit_solution(15111874063937157430)
XLA Ops:
  0.0 0.0 copy-start.7
  0.0 0.0 copy-start.4
  0.0 1.6 %copy-done.4 = bf16[1024,1024]{1,0:T(8,128)(2,1)S(1)} copy-done((bf16[1024,1024]{1,0:T(8,128)(2,1)S(1)}, bf16[1024,1024]{1,0:T(8,128)(2,1)}, u32[]{:S(2)}) %copy-start.4) | copy-done | bytes 2097176
  1.6 0.0 copy-start.5
  1.6 1.2 %copy-done.5 = bf16[4,128,1024]{2,1,0:T(8,128)(2,1)S(1)} copy-done((bf16[4,128,1024]{2,1,0:T(8,128)(2,1)S(1)}, bf16[4,128,1024]{2,1,0:T(8,128)(2,1)}, u32[]{:S(2)}) %copy-start.5) | copy-done | bytes 1048600
  2.8 0.0 copy-start.6
  2.8 0.8 %copy-done.6 = bf16[1024,16]{0,1:T(8,128)(2,1)S(1)} copy-done((bf16[1024,16]{0,1:T(8,128)(2,1)S(1)}, bf16[1024,16]{0,1:T(8,128)(2,1)}, u32[]{:S(2)}) %copy-start.6) | copy-done | bytes 32792
  3.6 0.0 copy-start
  3.6 0.0 copy-start.1
  3.6 2.4 %shard_map.82 = (bf16[32,1152]{1,0:T(8,128)(2,1)S(1)}, bf16[32,1152]{1,0:T(8,128)(2,1)S(1)}, bf16[32,1152]{1,0:T(8,128)(2,1)S(1)}, bf16[32,1152]{1,0:T(8,128)(2,1)S(1)}) custom-call(s32[1]{0:T(128)} %bitcast.me_ref, bf16[4,4,32,1024]{3,2,1,0:T(8,128)(2,1)S(1)} %bitcast.5, bf16[16,1024]{1,0:T(8,128)(2,1)S(1)} %bitcast.6, bf16[1024,1024]{1,0:T(8,128)(2,1)S(1)} %copy-done.4), custom_call_target="tpu_custom_call" | custom-call | flops 1073741824 | bytes 3473412 | tf_op jit(solution)/shard_map/pallas_call | solution.py:136
  6.0 3.1 %collective-permute-start = (bf16[32,1152]{1,0:T(8,128)(2,1)S(1)}, bf16[32,1152]{1,0:T(8,128)(2,1)S(1)}, u32[]{:S(2)}, u32[]{:S(2)}) collective-permute-start(bf16[32,1152]{1,0:T(8,128)(2,1)S(1)} %get-tuple-element.18), channel_id=1, source_target_pairs={{0,1},{1,0},{2,3},{3,2},{4,5},{5,4},{6,7},{7,6},{8,9},{9,8},{10,11... | collective-permute-start | bytes 221192 | tf_op jit(solution)/shard_map/ppermute | solution.py:149
  9.1 2.6 %collective-permute-start.1 = (bf16[32,1152]{1,0:T(8,128)(2,1)S(1)}, bf16[32,1152]{1,0:T(8,128)(2,1)S(1)}, u32[]{:S(2)}, u32[]{:S(2)}) collective-permute-start(bf16[32,1152]{1,0:T(8,128)(2,1)S(1)} %get-tuple-element.19), channel_id=1, source_target_pairs={{0,2},{1,3},{2,0},{3,1},{4,6},{5,7},{6,4},{7,5},{8,10},{9,11},{10,... | collective-permute-start | bytes 221192 | tf_op jit(solution)/shard_map/ppermute | solution.py:149
  11.7 0.0 collective-permute-start.2
  11.7 0.0 copy-done.7
  11.7 0.0 collective-permute-done.refs_1_
  11.7 5.2 %collective-permute-done.1.refs_2_ = bf16[32,1152]{1,0:T(8,128)(2,1)S(1)} collective-permute-done((bf16[32,1152]{1,0:T(8,128)(2,1)S(1)}, bf16[32,1152]{1,0:T(8,128)(2,1)S(1)}, u32[]{:S(2)}, u32[]{:S(2)}) %collective-permute-start.1) | collective-permute-done | bytes 73760 | tf_op jit(solution)/shard_map/ppermute | solution.py:149
  16.9 1.1 %collective-permute-done.2.refs_3_ = bf16[32,1152]{1,0:T(8,128)(2,1)S(1)} collective-permute-done((bf16[32,1152]{1,0:T(8,128)(2,1)S(1)}, bf16[32,1152]{1,0:T(8,128)(2,1)S(1)}, u32[]{:S(2)}, u32[]{:S(2)}) %collective-permute-start.2) | collective-permute-done | bytes 73760 | tf_op jit(solution)/shard_map/ppermute | solution.py:149
  17.9 0.6 %shard_map.83 = (bf16[32,1024]{1,0:T(8,128)(2,1)S(1)}, bf16[32,1024]{1,0:T(8,128)(2,1)S(1)}) custom-call(bf16[1,1024]{1,0:T(2,128)(2,1)S(1)} %reshape.9.gain_ref, bf16[32,1152]{1,0:T(8,128)(2,1)S(1)} %get-tuple-element.17.refs_0_, bf16[32,1152]{1,0:T(8,128)(2,1)S(1)} %collective-permute-done.refs_1_, bf16[32,1152]{1,0:T(8,128)(2,1)S(1)} %collective-permute-done.1.refs_2_, ...), custom_call_target="tpu_custom_call" | custom-call | bytes 428032 | tf_op jit(solution)/shard_map/pallas_call | solution.py:136
  18.5 2.3 %collective-permute-start.5 = (bf16[32,1024]{1,0:T(8,128)(2,1)S(1)}, bf16[32,1024]{1,0:T(8,128)(2,1)S(1)}, u32[]{:S(2)}, u32[]{:S(2)}) collective-permute-start(bf16[32,1024]{1,0:T(8,128)(2,1)S(1)} %get-tuple-element.22.refs_0_), channel_id=1, source_target_pairs={{0,3},{1,2},{2,1},{3,0},{4,7},{5,6},{6,5},{7,4},{8,11},{9,10},{10,... | collective-permute-start | bytes 196616 | tf_op jit(solution)/shard_map/ppermute | solution.py:149
  20.8 0.3 collective-permute-start.4
  21.1 1.8 %collective-permute-start.3 = (bf16[32,1024]{1,0:T(8,128)(2,1)S(1)}, bf16[32,1024]{1,0:T(8,128)(2,1)S(1)}, u32[]{:S(2)}, u32[]{:S(2)}) collective-permute-start(bf16[32,1024]{1,0:T(8,128)(2,1)S(1)} %get-tuple-element.22.refs_0_), channel_id=1, source_target_pairs={{0,1},{1,0},{2,3},{3,2},{4,5},{5,4},{6,7},{7,6},{8,9},{9,8},{10,11... | collective-permute-start | bytes 196616 | tf_op jit(solution)/shard_map/ppermute | solution.py:149
  22.9 1.7 %collective-permute-done.5.refs_3_ = bf16[32,1024]{1,0:T(8,128)(2,1)S(1)} collective-permute-done((bf16[32,1024]{1,0:T(8,128)(2,1)S(1)}, bf16[32,1024]{1,0:T(8,128)(2,1)S(1)}, u32[]{:S(2)}, u32[]{:S(2)}) %collective-permute-start.5) | collective-permute-done | bytes 65568 | tf_op jit(solution)/shard_map/ppermute | solution.py:149
  24.6 1.9 %collective-permute-done.4.refs_2_ = bf16[32,1024]{1,0:T(8,128)(2,1)S(1)} collective-permute-done((bf16[32,1024]{1,0:T(8,128)(2,1)S(1)}, bf16[32,1024]{1,0:T(8,128)(2,1)S(1)}, u32[]{:S(2)}, u32[]{:S(2)}) %collective-permute-start.4) | collective-permute-done | bytes 65568 | tf_op jit(solution)/shard_map/ppermute | solution.py:149
  26.5 0.0 collective-permute-done.3.refs_1_
  26.5 0.0 copy-start.2
  26.5 1.4 %copy-done.2 = bf16[1024,3,256]{2,0,1:T(8,128)(2,1)S(1)} copy-done((bf16[1024,3,256]{2,0,1:T(8,128)(2,1)S(1)}, bf16[1024,3,256]{2,0,1:T(8,128)(2,1)}, u32[]{:S(2)}) %copy-start.2) | copy-done | bytes 1572888
  27.9 0.4 shard_map.84
  28.3 0.0 copy-start.3
  28.3 2.5 %collective-permute-start.8 = (bf16[128,512]{1,0:T(8,128)(2,1)S(1)}, bf16[128,512]{1,0:T(8,128)(2,1)S(1)}, u32[]{:S(2)}, u32[]{:S(2)}) collective-permute-start(bf16[128,512]{1,0:T(8,128)(2,1)S(1)} %get-tuple-element.24.refs_0_), channel_id=1, source_target_pairs={{0,24},{4,28},{8,16},{12,20},{16,8},{20,12},{24,0},{28,4},{1,25},{... | collective-permute-start | bytes 393224 | tf_op jit(solution)/shard_map/ppermute | solution.py:163
  30.8 0.5 %collective-permute-start.7 = (bf16[128,512]{1,0:T(8,128)(2,1)S(1)}, bf16[128,512]{1,0:T(8,128)(2,1)S(1)}, u32[]{:S(2)}, u32[]{:S(2)}) collective-permute-start(bf16[128,512]{1,0:T(8,128)(2,1)S(1)} %get-tuple-element.24.refs_0_), channel_id=1, source_target_pairs={{0,16},{4,20},{8,24},{12,28},{16,0},{20,4},{24,8},{28,12},{1,17},{... | collective-permute-start | bytes 393224 | tf_op jit(solution)/shard_map/ppermute | solution.py:163
  31.3 0.5 %collective-permute-start.6 = (bf16[128,512]{1,0:T(8,128)(2,1)S(1)}, bf16[128,512]{1,0:T(8,128)(2,1)S(1)}, u32[]{:S(2)}, u32[]{:S(2)}) collective-permute-start(bf16[128,512]{1,0:T(8,128)(2,1)S(1)} %get-tuple-element.24.refs_0_), channel_id=1, source_target_pairs={{0,8},{4,12},{8,0},{12,4},{16,24},{20,28},{24,16},{28,20},{1,9},{5... | collective-permute-start | bytes 393224 | tf_op jit(solution)/shard_map/ppermute | solution.py:163
  31.9 0.0 collective-permute-start.9
  31.9 2.4 %collective-permute-done.8.refs_3_ = bf16[128,512]{1,0:T(8,128)(2,1)S(1)} collective-permute-done((bf16[128,512]{1,0:T(8,128)(2,1)S(1)}, bf16[128,512]{1,0:T(8,128)(2,1)S(1)}, u32[]{:S(2)}, u32[]{:S(2)}) %collective-permute-start.8) | collective-permute-done | bytes 131104 | tf_op jit(solution)/shard_map/ppermute | solution.py:163
  34.3 0.0 collective-permute-start.12
  34.3 1.5 %collective-permute-done.7.refs_2_ = bf16[128,512]{1,0:T(8,128)(2,1)S(1)} collective-permute-done((bf16[128,512]{1,0:T(8,128)(2,1)S(1)}, bf16[128,512]{1,0:T(8,128)(2,1)S(1)}, u32[]{:S(2)}, u32[]{:S(2)}) %collective-permute-start.7) | collective-permute-done | bytes 131104 | tf_op jit(solution)/shard_map/ppermute | solution.py:163
  35.8 0.0 collective-permute-start.11
  35.8 0.5 %collective-permute-done.6.refs_1_ = bf16[128,512]{1,0:T(8,128)(2,1)S(1)} collective-permute-done((bf16[128,512]{1,0:T(8,128)(2,1)S(1)}, bf16[128,512]{1,0:T(8,128)(2,1)S(1)}, u32[]{:S(2)}, u32[]{:S(2)}) %collective-permute-start.6) | collective-permute-done | bytes 131104 | tf_op jit(solution)/shard_map/ppermute | solution.py:163
  36.3 0.0 collective-permute-start.10
  36.3 0.0 copy-done
  36.3 0.0 copy-done.1
  36.3 0.8 %shard_map.85.ffn_ref = f32[128,1024]{1,0:T(8,128)S(1)} custom-call(bf16[1024,1024]{1,0:T(8,128)(2,1)S(1)} %copy-done, bf16[1024,1024]{1,0:T(8,128)(2,1)S(1)} %copy-done.1, bf16[32,1024]{1,0:T(8,128)(2,1)S(1)} %get-tuple-element.22.refs_0_, bf16[32,1024]{1,0:T(8,128)(2,1)S(1)} %collective-permute-done.3.refs_1_, ...), custom_call_target="tpu_custom_call" | custom-call | flops 536870912 | bytes 4980736 | tf_op jit(solution)/shard_map/pallas_call | solution.py:136
  37.2 0.0 collective-permute-done.9.refs_4_
  37.2 0.0 collective-permute-done.12.refs_7_
  37.2 0.0 collective-permute-done.11.refs_6_
  37.2 0.5 collective-permute-done.10.refs_5_
  37.7 0.0 copy-done.3
  37.7 1.7 %shard_map.86 = (bf16[32,1024]{1,0:T(8,128)(2,1)S(1)}, bf16[32,1024]{1,0:T(8,128)(2,1)S(1)}, bf16[32,1024]{1,0:T(8,128)(2,1)S(1)}, bf16[32,1024]{1,0:T(8,128)(2,1)S(1)}) custom-call(bf16[128,256]{1,0:T(8,128)(2,1)S(1)} %get-tuple-element.23.q_ref, f32[128,1024]{1,0:T(8,128)S(1)} %shard_map.85.ffn_ref, bf16[256,1024]{1,0:T(8,128)(2,1)S(1)} %copy-done.3, ...), custom_call_target="tpu_custom_call" | custom-call | flops 134217728 | bytes 2424832 | tf_op jit(solution)/shard_map/pallas_call | solution.py:136
  39.3 0.8 %collective-permute-start.13 = (bf16[32,1024]{1,0:T(8,128)(2,1)S(1)}, bf16[32,1024]{1,0:T(8,128)(2,1)S(1)}, u32[]{:S(2)}, u32[]{:S(2)}) collective-permute-start(bf16[32,1024]{1,0:T(8,128)(2,1)S(1)} %get-tuple-element.26), channel_id=1, source_target_pairs={{0,1},{1,0},{2,3},{3,2},{4,5},{5,4},{6,7},{7,6},{8,9},{9,8},{10,11... | collective-permute-start | bytes 196616 | tf_op jit(solution)/shard_map/ppermute | solution.py:149
  40.1 1.9 %collective-permute-start.14 = (bf16[32,1024]{1,0:T(8,128)(2,1)S(1)}, bf16[32,1024]{1,0:T(8,128)(2,1)S(1)}, u32[]{:S(2)}, u32[]{:S(2)}) collective-permute-start(bf16[32,1024]{1,0:T(8,128)(2,1)S(1)} %get-tuple-element.27), channel_id=1, source_target_pairs={{0,2},{1,3},{2,0},{3,1},{4,6},{5,7},{6,4},{7,5},{8,10},{9,11},{10,... | collective-permute-start | bytes 196616 | tf_op jit(solution)/shard_map/ppermute | solution.py:149
  41.9 1.8 %collective-permute-start.15 = (bf16[32,1024]{1,0:T(8,128)(2,1)S(1)}, bf16[32,1024]{1,0:T(8,128)(2,1)S(1)}, u32[]{:S(2)}, u32[]{:S(2)}) collective-permute-start(bf16[32,1024]{1,0:T(8,128)(2,1)S(1)} %get-tuple-element.28), channel_id=1, source_target_pairs={{0,3},{1,2},{2,1},{3,0},{4,7},{5,6},{6,5},{7,4},{8,11},{9,10},{10,... | collective-permute-start | bytes 196616 | tf_op jit(solution)/shard_map/ppermute | solution.py:149
  43.8 0.6 %collective-permute-done.13.refs_2_ = bf16[32,1024]{1,0:T(8,128)(2,1)S(1)} collective-permute-done((bf16[32,1024]{1,0:T(8,128)(2,1)S(1)}, bf16[32,1024]{1,0:T(8,128)(2,1)S(1)}, u32[]{:S(2)}, u32[]{:S(2)}) %collective-permute-start.13) | collective-permute-done | bytes 65568 | tf_op jit(solution)/shard_map/ppermute | solution.py:149
  44.4 4.2 %collective-permute-done.14.refs_3_ = bf16[32,1024]{1,0:T(8,128)(2,1)S(1)} collective-permute-done((bf16[32,1024]{1,0:T(8,128)(2,1)S(1)}, bf16[32,1024]{1,0:T(8,128)(2,1)S(1)}, u32[]{:S(2)}, u32[]{:S(2)}) %collective-permute-start.14) | collective-permute-done | bytes 65568 | tf_op jit(solution)/shard_map/ppermute | solution.py:149
  48.5 0.0 collective-permute-done.15.refs_4_
  48.5 0.7 %shard_map.87 = bf16[32,1024]{1,0:T(8,128)(2,1)} custom-call(bf16[32,1024]{1,0:T(8,128)(2,1)S(1)} %get-tuple-element.21.refs_0_, bf16[32,1024]{1,0:T(8,128)(2,1)S(1)} %get-tuple-element.25.refs_1_, bf16[32,1024]{1,0:T(8,128)(2,1)S(1)} %collective-permute-done.13.refs_2_, bf16[32,1024]{1,0:T(8,128)(2,1)S(1)} %collective-permute-done.14.refs_3_, ...), custom_call_target="tpu_custom_call" | custom-call | bytes 393216 | tf_op jit(solution)/shard_map/pallas_call | solution.py:136
  (1 shorter events, 0.0 us)
Async XLA Ops:
  0.0 11.7 %copy-start.7 = (bf16[1024]{0:T(1024)(128)(2,1)S(1)}, bf16[1024]{0:T(1024)(128)(2,1)}, u32[]{:S(2)}) copy-start(bf16[1024]{0:T(1024)(128)(2,1)} %param.15) | copy-start | bytes 6148
  0.0 1.6 %copy-start.4 = (bf16[1024,1024]{1,0:T(8,128)(2,1)S(1)}, bf16[1024,1024]{1,0:T(8,128)(2,1)}, u32[]{:S(2)}) copy-start(bf16[1024,1024]{1,0:T(8,128)(2,1)} %wv_ref.1) | copy-start | bytes 6291460
  1.6 1.2 %copy-start.5 = (bf16[4,128,1024]{2,1,0:T(8,128)(2,1)S(1)}, bf16[4,128,1024]{2,1,0:T(8,128)(2,1)}, u32[]{:S(2)}) copy-start(bf16[4,128,1024]{2,1,0:T(8,128)(2,1)} %param.8) | copy-start | bytes 3145732
  2.8 0.8 %copy-start.6 = (bf16[1024,16]{0,1:T(8,128)(2,1)S(1)}, bf16[1024,16]{0,1:T(8,128)(2,1)}, u32[]{:S(2)}) copy-start(bf16[1024,16]{0,1:T(8,128)(2,1)} %param.9) | copy-start | bytes 98308
  3.6 32.7 %copy-start = (bf16[1024,1024]{1,0:T(8,128)(2,1)S(1)}, bf16[1024,1024]{1,0:T(8,128)(2,1)}, u32[]{:S(2)}) copy-start(bf16[1024,1024]{1,0:T(8,128)(2,1)} %up_ref.1) | copy-start | bytes 6291460
  3.6 32.7 %copy-start.1 = (bf16[1024,1024]{1,0:T(8,128)(2,1)S(1)}, bf16[1024,1024]{1,0:T(8,128)(2,1)}, u32[]{:S(2)}) copy-start(bf16[1024,1024]{1,0:T(8,128)(2,1)} %down_ref.1) | copy-start | bytes 6291460
  6.0 5.7 %collective-permute-start = (bf16[32,1152]{1,0:T(8,128)(2,1)S(1)}, bf16[32,1152]{1,0:T(8,128)(2,1)S(1)}, u32[]{:S(2)}, u32[]{:S(2)}) collective-permute-start(bf16[32,1152]{1,0:T(8,128)(2,1)S(1)} %get-tuple-element.18), channel_id=1, source_target_pairs={{0,1},{1,0},{2,3},{3,2},{4,5},{5,4},{6,7},{7,6},{8,9},{9,8},{10,11... | collective-permute-start | bytes 221192 | tf_op jit(solution)/shard_map/ppermute | solution.py:149
  9.1 7.8 %collective-permute-start.1 = (bf16[32,1152]{1,0:T(8,128)(2,1)S(1)}, bf16[32,1152]{1,0:T(8,128)(2,1)S(1)}, u32[]{:S(2)}, u32[]{:S(2)}) collective-permute-start(bf16[32,1152]{1,0:T(8,128)(2,1)S(1)} %get-tuple-element.19), channel_id=1, source_target_pairs={{0,2},{1,3},{2,0},{3,1},{4,6},{5,7},{6,4},{7,5},{8,10},{9,11},{10,... | collective-permute-start | bytes 221192 | tf_op jit(solution)/shard_map/ppermute | solution.py:149
  11.7 6.3 %collective-permute-start.2 = (bf16[32,1152]{1,0:T(8,128)(2,1)S(1)}, bf16[32,1152]{1,0:T(8,128)(2,1)S(1)}, u32[]{:S(2)}, u32[]{:S(2)}) collective-permute-start(bf16[32,1152]{1,0:T(8,128)(2,1)S(1)} %get-tuple-element.20), channel_id=1, source_target_pairs={{0,3},{1,2},{2,1},{3,0},{4,7},{5,6},{6,5},{7,4},{8,11},{9,10},{10,... | collective-permute-start | bytes 221192 | tf_op jit(solution)/shard_map/ppermute | solution.py:149
  18.5 6.1 %collective-permute-start.5 = (bf16[32,1024]{1,0:T(8,128)(2,1)S(1)}, bf16[32,1024]{1,0:T(8,128)(2,1)S(1)}, u32[]{:S(2)}, u32[]{:S(2)}) collective-permute-start(bf16[32,1024]{1,0:T(8,128)(2,1)S(1)} %get-tuple-element.22.refs_0_), channel_id=1, source_target_pairs={{0,3},{1,2},{2,1},{3,0},{4,7},{5,6},{6,5},{7,4},{8,11},{9,10},{10,... | collective-permute-start | bytes 196616 | tf_op jit(solution)/shard_map/ppermute | solution.py:149
  20.8 5.8 %collective-permute-start.4 = (bf16[32,1024]{1,0:T(8,128)(2,1)S(1)}, bf16[32,1024]{1,0:T(8,128)(2,1)S(1)}, u32[]{:S(2)}, u32[]{:S(2)}) collective-permute-start(bf16[32,1024]{1,0:T(8,128)(2,1)S(1)} %get-tuple-element.22.refs_0_), channel_id=1, source_target_pairs={{0,2},{1,3},{2,0},{3,1},{4,6},{5,7},{6,4},{7,5},{8,10},{9,11},{10,... | collective-permute-start | bytes 196616 | tf_op jit(solution)/shard_map/ppermute | solution.py:149
  21.1 5.4 %collective-permute-start.3 = (bf16[32,1024]{1,0:T(8,128)(2,1)S(1)}, bf16[32,1024]{1,0:T(8,128)(2,1)S(1)}, u32[]{:S(2)}, u32[]{:S(2)}) collective-permute-start(bf16[32,1024]{1,0:T(8,128)(2,1)S(1)} %get-tuple-element.22.refs_0_), channel_id=1, source_target_pairs={{0,1},{1,0},{2,3},{3,2},{4,5},{5,4},{6,7},{7,6},{8,9},{9,8},{10,11... | collective-permute-start | bytes 196616 | tf_op jit(solution)/shard_map/ppermute | solution.py:149
  26.5 1.4 %copy-start.2 = (bf16[1024,3,256]{2,0,1:T(8,128)(2,1)S(1)}, bf16[1024,3,256]{2,0,1:T(8,128)(2,1)}, u32[]{:S(2)}) copy-start(bf16[1024,3,256]{2,0,1:T(8,128)(2,1)} %param.11) | copy-start | bytes 4718596
  28.3 9.4 %copy-start.3 = (bf16[256,1024]{1,0:T(8,128)(2,1)S(1)}, bf16[256,1024]{1,0:T(8,128)(2,1)}, u32[]{:S(2)}) copy-start(bf16[256,1024]{1,0:T(8,128)(2,1)} %wo_ref.1) | copy-start | bytes 1572868
  28.3 5.9 %collective-permute-start.8 = (bf16[128,512]{1,0:T(8,128)(2,1)S(1)}, bf16[128,512]{1,0:T(8,128)(2,1)S(1)}, u32[]{:S(2)}, u32[]{:S(2)}) collective-permute-start(bf16[128,512]{1,0:T(8,128)(2,1)S(1)} %get-tuple-element.24.refs_0_), channel_id=1, source_target_pairs={{0,24},{4,28},{8,16},{12,20},{16,8},{20,12},{24,0},{28,4},{1,25},{... | collective-permute-start | bytes 393224 | tf_op jit(solution)/shard_map/ppermute | solution.py:163
  30.8 5.0 %collective-permute-start.7 = (bf16[128,512]{1,0:T(8,128)(2,1)S(1)}, bf16[128,512]{1,0:T(8,128)(2,1)S(1)}, u32[]{:S(2)}, u32[]{:S(2)}) collective-permute-start(bf16[128,512]{1,0:T(8,128)(2,1)S(1)} %get-tuple-element.24.refs_0_), channel_id=1, source_target_pairs={{0,16},{4,20},{8,24},{12,28},{16,0},{20,4},{24,8},{28,12},{1,17},{... | collective-permute-start | bytes 393224 | tf_op jit(solution)/shard_map/ppermute | solution.py:163
  31.3 5.0 %collective-permute-start.6 = (bf16[128,512]{1,0:T(8,128)(2,1)S(1)}, bf16[128,512]{1,0:T(8,128)(2,1)S(1)}, u32[]{:S(2)}, u32[]{:S(2)}) collective-permute-start(bf16[128,512]{1,0:T(8,128)(2,1)S(1)} %get-tuple-element.24.refs_0_), channel_id=1, source_target_pairs={{0,8},{4,12},{8,0},{12,4},{16,24},{20,28},{24,16},{28,20},{1,9},{5... | collective-permute-start | bytes 393224 | tf_op jit(solution)/shard_map/ppermute | solution.py:163
  31.9 5.3 %collective-permute-start.9 = (bf16[128,512]{1,0:T(8,128)(2,1)S(1)}, bf16[128,512]{1,0:T(8,128)(2,1)S(1)}, u32[]{:S(2)}, u32[]{:S(2)}) collective-permute-start(bf16[128,512]{1,0:T(8,128)(2,1)S(1)} %get-tuple-element.24.refs_0_), channel_id=1, source_target_pairs={{0,4},{4,0},{8,12},{12,8},{16,20},{20,16},{24,28},{28,24},{1,5},{5... | collective-permute-start | bytes 393224 | tf_op jit(solution)/shard_map/ppermute | solution.py:158
  34.3 2.9 %collective-permute-start.12 = (bf16[128,512]{1,0:T(8,128)(2,1)S(1)}, bf16[128,512]{1,0:T(8,128)(2,1)S(1)}, u32[]{:S(2)}, u32[]{:S(2)}) collective-permute-start(bf16[128,512]{1,0:T(8,128)(2,1)S(1)} %collective-permute-done.8.refs_3_), channel_id=1, source_target_pairs={{0,4},{4,0},{8,12},{12,8},{16,20},{20,16},{24,28},{28,24},{1,5},{5... | collective-permute-start | bytes 393224 | tf_op jit(solution)/shard_map/ppermute | solution.py:158
  35.8 1.4 %collective-permute-start.11 = (bf16[128,512]{1,0:T(8,128)(2,1)S(1)}, bf16[128,512]{1,0:T(8,128)(2,1)S(1)}, u32[]{:S(2)}, u32[]{:S(2)}) collective-permute-start(bf16[128,512]{1,0:T(8,128)(2,1)S(1)} %collective-permute-done.7.refs_2_), channel_id=1, source_target_pairs={{0,4},{4,0},{8,12},{12,8},{16,20},{20,16},{24,28},{28,24},{1,5},{5... | collective-permute-start | bytes 393224 | tf_op jit(solution)/shard_map/ppermute | solution.py:158
  36.3 1.3 %collective-permute-start.10 = (bf16[128,512]{1,0:T(8,128)(2,1)S(1)}, bf16[128,512]{1,0:T(8,128)(2,1)S(1)}, u32[]{:S(2)}, u32[]{:S(2)}) collective-permute-start(bf16[128,512]{1,0:T(8,128)(2,1)S(1)} %collective-permute-done.6.refs_1_), channel_id=1, source_target_pairs={{0,4},{4,0},{8,12},{12,8},{16,20},{20,16},{24,28},{28,24},{1,5},{5... | collective-permute-start | bytes 393224 | tf_op jit(solution)/shard_map/ppermute | solution.py:158
  39.3 5.0 %collective-permute-start.13 = (bf16[32,1024]{1,0:T(8,128)(2,1)S(1)}, bf16[32,1024]{1,0:T(8,128)(2,1)S(1)}, u32[]{:S(2)}, u32[]{:S(2)}) collective-permute-start(bf16[32,1024]{1,0:T(8,128)(2,1)S(1)} %get-tuple-element.26), channel_id=1, source_target_pairs={{0,1},{1,0},{2,3},{3,2},{4,5},{5,4},{6,7},{7,6},{8,9},{9,8},{10,11... | collective-permute-start | bytes 196616 | tf_op jit(solution)/shard_map/ppermute | solution.py:149
  40.1 8.4 %collective-permute-start.14 = (bf16[32,1024]{1,0:T(8,128)(2,1)S(1)}, bf16[32,1024]{1,0:T(8,128)(2,1)S(1)}, u32[]{:S(2)}, u32[]{:S(2)}) collective-permute-start(bf16[32,1024]{1,0:T(8,128)(2,1)S(1)} %get-tuple-element.27), channel_id=1, source_target_pairs={{0,2},{1,3},{2,0},{3,1},{4,6},{5,7},{6,4},{7,5},{8,10},{9,11},{10,... | collective-permute-start | bytes 196616 | tf_op jit(solution)/shard_map/ppermute | solution.py:149
  41.9 6.6 %collective-permute-start.15 = (bf16[32,1024]{1,0:T(8,128)(2,1)S(1)}, bf16[32,1024]{1,0:T(8,128)(2,1)S(1)}, u32[]{:S(2)}, u32[]{:S(2)}) collective-permute-start(bf16[32,1024]{1,0:T(8,128)(2,1)S(1)} %get-tuple-element.28), channel_id=1, source_target_pairs={{0,3},{1,2},{2,1},{3,0},{4,7},{5,6},{6,5},{7,4},{8,11},{9,10},{10,... | collective-permute-start | bytes 196616 | tf_op jit(solution)/shard_map/ppermute | solution.py:149

commit v2 on v1

--- a/solution.py
+++ b/solution.py
@@ -1,4 +1,5 @@
 import functools
+import math
 
 import jax
 import jax.numpy as jnp
@@ -15,11 +16,7 @@
 
 
 def rows_of(refs):
-    if len(refs) == 1:
-        return refs[0][...]
-    if refs[0].shape[0] % 16 == 0:
-        return jnp.concatenate([r[...] for r in refs], axis=0)
-    return jnp.concatenate([r[...].astype(f32) for r in refs], axis=0).astype(bf16)
+    return below([r[...] for r in refs])
 
 
 def head_spread(first, last, width):
@@ -36,31 +33,45 @@
     return hi, mid, x - hi - mid
 
 
-def pool_kernel(me_ref, x_ref, kq_ref, wv_ref, *out_refs):
-    n_vars, groups, rows, width = x_ref.shape
-    me = me_ref[0]
-    x = jnp.concatenate(
-        [x_ref[v, me ^ k] for k in range(groups) for v in range(n_vars)], axis=0
-    ) if rows % 16 == 0 else jnp.concatenate(
-        [x_ref[v, me ^ k].astype(f32) for k in range(groups) for v in range(n_vars)], axis=0
-    ).astype(bf16)
+def below(blocks):
+    if blocks[0].shape[0] % 16 == 0:
+        return jnp.concatenate(blocks, axis=0)
+    return jnp.concatenate([b.astype(f32) for b in blocks], axis=0).astype(bf16)
+
+
+def pool_kernel(batch, x_hbm, kq_hbm, wv_hbm, *refs):
+    refs = refs[-len(batch) - 4 :]
+    out_refs, (x_ref, kq_ref, wv_ref, sem) = refs[:-4], refs[-4:]
+    me = lax.axis_index("var")
+    copies = [pltpu.make_async_copy(kq_hbm, kq_ref, sem.at[0])]
+    for i, k in enumerate(batch):
+        copies.append(pltpu.make_async_copy(x_hbm.at[:, me ^ k], x_ref.at[i], sem.at[2 + i]))
+    weights = pltpu.make_async_copy(wv_hbm, wv_ref, sem.at[1])
+    for copy in (*copies, weights):
+        copy.start()
+    for copy in copies:
+        copy.wait()
+    slots, n_vars, rows, width = x_ref.shape
+    x = below([x_ref[k, v] for k in range(slots) for v in range(n_vars)])
     kq = jnp.concatenate([kq_ref[...]] * (LANES // H), axis=0)
     scores = lax.dot_general(x, kq, (((1,), (1,)), ((), ())), preferred_element_type=f32)
-    scores = scores.reshape(groups, n_vars, rows, LANES)
+    scores = scores.reshape(slots, n_vars, rows, LANES)
     top = jnp.max(scores, axis=1)
     terms = jnp.exp(scores - top[:, None])
     total = jnp.sum(terms, axis=1)
-    share = (terms / total[:, None]).astype(bf16).reshape(groups * n_vars * rows, LANES)
-    weights = jnp.dot(share, head_spread(0, 1, width), preferred_element_type=f32)
-    values = jnp.dot(x, wv_ref[...], preferred_element_type=f32)
-    mean = jnp.sum((weights * values).reshape(groups, n_vars, rows, width), axis=1)
+    share = (terms / total[:, None]).astype(bf16).reshape(slots * n_vars * rows, LANES)
     lane = lax.broadcasted_iota(jnp.int32, (rows, LANES), 1) // H
-    for k in range(groups):
+    for k in range(slots):
         stats = jnp.zeros((rows, LANES), f32)
         for j, part in enumerate(split3(top[k]) + split3(total[k])):
             stats = jnp.where(lane == j, part, stats)
+        out_refs[k][:, width:] = stats.astype(bf16)
+    share = jnp.dot(share, head_spread(0, 1, width), preferred_element_type=f32)
+    weights.wait()
+    values = jnp.dot(x, wv_ref[...], preferred_element_type=f32)
+    mean = jnp.sum((share * values).reshape(slots, n_vars, rows, width), axis=1)
+    for k in range(slots):
         out_refs[k][:, :width] = mean[k].astype(bf16)
-        out_refs[k][:, width:] = stats.astype(bf16)
 
 
 def norm_kernel(gain_ref, *refs):
@@ -128,26 +139,30 @@
     out_ref[...] = functools.reduce(jnp.add, [r[...].astype(f32) for r in refs[:-1]]).astype(bf16)
 
 
-def call(kernel, out_shapes, *args, flops=0, smem=0, vmem=48):
-    vmem_spec = pl.BlockSpec(memory_space=pltpu.VMEM)
-    single = not isinstance(out_shapes, list)
-    outs = [out_shapes] if single else out_shapes
-    moved = sum(a.size * a.dtype.itemsize for a in (*args, *outs))
-    result = pl.pallas_call(
+def call(kernel, out_shapes, *args, flops=0, vmem=16, hbm=0, scratch=()):
+    spec = pl.BlockSpec(memory_space=pltpu.VMEM)
+    moved = sum(math.prod(a.shape) * jnp.dtype(a.dtype).itemsize for a in (*args, *out_shapes))
+    args = [
+        pltpu.with_memory_space_constraint(a, pltpu.HBM if i < hbm else pltpu.VMEM)
+        for i, a in enumerate(args)
+    ]
+    return pl.pallas_call(
         kernel,
-        out_shape=outs,
-        in_specs=[pl.BlockSpec(memory_space=pltpu.SMEM)] * smem + [vmem_spec] * (len(args) - smem),
-        out_specs=[vmem_spec] * len(outs),
+        out_shape=out_shapes,
+        in_specs=[pl.BlockSpec(memory_space=pltpu.HBM)] * hbm + [spec] * (len(args) - hbm),
+        out_specs=[spec] * len(out_shapes),
+        scratch_shapes=scratch,
         compiler_params=pltpu.CompilerParams(vmem_limit_bytes=vmem << 20),
         cost_estimate=pl.CostEstimate(flops=flops, bytes_accessed=moved, transcendentals=0),
     )(*args)
-    return result[0] if single else result
 
 
 def exchange(parts, axis, size):
-    return [parts[0]] + [
-        lax.ppermute(parts[k], axis, [(i, i ^ k) for i in range(size)]) for k in range(1, size)
+    got = [
+        lax.ppermute(parts[k], axis, [(i, i ^ k) for i in range(size)])
+        for k in reversed(range(1, size))
     ]
+    return [*got, parts[0]]
 
 
 def gather_space(block, size):
@@ -160,7 +175,8 @@
 
 def exchange_chips(block, size):
     return [block] + [
-        lax.ppermute(block, "space", [(i, i ^ k) for i in range(size)]) for k in range(2, size, 2)
+        lax.ppermute(block, "space", [(i, i ^ k) for i in range(size)])
+        for k in reversed(range(2, size, 2))
     ]
 
 
@@ -172,17 +188,24 @@
     n_vars, rows, width = var_tokens.shape
     part = rows // groups
     local = qkv_weight.shape[2]
-    me = lax.axis_index("var").astype(jnp.int32).reshape(1)
-
-    tokens = var_tokens.reshape(n_vars, groups, part, width)
-    shape = jax.ShapeDtypeStruct
-    sent = call(
-        pool_kernel,
-        [shape((part, width + LANES), bf16)] * groups,
-        me, tokens, key_query.T, value_weight,
-        flops=2 * n_vars * rows * width * width, smem=1,
-    )
-    got = exchange(sent, "var", groups)
+
+    shape = pltpu.VMEM
+    order = list(reversed(range(groups)))
+    sent = []
+    for batch in (order[: groups // 2], order[groups // 2 :]):
+        sent += call(
+            functools.partial(pool_kernel, batch),
+            [shape((part, width + LANES), bf16)] * len(batch),
+            var_tokens.reshape(n_vars, groups, part, width), key_query.T, value_weight, *sent[:1],
+            flops=2 * n_vars * part * width * width * len(batch), hbm=3, vmem=24,
+            scratch=[
+                pltpu.VMEM((len(batch), n_vars, part, width), bf16),
+                pltpu.VMEM((H, width), bf16),
+                pltpu.VMEM((width, width), bf16),
+                pltpu.SemaphoreType.DMA((2 + len(batch),)),
+            ],
+        )
+    got = exchange(sent[::-1], "var", groups)
     normed, pooled = call(
         norm_kernel, [shape((part, width), bf16)] * 2, norm_gain.reshape(1, width), *got
     )
@@ -195,17 +218,18 @@
     )
     kv_blocks = gather_space(kv, spaces)
     hidden = up_weight.shape[1]
-    ffn = call(
-        ffn_kernel, shape((rows, width), f32), up_weight, down_weight, *blocks,
+    (ffn,) = call(
+        ffn_kernel, [shape((rows, width), f32)], up_weight, down_weight, *blocks,
         flops=4 * rows * width * hidden,
     )
     sums = call(
         functools.partial(attend_kernel, H // groups, groups),
         [shape((part, width), bf16)] * groups,
         q, ffn, out_weight, *kv_blocks,
-        flops=4 * rows * rows * spaces * local,
-    )
-    return call(add_kernel, shape((part, width), bf16), pooled, *exchange(sums, "var", groups))
+        flops=4 * rows * rows * spaces * local, vmem=32,
+    )
+    (out,) = call(add_kernel, [jax.ShapeDtypeStruct((part, width), bf16)], pooled, *exchange(sums[::-1], "var", groups))
+    return out
 
 
 def solution(mesh):

time: 49.5 us -> 46.9 us (0.947)
  local copies, waits for them, and re-layouts: 5.02 us -> 0.03 us
  Pallas kernels: 6.47 us -> 9.41 us
  waiting for transfers between devices: 19.4 us -> 18.9 us
    unnamed x16 -> x10, local copies, waits for them, and re-layouts: 5.01 us -> 0.02 us
    pallas_call x6 -> x7, Pallas kernels: 6.47 us -> 9.41 us  [call(): pl.pallas_call(kernel, out_shape=out_shapes, in_specs=[pl.BlockSpec(memor...]
    ppermute x9, waiting for transfers between devices: 14.5 us -> 13 us  [exchange(): lax.ppermute(parts[k], axis, [(i, i ^ k) for i in range(size)])]
    ppermute x3, waiting for transfers between devices: 4.42 us -> 5.37 us  [exchange_chips(): lax.ppermute(block, 'space', [(i, i ^ k) for i in range(size)])]
  transfers between devices with their start and end apart: 16 -> 16, of which waited for: 10 -> 11; matrix products, arithmetic and copies ran while one was open for 0% -> 0% of each run, Pallas kernels for 2% -> 7%
where the time goes in v2:
time: 46.9 us; the launch traced here: 46.8 us
  waiting for transfers between devices  18.9 us (40%)
  starting transfers between devices  18.4 us (39%)
  Pallas kernels  9.41 us (20%)
    ppermute x9, starting transfers between devices, exchange(): lax.ppermute(parts[k], axis, [(i, i ^ k) for i in range(size)])  14.8 us
    ppermute x9, waiting for transfers between devices, exchange(): lax.ppermute(parts[k], axis, [(i, i ^ k) for i in range(size)])  13 us
    pallas_call x7, Pallas kernels, call(): pl.pallas_call(kernel, out_shape=out_shapes, in_specs=[pl.BlockSpec(memor...  9.41 us
    ppermute x3, waiting for transfers between devices, exchange_chips(): lax.ppermute(block, 'space', [(i, i ^ k) for i in range(size)])  5.37 us
    ppermute x3, starting transfers between devices, exchange_chips(): lax.ppermute(block, 'space', [(i, i ^ k) for i in range(size)])  3.55 us
  transfers between devices with their start and end apart: 16, of which 11 were waited for; matrix products, arithmetic and copies ran while one was open for 0% of the time, Pallas kernels for 7%

profile of v2, /device:TPU:0, one launch (start us, length us, event | category | flops | bytes accessed | tf_op | source)
XLA Modules:
  0.0 46.8 jit_solution(14309870783016494138)
XLA Ops:
  0.0 0.0 copy-start.2
  0.0 2.7 %shard_map.82 = (bf16[32,1152]{1,0:T(8,128)(2,1)S(1)}, bf16[32,1152]{1,0:T(8,128)(2,1)S(1)}) custom-call(bf16[4,4,32,1024]{3,2,1,0:T(8,128)(2,1)} %bitcast.4, bf16[16,1024]{1,0:T(8,128)(2,1)} %bitcast.6, bf16[1024,1024]{1,0:T(8,128)(2,1)} %wv_hbm.3), custom_call_target="tpu_custom_call" | custom-call | flops 536870912 | bytes 3325952 | tf_op jit(solution)/shard_map/pallas_call | solution.py:149
  2.7 0.0 copy-start.4
  2.7 4.1 %collective-permute-start.1 = (bf16[32,1152]{1,0:T(8,128)(2,1)S(1)}, bf16[32,1152]{1,0:T(8,128)(2,1)S(1)}, u32[]{:S(2)}, u32[]{:S(2)}) collective-permute-start(bf16[32,1152]{1,0:T(8,128)(2,1)S(1)} %get-tuple-element.18), channel_id=1, source_target_pairs={{0,2},{1,3},{2,0},{3,1},{4,6},{5,7},{6,4},{7,5},{8,10},{9,11},{10,... | collective-permute-start | bytes 221192 | tf_op jit(solution)/shard_map/ppermute | solution.py:162
  6.8 0.0 copy-start
  6.8 0.0 copy-start.1
  6.8 1.3 %collective-permute-start = (bf16[32,1152]{1,0:T(8,128)(2,1)S(1)}, bf16[32,1152]{1,0:T(8,128)(2,1)S(1)}, u32[]{:S(2)}, u32[]{:S(2)}) collective-permute-start(bf16[32,1152]{1,0:T(8,128)(2,1)S(1)} %get-tuple-element.17.refs_0_), channel_id=1, source_target_pairs={{0,3},{1,2},{2,1},{3,0},{4,7},{5,6},{6,5},{7,4},{8,11},{9,10},{10,... | collective-permute-start | bytes 221192 | tf_op jit(solution)/shard_map/ppermute | solution.py:162
  8.2 2.6 %shard_map.83 = (bf16[32,1152]{1,0:T(8,128)(2,1)S(1)}, bf16[32,1152]{1,0:T(8,128)(2,1)S(1)}) custom-call(bf16[4,4,32,1024]{3,2,1,0:T(8,128)(2,1)} %bitcast.5, bf16[16,1024]{1,0:T(8,128)(2,1)} %bitcast.7, bf16[1024,1024]{1,0:T(8,128)(2,1)} %wv_hbm.3, bf16[32,1152]{1,0:T(8,128)(2,1)S(1)} %get-tuple-element.17.refs_0_), custom_call_target="tpu_custom_call" | custom-call | flops 536870912 | bytes 3399680 | tf_op jit(solution)/shard_map/pallas_call | solution.py:149
  10.8 0.4 collective-permute-start.2
  11.3 0.0 copy-done.4
  11.3 0.5 collective-permute-done.1.refs_1_
  11.7 1.4 %collective-permute-done.refs_0_ = bf16[32,1152]{1,0:T(8,128)(2,1)S(1)} collective-permute-done((bf16[32,1152]{1,0:T(8,128)(2,1)S(1)}, bf16[32,1152]{1,0:T(8,128)(2,1)S(1)}, u32[]{:S(2)}, u32[]{:S(2)}) %collective-permute-start) | collective-permute-done | bytes 73760 | tf_op jit(solution)/shard_map/ppermute | solution.py:162
  13.1 2.1 %collective-permute-done.2.refs_2_ = bf16[32,1152]{1,0:T(8,128)(2,1)S(1)} collective-permute-done((bf16[32,1152]{1,0:T(8,128)(2,1)S(1)}, bf16[32,1152]{1,0:T(8,128)(2,1)S(1)}, u32[]{:S(2)}, u32[]{:S(2)}) %collective-permute-start.2) | collective-permute-done | bytes 73760 | tf_op jit(solution)/shard_map/ppermute | solution.py:162
  15.2 0.5 %shard_map.84 = (bf16[32,1024]{1,0:T(8,128)(2,1)S(1)}, bf16[32,1024]{1,0:T(8,128)(2,1)S(1)}) custom-call(bf16[1,1024]{1,0:T(2,128)(2,1)S(1)} %reshape.7.gain_ref, bf16[32,1152]{1,0:T(8,128)(2,1)S(1)} %collective-permute-done.refs_0_, bf16[32,1152]{1,0:T(8,128)(2,1)S(1)} %collective-permute-done.1.refs_1_, ...), custom_call_target="tpu_custom_call" | custom-call | bytes 428032 | tf_op jit(solution)/shard_map/pallas_call | solution.py:149
  15.8 0.4 collective-permute-start.5
  16.2 2.7 %collective-permute-start.4 = (bf16[32,1024]{1,0:T(8,128)(2,1)S(1)}, bf16[32,1024]{1,0:T(8,128)(2,1)S(1)}, u32[]{:S(2)}, u32[]{:S(2)}) collective-permute-start(bf16[32,1024]{1,0:T(8,128)(2,1)S(1)} %get-tuple-element.22.refs_3_), channel_id=1, source_target_pairs={{0,2},{1,3},{2,0},{3,1},{4,6},{5,7},{6,4},{7,5},{8,10},{9,11},{10,... | collective-permute-start | bytes 196616 | tf_op jit(solution)/shard_map/ppermute | solution.py:162
  18.9 1.3 %collective-permute-start.3 = (bf16[32,1024]{1,0:T(8,128)(2,1)S(1)}, bf16[32,1024]{1,0:T(8,128)(2,1)S(1)}, u32[]{:S(2)}, u32[]{:S(2)}) collective-permute-start(bf16[32,1024]{1,0:T(8,128)(2,1)S(1)} %get-tuple-element.22.refs_3_), channel_id=1, source_target_pairs={{0,3},{1,2},{2,1},{3,0},{4,7},{5,6},{6,5},{7,4},{8,11},{9,10},{10,... | collective-permute-start | bytes 196616 | tf_op jit(solution)/shard_map/ppermute | solution.py:162
  20.2 0.0 collective-permute-done.5.refs_2_
  20.2 3.0 %collective-permute-done.4.refs_1_ = bf16[32,1024]{1,0:T(8,128)(2,1)S(1)} collective-permute-done((bf16[32,1024]{1,0:T(8,128)(2,1)S(1)}, bf16[32,1024]{1,0:T(8,128)(2,1)S(1)}, u32[]{:S(2)}, u32[]{:S(2)}) %collective-permute-start.4) | collective-permute-done | bytes 65568 | tf_op jit(solution)/shard_map/ppermute | solution.py:162
  23.2 1.7 %collective-permute-done.3.refs_0_ = bf16[32,1024]{1,0:T(8,128)(2,1)S(1)} collective-permute-done((bf16[32,1024]{1,0:T(8,128)(2,1)S(1)}, bf16[32,1024]{1,0:T(8,128)(2,1)S(1)}, u32[]{:S(2)}, u32[]{:S(2)}) %collective-permute-start.3) | collective-permute-done | bytes 65568 | tf_op jit(solution)/shard_map/ppermute | solution.py:162
  24.9 0.0 copy-done.2
  24.9 0.4 shard_map.85
  25.3 0.0 copy-start.3
  25.4 1.5 %collective-permute-start.8 = (bf16[128,512]{1,0:T(8,128)(2,1)S(1)}, bf16[128,512]{1,0:T(8,128)(2,1)S(1)}, u32[]{:S(2)}, u32[]{:S(2)}) collective-permute-start(bf16[128,512]{1,0:T(8,128)(2,1)S(1)} %get-tuple-element.24.refs_0_), channel_id=1, source_target_pairs={{0,8},{4,12},{8,0},{12,4},{16,24},{20,28},{24,16},{28,20},{1,9},{5... | collective-permute-start | bytes 393224 | tf_op jit(solution)/shard_map/ppermute | solution.py:178
  26.9 1.5 %collective-permute-start.7 = (bf16[128,512]{1,0:T(8,128)(2,1)S(1)}, bf16[128,512]{1,0:T(8,128)(2,1)S(1)}, u32[]{:S(2)}, u32[]{:S(2)}) collective-permute-start(bf16[128,512]{1,0:T(8,128)(2,1)S(1)} %get-tuple-element.24.refs_0_), channel_id=1, source_target_pairs={{0,16},{4,20},{8,24},{12,28},{16,0},{20,4},{24,8},{28,12},{1,17},{... | collective-permute-start | bytes 393224 | tf_op jit(solution)/shard_map/ppermute | solution.py:178
  28.4 0.5 %collective-permute-start.6 = (bf16[128,512]{1,0:T(8,128)(2,1)S(1)}, bf16[128,512]{1,0:T(8,128)(2,1)S(1)}, u32[]{:S(2)}, u32[]{:S(2)}) collective-permute-start(bf16[128,512]{1,0:T(8,128)(2,1)S(1)} %get-tuple-element.24.refs_0_), channel_id=1, source_target_pairs={{0,24},{4,28},{8,16},{12,20},{16,8},{20,12},{24,0},{28,4},{1,25},{... | collective-permute-start | bytes 393224 | tf_op jit(solution)/shard_map/ppermute | solution.py:178
  28.9 0.0 collective-permute-start.9
  28.9 1.8 %collective-permute-done.8.refs_3_ = bf16[128,512]{1,0:T(8,128)(2,1)S(1)} collective-permute-done((bf16[128,512]{1,0:T(8,128)(2,1)S(1)}, bf16[128,512]{1,0:T(8,128)(2,1)S(1)}, u32[]{:S(2)}, u32[]{:S(2)}) %collective-permute-start.8) | collective-permute-done | bytes 131104 | tf_op jit(solution)/shard_map/ppermute | solution.py:178
  30.7 0.0 collective-permute-start.12
  30.7 1.2 %collective-permute-done.7.refs_2_ = bf16[128,512]{1,0:T(8,128)(2,1)S(1)} collective-permute-done((bf16[128,512]{1,0:T(8,128)(2,1)S(1)}, bf16[128,512]{1,0:T(8,128)(2,1)S(1)}, u32[]{:S(2)}, u32[]{:S(2)}) %collective-permute-start.7) | collective-permute-done | bytes 131104 | tf_op jit(solution)/shard_map/ppermute | solution.py:178
  31.9 0.0 collective-permute-start.11
  31.9 2.4 %collective-permute-done.6.refs_1_ = bf16[128,512]{1,0:T(8,128)(2,1)S(1)} collective-permute-done((bf16[128,512]{1,0:T(8,128)(2,1)S(1)}, bf16[128,512]{1,0:T(8,128)(2,1)S(1)}, u32[]{:S(2)}, u32[]{:S(2)}) %collective-permute-start.6) | collective-permute-done | bytes 131104 | tf_op jit(solution)/shard_map/ppermute | solution.py:178
  34.3 0.0 collective-permute-start.10
  34.3 0.0 copy-done
  34.3 0.0 copy-done.1
  34.3 0.8 %shard_map.86.ffn_ref = f32[128,1024]{1,0:T(8,128)S(1)} custom-call(bf16[1024,1024]{1,0:T(8,128)(2,1)S(1)} %copy-done, bf16[1024,1024]{1,0:T(8,128)(2,1)S(1)} %copy-done.1, bf16[32,1024]{1,0:T(8,128)(2,1)S(1)} %collective-permute-done.3.refs_0_, bf16[32,1024]{1,0:T(8,128)(2,1)S(1)} %collective-permute-done.4.refs_1_, ...), custom_call_target="tpu_custom_call" | custom-call | flops 536870912 | bytes 4980736 | tf_op jit(solution)/shard_map/pallas_call | solution.py:149
  35.1 0.0 collective-permute-done.9.refs_4_
  35.2 0.0 collective-permute-done.12.refs_7_
  35.2 0.0 collective-permute-done.11.refs_6_
  35.2 0.5 collective-permute-done.10.refs_5_
  35.6 0.0 copy-done.3
  35.6 1.7 %shard_map.87 = (bf16[32,1024]{1,0:T(8,128)(2,1)S(1)}, bf16[32,1024]{1,0:T(8,128)(2,1)S(1)}, bf16[32,1024]{1,0:T(8,128)(2,1)S(1)}, bf16[32,1024]{1,0:T(8,128)(2,1)S(1)}) custom-call(bf16[128,256]{1,0:T(8,128)(2,1)S(1)} %get-tuple-element.23.q_ref, f32[128,1024]{1,0:T(8,128)S(1)} %shard_map.86.ffn_ref, bf16[256,1024]{1,0:T(8,128)(2,1)S(1)} %copy-done.3, ...), custom_call_target="tpu_custom_call" | custom-call | flops 134217728 | bytes 2424832 | tf_op jit(solution)/shard_map/pallas_call | solution.py:149
  37.3 1.6 %collective-permute-start.13 = (bf16[32,1024]{1,0:T(8,128)(2,1)S(1)}, bf16[32,1024]{1,0:T(8,128)(2,1)S(1)}, u32[]{:S(2)}, u32[]{:S(2)}) collective-permute-start(bf16[32,1024]{1,0:T(8,128)(2,1)S(1)} %get-tuple-element.25), channel_id=1, source_target_pairs={{0,3},{1,2},{2,1},{3,0},{4,7},{5,6},{6,5},{7,4},{8,11},{9,10},{10,... | collective-permute-start | bytes 196616 | tf_op jit(solution)/shard_map/ppermute | solution.py:162
  38.9 0.0 collective-permute-start.14
  38.9 2.8 %collective-permute-start.15 = (bf16[32,1024]{1,0:T(8,128)(2,1)S(1)}, bf16[32,1024]{1,0:T(8,128)(2,1)S(1)}, u32[]{:S(2)}, u32[]{:S(2)}) collective-permute-start(bf16[32,1024]{1,0:T(8,128)(2,1)S(1)} %get-tuple-element.27), channel_id=1, source_target_pairs={{0,1},{1,0},{2,3},{3,2},{4,5},{5,4},{6,7},{7,6},{8,9},{9,8},{10,11... | collective-permute-start | bytes 196616 | tf_op jit(solution)/shard_map/ppermute | solution.py:162
  41.8 2.4 %collective-permute-done.13.refs_1_ = bf16[32,1024]{1,0:T(8,128)(2,1)S(1)} collective-permute-done((bf16[32,1024]{1,0:T(8,128)(2,1)S(1)}, bf16[32,1024]{1,0:T(8,128)(2,1)S(1)}, u32[]{:S(2)}, u32[]{:S(2)}) %collective-permute-start.13) | collective-permute-done | bytes 65568 | tf_op jit(solution)/shard_map/ppermute | solution.py:162
  44.1 2.0 %collective-permute-done.14.refs_2_ = bf16[32,1024]{1,0:T(8,128)(2,1)S(1)} collective-permute-done((bf16[32,1024]{1,0:T(8,128)(2,1)S(1)}, bf16[32,1024]{1,0:T(8,128)(2,1)S(1)}, u32[]{:S(2)}, u32[]{:S(2)}) %collective-permute-start.14) | collective-permute-done | bytes 65568 | tf_op jit(solution)/shard_map/ppermute | solution.py:162
  46.1 0.0 collective-permute-done.15.refs_3_
  46.1 0.7 %shard_map.88 = bf16[32,1024]{1,0:T(8,128)(2,1)} custom-call(bf16[32,1024]{1,0:T(8,128)(2,1)S(1)} %get-tuple-element.21.refs_0_, bf16[32,1024]{1,0:T(8,128)(2,1)S(1)} %collective-permute-done.13.refs_1_, bf16[32,1024]{1,0:T(8,128)(2,1)S(1)} %collective-permute-done.14.refs_2_, bf16[32,1024]{1,0:T(8,128)(2,1)S(1)} %collective-permute-done.15.refs_3_, ...), custom_call_target="tpu_custom_call" | custom-call | bytes 393216 | tf_op jit(solution)/shard_map/pallas_call | solution.py:149
  (1 shorter events, 0.0 us)
Async XLA Ops:
  0.0 24.9 %copy-start.2 = (bf16[1024,3,256]{2,0,1:T(8,128)(2,1)S(1)}, bf16[1024,3,256]{2,0,1:T(8,128)(2,1)}, u32[]{:S(2)}) copy-start(bf16[1024,3,256]{2,0,1:T(8,128)(2,1)} %param.11) | copy-start | bytes 4718596
  2.7 8.5 %copy-start.4 = (bf16[1024]{0:T(1024)(128)(2,1)S(1)}, bf16[1024]{0:T(1024)(128)(2,1)}, u32[]{:S(2)}) copy-start(bf16[1024]{0:T(1024)(128)(2,1)} %param.15) | copy-start | bytes 6148
  2.7 9.0 %collective-permute-start.1 = (bf16[32,1152]{1,0:T(8,128)(2,1)S(1)}, bf16[32,1152]{1,0:T(8,128)(2,1)S(1)}, u32[]{:S(2)}, u32[]{:S(2)}) collective-permute-start(bf16[32,1152]{1,0:T(8,128)(2,1)S(1)} %get-tuple-element.18), channel_id=1, source_target_pairs={{0,2},{1,3},{2,0},{3,1},{4,6},{5,7},{6,4},{7,5},{8,10},{9,11},{10,... | collective-permute-start | bytes 221192 | tf_op jit(solution)/shard_map/ppermute | solution.py:162
  6.8 27.4 %copy-start = (bf16[1024,1024]{1,0:T(8,128)(2,1)S(1)}, bf16[1024,1024]{1,0:T(8,128)(2,1)}, u32[]{:S(2)}) copy-start(bf16[1024,1024]{1,0:T(8,128)(2,1)} %up_ref.1) | copy-start | bytes 6291460
  6.8 27.5 %copy-start.1 = (bf16[1024,1024]{1,0:T(8,128)(2,1)S(1)}, bf16[1024,1024]{1,0:T(8,128)(2,1)}, u32[]{:S(2)}) copy-start(bf16[1024,1024]{1,0:T(8,128)(2,1)} %down_ref.1) | copy-start | bytes 6291460
  6.8 6.3 %collective-permute-start = (bf16[32,1152]{1,0:T(8,128)(2,1)S(1)}, bf16[32,1152]{1,0:T(8,128)(2,1)S(1)}, u32[]{:S(2)}, u32[]{:S(2)}) collective-permute-start(bf16[32,1152]{1,0:T(8,128)(2,1)S(1)} %get-tuple-element.17.refs_0_), channel_id=1, source_target_pairs={{0,3},{1,2},{2,1},{3,0},{4,7},{5,6},{6,5},{7,4},{8,11},{9,10},{10,... | collective-permute-start | bytes 221192 | tf_op jit(solution)/shard_map/ppermute | solution.py:162
  10.8 4.4 %collective-permute-start.2 = (bf16[32,1152]{1,0:T(8,128)(2,1)S(1)}, bf16[32,1152]{1,0:T(8,128)(2,1)S(1)}, u32[]{:S(2)}, u32[]{:S(2)}) collective-permute-start(bf16[32,1152]{1,0:T(8,128)(2,1)S(1)} %get-tuple-element.19), channel_id=1, source_target_pairs={{0,1},{1,0},{2,3},{3,2},{4,5},{5,4},{6,7},{7,6},{8,9},{9,8},{10,11... | collective-permute-start | bytes 221192 | tf_op jit(solution)/shard_map/ppermute | solution.py:162
  15.8 4.5 %collective-permute-start.5 = (bf16[32,1024]{1,0:T(8,128)(2,1)S(1)}, bf16[32,1024]{1,0:T(8,128)(2,1)S(1)}, u32[]{:S(2)}, u32[]{:S(2)}) collective-permute-start(bf16[32,1024]{1,0:T(8,128)(2,1)S(1)} %get-tuple-element.22.refs_3_), channel_id=1, source_target_pairs={{0,1},{1,0},{2,3},{3,2},{4,5},{5,4},{6,7},{7,6},{8,9},{9,8},{10,11... | collective-permute-start | bytes 196616 | tf_op jit(solution)/shard_map/ppermute | solution.py:162
  16.2 7.0 %collective-permute-start.4 = (bf16[32,1024]{1,0:T(8,128)(2,1)S(1)}, bf16[32,1024]{1,0:T(8,128)(2,1)S(1)}, u32[]{:S(2)}, u32[]{:S(2)}) collective-permute-start(bf16[32,1024]{1,0:T(8,128)(2,1)S(1)} %get-tuple-element.22.refs_3_), channel_id=1, source_target_pairs={{0,2},{1,3},{2,0},{3,1},{4,6},{5,7},{6,4},{7,5},{8,10},{9,11},{10,... | collective-permute-start | bytes 196616 | tf_op jit(solution)/shard_map/ppermute | solution.py:162
  18.9 6.1 %collective-permute-start.3 = (bf16[32,1024]{1,0:T(8,128)(2,1)S(1)}, bf16[32,1024]{1,0:T(8,128)(2,1)S(1)}, u32[]{:S(2)}, u32[]{:S(2)}) collective-permute-start(bf16[32,1024]{1,0:T(8,128)(2,1)S(1)} %get-tuple-element.22.refs_3_), channel_id=1, source_target_pairs={{0,3},{1,2},{2,1},{3,0},{4,7},{5,6},{6,5},{7,4},{8,11},{9,10},{10,... | collective-permute-start | bytes 196616 | tf_op jit(solution)/shard_map/ppermute | solution.py:162
  25.3 10.3 %copy-start.3 = (bf16[256,1024]{1,0:T(8,128)(2,1)S(1)}, bf16[256,1024]{1,0:T(8,128)(2,1)}, u32[]{:S(2)}) copy-start(bf16[256,1024]{1,0:T(8,128)(2,1)} %wo_ref.1) | copy-start | bytes 1572868
  25.4 5.4 %collective-permute-start.8 = (bf16[128,512]{1,0:T(8,128)(2,1)S(1)}, bf16[128,512]{1,0:T(8,128)(2,1)S(1)}, u32[]{:S(2)}, u32[]{:S(2)}) collective-permute-start(bf16[128,512]{1,0:T(8,128)(2,1)S(1)} %get-tuple-element.24.refs_0_), channel_id=1, source_target_pairs={{0,8},{4,12},{8,0},{12,4},{16,24},{20,28},{24,16},{28,20},{1,9},{5... | collective-permute-start | bytes 393224 | tf_op jit(solution)/shard_map/ppermute | solution.py:178
  26.9 5.0 %collective-permute-start.7 = (bf16[128,512]{1,0:T(8,128)(2,1)S(1)}, bf16[128,512]{1,0:T(8,128)(2,1)S(1)}, u32[]{:S(2)}, u32[]{:S(2)}) collective-permute-start(bf16[128,512]{1,0:T(8,128)(2,1)S(1)} %get-tuple-element.24.refs_0_), channel_id=1, source_target_pairs={{0,16},{4,20},{8,24},{12,28},{16,0},{20,4},{24,8},{28,12},{1,17},{... | collective-permute-start | bytes 393224 | tf_op jit(solution)/shard_map/ppermute | solution.py:178
  28.4 5.9 %collective-permute-start.6 = (bf16[128,512]{1,0:T(8,128)(2,1)S(1)}, bf16[128,512]{1,0:T(8,128)(2,1)S(1)}, u32[]{:S(2)}, u32[]{:S(2)}) collective-permute-start(bf16[128,512]{1,0:T(8,128)(2,1)S(1)} %get-tuple-element.24.refs_0_), channel_id=1, source_target_pairs={{0,24},{4,28},{8,16},{12,20},{16,8},{20,12},{24,0},{28,4},{1,25},{... | collective-permute-start | bytes 393224 | tf_op jit(solution)/shard_map/ppermute | solution.py:178
  28.9 6.2 %collective-permute-start.9 = (bf16[128,512]{1,0:T(8,128)(2,1)S(1)}, bf16[128,512]{1,0:T(8,128)(2,1)S(1)}, u32[]{:S(2)}, u32[]{:S(2)}) collective-permute-start(bf16[128,512]{1,0:T(8,128)(2,1)S(1)} %get-tuple-element.24.refs_0_), channel_id=1, source_target_pairs={{0,4},{4,0},{8,12},{12,8},{16,20},{20,16},{24,28},{28,24},{1,5},{5... | collective-permute-start | bytes 393224 | tf_op jit(solution)/shard_map/ppermute | solution.py:173
  30.7 4.4 %collective-permute-start.12 = (bf16[128,512]{1,0:T(8,128)(2,1)S(1)}, bf16[128,512]{1,0:T(8,128)(2,1)S(1)}, u32[]{:S(2)}, u32[]{:S(2)}) collective-permute-start(bf16[128,512]{1,0:T(8,128)(2,1)S(1)} %collective-permute-done.8.refs_3_), channel_id=1, source_target_pairs={{0,4},{4,0},{8,12},{12,8},{16,20},{20,16},{24,28},{28,24},{1,5},{5... | collective-permute-start | bytes 393224 | tf_op jit(solution)/shard_map/ppermute | solution.py:173
  31.9 3.3 %collective-permute-start.11 = (bf16[128,512]{1,0:T(8,128)(2,1)S(1)}, bf16[128,512]{1,0:T(8,128)(2,1)S(1)}, u32[]{:S(2)}, u32[]{:S(2)}) collective-permute-start(bf16[128,512]{1,0:T(8,128)(2,1)S(1)} %collective-permute-done.7.refs_2_), channel_id=1, source_target_pairs={{0,4},{4,0},{8,12},{12,8},{16,20},{20,16},{24,28},{28,24},{1,5},{5... | collective-permute-start | bytes 393224 | tf_op jit(solution)/shard_map/ppermute | solution.py:173
  34.3 1.3 %collective-permute-start.10 = (bf16[128,512]{1,0:T(8,128)(2,1)S(1)}, bf16[128,512]{1,0:T(8,128)(2,1)S(1)}, u32[]{:S(2)}, u32[]{:S(2)}) collective-permute-start(bf16[128,512]{1,0:T(8,128)(2,1)S(1)} %collective-permute-done.6.refs_1_), channel_id=1, source_target_pairs={{0,4},{4,0},{8,12},{12,8},{16,20},{20,16},{24,28},{28,24},{1,5},{5... | collective-permute-start | bytes 393224 | tf_op jit(solution)/shard_map/ppermute | solution.py:173
  37.3 6.8 %collective-permute-start.13 = (bf16[32,1024]{1,0:T(8,128)(2,1)S(1)}, bf16[32,1024]{1,0:T(8,128)(2,1)S(1)}, u32[]{:S(2)}, u32[]{:S(2)}) collective-permute-start(bf16[32,1024]{1,0:T(8,128)(2,1)S(1)} %get-tuple-element.25), channel_id=1, source_target_pairs={{0,3},{1,2},{2,1},{3,0},{4,7},{5,6},{6,5},{7,4},{8,11},{9,10},{10,... | collective-permute-start | bytes 196616 | tf_op jit(solution)/shard_map/ppermute | solution.py:162
  38.9 7.2 %collective-permute-start.14 = (bf16[32,1024]{1,0:T(8,128)(2,1)S(1)}, bf16[32,1024]{1,0:T(8,128)(2,1)S(1)}, u32[]{:S(2)}, u32[]{:S(2)}) collective-permute-start(bf16[32,1024]{1,0:T(8,128)(2,1)S(1)} %get-tuple-element.26), channel_id=1, source_target_pairs={{0,2},{1,3},{2,0},{3,1},{4,6},{5,7},{6,4},{7,5},{8,10},{9,11},{10,... | collective-permute-start | bytes 196616 | tf_op jit(solution)/shard_map/ppermute | solution.py:162
  38.9 7.2 %collective-permute-start.15 = (bf16[32,1024]{1,0:T(8,128)(2,1)S(1)}, bf16[32,1024]{1,0:T(8,128)(2,1)S(1)}, u32[]{:S(2)}, u32[]{:S(2)}) collective-permute-start(bf16[32,1024]{1,0:T(8,128)(2,1)S(1)} %get-tuple-element.27), channel_id=1, source_target_pairs={{0,1},{1,0},{2,3},{3,2},{4,5},{5,4},{6,7},{7,6},{8,9},{9,8},{10,11... | collective-permute-start | bytes 196616 | tf_op jit(solution)/shard_map/ppermute | solution.py:162

commit v3 on v2

v3 whole, which is shorter than its diff:
```python
import functools
import math

import jax
import jax.numpy as jnp
from jax import lax
from jax.experimental import pallas as pl
from jax.experimental.pallas import tpu as pltpu
from jax.sharding import PartitionSpec as P

H = 16
LANES = 128
EPS = 1e-05
f32 = jnp.float32
bf16 = jnp.bfloat16


def rows_of(refs):
    return below([r[...] for r in refs])


def head_spread(first, last, width):
    lane = lax.broadcasted_iota(jnp.int32, (LANES, width), 0)
    column = lax.broadcasted_iota(jnp.int32, (LANES, width), 1)
    group = lane // H
    hit = (lane % H == column // (width // H)) & (group >= first) & (group < last)
    return hit.astype(bf16)


def split3(x):
    hi = x.astype(bf16).astype(f32)
    mid = (x - hi).astype(bf16).astype(f32)
    return hi, mid, x - hi - mid


def below(blocks):
    if blocks[0].shape[0] % 16 == 0:
        return jnp.concatenate(blocks, axis=0)
    return jnp.concatenate([b.astype(f32) for b in blocks], axis=0).astype(bf16)


def load_kernel(x_hbm, kq_hbm, wv_hbm, tokens_any, wv_any, share_ref, stats_ref, x_ref, kq_ref, sem):
    me = lax.axis_index("var")
    slots, n_vars, rows, _ = x_ref.shape
    copies = [pltpu.make_async_copy(kq_hbm, kq_ref, sem.at[0])]
    for k in range(slots):
        copies.append(pltpu.make_async_copy(x_hbm.at[:, me ^ k], x_ref.at[k], sem.at[3 + k]))
    weights = pltpu.make_async_copy(wv_hbm, wv_any, sem.at[1])
    for copy in (*copies, weights):
        copy.start()
    for copy in copies:
        copy.wait()
    passing = pltpu.make_async_copy(x_ref, tokens_any, sem.at[2])
    passing.start()
    x = below([x_ref[k, v] for k in range(slots) for v in range(n_vars)])
    kq = jnp.concatenate([kq_ref[...]] * (LANES // H), axis=0)
    scores = lax.dot_general(x, kq, (((1,), (1,)), ((), ())), preferred_element_type=f32)
    scores = scores.reshape(slots, n_vars, rows, LANES)
    top = jnp.max(scores, axis=1)
    terms = jnp.exp(scores - top[:, None])
    total = jnp.sum(terms, axis=1)
    share_ref[...] = (terms / total[:, None]).astype(bf16)
    lane = lax.broadcasted_iota(jnp.int32, top.shape, 2) // H
    stats = jnp.zeros(top.shape, f32)
    for j, part in enumerate(split3(top) + split3(total)):
        stats = jnp.where(lane == j, part, stats)
    stats_ref[...] = stats.astype(bf16)
    passing.wait()
    weights.wait()


def pool_kernel(slot, x_ref, wv_ref, share_ref, stats_ref, *refs):
    out_ref = refs[-1]
    n_vars, rows, width = x_ref.shape[1:]
    share = below([share_ref[slot, v] for v in range(n_vars)])
    share = jnp.dot(share, head_spread(0, 1, width), preferred_element_type=f32)
    x = below([x_ref[slot, v] for v in range(n_vars)])
    values = jnp.dot(x, wv_ref[...], preferred_element_type=f32)
    mean = jnp.sum((share * values).reshape(n_vars, rows, width), axis=0)
    out_ref[:, :width] = mean.astype(bf16)
    out_ref[:, width:] = stats_ref[slot]


def norm_kernel(gain_ref, *refs):
    parts, (normed_ref, pooled_ref) = refs[:-2], refs[-2:]
    rows, width = normed_ref.shape
    to_top = head_spread(0, 3, width)
    to_total = head_spread(3, 6, width)
    tops = [jnp.dot(p[:, width:], to_top, preferred_element_type=f32) for p in parts]
    totals = [jnp.dot(p[:, width:], to_total, preferred_element_type=f32) for p in parts]
    top = functools.reduce(jnp.maximum, tops)
    scales = [t * jnp.exp(m - top) for t, m in zip(totals, tops)]
    summed = functools.reduce(
        jnp.add, [s * p[:, :width].astype(f32) for s, p in zip(scales, parts)]
    )
    pooled = (summed / functools.reduce(jnp.add, scales)).astype(bf16)
    pooled_ref[...] = pooled
    pooled = pooled.astype(f32)
    centered = pooled - jnp.mean(pooled, axis=1, keepdims=True)
    spread = jnp.mean(centered * centered, axis=1, keepdims=True)
    normed_ref[...] = (centered * lax.rsqrt(spread + EPS) * gain_ref[...].astype(f32)).astype(bf16)


def qkv_kernel(w_ref, *refs):
    blocks, (q_ref, kv_ref) = refs[:-2], refs[-2:]
    x = rows_of(blocks)
    width = q_ref.shape[1]
    q_ref[...] = jnp.dot(x, w_ref[0], preferred_element_type=f32).astype(bf16)
    kv_ref[:, :width] = jnp.dot(x, w_ref[1], preferred_element_type=f32).astype(bf16)
    kv_ref[:, width:] = jnp.dot(x, w_ref[2], preferred_element_type=f32).astype(bf16)


def ffn_kernel(up_ref, down_ref, *refs):
    blocks, out_ref = refs[:-3], refs[-2]
    x = rows_of(blocks)
    hidden = jnp.dot(x, up_ref[...], preferred_element_type=f32)
    hidden = jax.nn.gelu(hidden, approximate=True).astype(bf16)
    out_ref[...] = jnp.dot(hidden, down_ref[...], preferred_element_type=f32)


def attend(heads, q_ref, blocks):
    rows, width = q_ref.shape
    head_dim = width // heads
    q = q_ref[...].astype(f32) * head_dim ** (-0.5)
    owner = lax.broadcasted_iota(jnp.int32, (rows, width), 1) // head_dim
    stacked = jnp.concatenate([jnp.where(owner == h, q, 0.0) for h in range(heads)], axis=0)
    stacked = stacked.astype(bf16)
    keys = jnp.concatenate([b[:, :width] for b in blocks], axis=0)
    vals = jnp.concatenate([b[:, width:] for b in blocks], axis=0)
    logits = lax.dot_general(stacked, keys, (((1,), (1,)), ((), ())), preferred_element_type=f32)
    top = jnp.max(logits, axis=1, keepdims=True)
    terms = jnp.exp(logits - top)
    total = jnp.sum(terms, axis=1, keepdims=True)
    mixed = jnp.dot(terms.astype(bf16), vals, preferred_element_type=f32)

    def own_head(stack):
        out = jnp.broadcast_to(stack[:rows], (rows, width))
        for h in range(1, heads):
            out = jnp.where(owner == h, stack[h * rows : (h + 1) * rows], out)
        return out

    return own_head(mixed), own_head(top), own_head(total)


def early_kernel(heads, q_ref, *refs):
    blocks, out_refs = refs[:-3], refs[-3:]
    for ref, value in zip(out_refs, attend(heads, q_ref, blocks)):
        ref[...] = value


def attend_kernel(heads, groups, q_ref, ffn_ref, wo_ref, mixed_ref, top_ref, total_ref, *refs):
    blocks, out_refs = refs[:-groups], refs[-groups:]
    mixed, top, total = attend(heads, q_ref, blocks)
    both = jnp.maximum(top, top_ref[...])
    late, early = jnp.exp(top - both), jnp.exp(top_ref[...] - both)
    attended = (mixed * late + mixed_ref[...] * early) / (total * late + total_ref[...] * early)
    out = jnp.dot(attended.astype(bf16), wo_ref[...], preferred_element_type=f32) + ffn_ref[...]
    part = out.shape[0] // groups
    for k in range(groups):
        out_refs[k][...] = out[k * part : (k + 1) * part].astype(bf16)


def add_kernel(*refs):
    out_ref = refs[-1]
    out_ref[...] = functools.reduce(jnp.add, [r[...].astype(f32) for r in refs[:-1]]).astype(bf16)


def call(kernel, out_shapes, *args, flops=0, vmem=16, hbm=0, scratch=(), any_outs=(), aliases={}):
    moved = sum(math.prod(a.shape) * jnp.dtype(a.dtype).itemsize for a in (*args, *out_shapes))
    args = [
        pltpu.with_memory_space_constraint(a, pltpu.HBM if i < hbm else pltpu.VMEM)
        for i, a in enumerate(args)
    ]
    in_specs = [pl.BlockSpec(memory_space=pltpu.HBM if i < hbm else pltpu.VMEM) for i in range(len(args))]
    out_specs = [pl.BlockSpec(memory_space=pltpu.VMEM)] * len(out_shapes)
    for i in any_outs:
        out_specs[i] = pl.BlockSpec(memory_space=pl.ANY)
    for i, o in aliases.items():
        in_specs[i] = out_specs[o] = pl.BlockSpec(memory_space=pl.ANY)
    return pl.pallas_call(
        kernel,
        out_shape=out_shapes,
        in_specs=in_specs,
        out_specs=out_specs,
        input_output_aliases=aliases,
        scratch_shapes=scratch,
        compiler_params=pltpu.CompilerParams(vmem_limit_bytes=vmem << 20),
        cost_estimate=pl.CostEstimate(flops=flops, bytes_accessed=moved, transcendentals=0),
    )(*args)


def exchange(parts, axis, size):
    got = [
        lax.ppermute(parts[k], axis, [(i, i ^ k) for i in range(size)])
        for k in reversed(range(1, size))
    ]
    return [*got, parts[0]]


def gather_space(block, size, between):
    if size > 8:
        blocks = between(lax.all_gather(block, "space", axis=0, tiled=True))
        half = blocks.shape[0] // 2
        return [blocks[:half]], [blocks[half:]]
    blocks = [block] + [
        lax.ppermute(block, "space", [(i, i ^ k) for i in range(size)]) for k in reversed(range(2, size, 2))
    ]
    blocks[1] = between(blocks[1])
    twin = [(i, i ^ 1) for i in range(size)]
    twins = [lax.ppermute(b, "space", twin) for b in blocks]
    return blocks + twins[:2], twins[2:]


def per_device(
    var_tokens, key_query, value_weight, qkv_weight, out_weight, up_weight, down_weight, norm_gain
):
    groups = lax.axis_size("var")
    spaces = lax.axis_size("space")
    n_vars, rows, width = var_tokens.shape
    part = rows // groups
    local = qkv_weight.shape[2]

    shape = pltpu.VMEM
    kept = (groups, n_vars, part)
    loaded = call(
        load_kernel,
        [
            shape((*kept, width), bf16),
            shape(value_weight.shape, bf16),
            shape((*kept, LANES), bf16),
            shape((groups, part, LANES), bf16),
        ],
        var_tokens.reshape(n_vars, groups, part, width), key_query.T, value_weight,
        flops=2 * n_vars * rows * width * LANES, hbm=3, any_outs=(0, 1),
        scratch=[
            pltpu.VMEM((*kept, width), bf16),
            pltpu.VMEM((H, width), bf16),
            pltpu.SemaphoreType.DMA((3 + groups,)),
        ],
    )
    sent = []
    for slot in reversed(range(groups)):
        sent += call(
            functools.partial(pool_kernel, slot), [shape((part, width + LANES), bf16)],
            *loaded, *sent[-1:],
            flops=2 * n_vars * part * width * width,
        )
    got = exchange(sent[::-1], "var", groups)
    normed, pooled = call(
        norm_kernel, [shape((part, width), bf16)] * 2, norm_gain.reshape(1, width), *got
    )
    blocks = exchange([normed] * groups, "var", groups)
    q, kv = call(
        qkv_kernel,
        [shape((rows, local), bf16), shape((rows, 2 * local), bf16)],
        qkv_weight.transpose(1, 0, 2), *blocks,
        flops=6 * rows * width * local,
    )
    ffn = []

    def feed_forward(arrived):
        made = call(
            ffn_kernel, [shape((rows, width), f32), shape(arrived.shape, bf16)],
            up_weight, down_weight, *blocks, arrived,
            flops=4 * rows * width * up_weight.shape[1], aliases={2 + len(blocks): 1},
        )
        ffn.append(made[0])
        return made[1]

    early, late = gather_space(kv, spaces, feed_forward)
    heads = H // groups
    state = call(
        functools.partial(early_kernel, heads), [shape((rows, local), f32)] * 3, q, *early,
        flops=4 * rows * rows * len(early) * local * heads, vmem=32,
    )
    sums = call(
        functools.partial(attend_kernel, heads, groups),
        [shape((part, width), bf16)] * groups,
        q, *ffn, out_weight, *state, *late,
        flops=4 * rows * rows * len(late) * local * heads, vmem=32,
    )
    (out,) = call(add_kernel, [jax.ShapeDtypeStruct((part, width), bf16)], pooled, *exchange(sums[::-1], "var", groups))
    return out


def solution(mesh):
    placed = (
        P("var", "space", None),
        P(),
        P(),
        P(None, None, "var"),
        P("var", None),
        P(None, "var"),
        P("var", None),
        P(),
    )
    return jax.shard_map(
        per_device, mesh=mesh, in_specs=placed, out_specs=P(("space", "var"), None), check_vma=False
    )
```

time: 46.9 us -> 44.4 us (0.947)
  waiting for transfers between devices: 18.9 us -> 17.5 us
  Pallas kernels: 9.41 us -> 8.3 us
    ppermute x7, waiting for transfers between devices: 5.84 us -> 3.68 us  [the longest x3 3.46 us: gather_space(): lax.ppermute(block, 'space', [(i, i ^ k) for i in range(size)])]
    pallas_call x7 -> x11, Pallas kernels: 9.41 us -> 8.3 us  [call(): pl.pallas_call(kernel, out_shape=out_shapes, in_specs=in_specs, out_specs...]
    ppermute x9, waiting for transfers between devices: 13 us -> 13.8 us  [exchange(): lax.ppermute(parts[k], axis, [(i, i ^ k) for i in range(size)])]
  transfers between devices with their start and end apart: 16 -> 16, of which waited for: 11 -> 10; matrix products, arithmetic and copies ran while one was open for 0% -> 0% of each run, Pallas kernels for 7% -> 6%
where the time goes in v3:
time: 44.4 us; the launch traced here: 44.2 us
  starting transfers between devices  18.2 us (41%)
  waiting for transfers between devices  17.5 us (39%)
  Pallas kernels  8.3 us (19%)
    ppermute x9, starting transfers between devices, exchange(): lax.ppermute(parts[k], axis, [(i, i ^ k) for i in range(size)])  14.6 us
    ppermute x9, waiting for transfers between devices, exchange(): lax.ppermute(parts[k], axis, [(i, i ^ k) for i in range(size)])  13.8 us
    pallas_call x11, Pallas kernels, call(): pl.pallas_call(kernel, out_shape=out_shapes, in_specs=in_specs, out_specs...  8.3 us
    ppermute x3, starting transfers between devices, gather_space(): lax.ppermute(block, 'space', [(i, i ^ k) for i in range(size)])  3.55 us
    ppermute x3, waiting for transfers between devices, gather_space(): lax.ppermute(block, 'space', [(i, i ^ k) for i in range(size)])  3.46 us
  transfers between devices with their start and end apart: 16, of which 10 were waited for; matrix products, arithmetic and copies ran while one was open for 0% of the time, Pallas kernels for 6%

profile of v3, /device:TPU:0, one launch (start us, length us, event | category | flops | bytes accessed | tf_op | source)
XLA Modules:
  0.0 44.2 jit_solution(14389026790072922513)
XLA Ops:
  0.0 2.0 %shard_map.82 = (bf16[4,4,32,1024]{3,2,1,0:T(8,128)(2,1)S(1)}, bf16[1024,1024]{1,0:T(8,128)(2,1)S(1)}, bf16[4,4,32,128]{3,2,1,0:T(8,128)(2,1)S(1)}, bf16[4,32,128]{2,1,0:T(8,128)(2,1)S(1)}) custom-call(bf16[4,4,32,1024]{3,2,1,0:T(8,128)(2,1)} %bitcast.4, bf16[16,1024]{1,0:T(8,128)(2,1)} %bitcast.5, bf16[1024,1024]{1,0:T(8,128)(2,1)} %wv_hbm.1), custom_call_target="tpu_custom_call" | custom-call | flops 134217728 | bytes 6488064 | tf_op jit(solution)/shard_map/pallas_call | solution.py:180
  2.0 0.5 %shard_map.83.refs_0_ = bf16[32,1152]{1,0:T(8,128)(2,1)S(1)} custom-call(bf16[4,4,32,1024]{3,2,1,0:T(8,128)(2,1)S(1)} %get-tuple-element.22.x_ref, bf16[1024,1024]{1,0:T(8,128)(2,1)S(1)} %get-tuple-element.23.wv_ref, bf16[4,4,32,128]{3,2,1,0:T(8,128)(2,1)S(1)} %get-tuple-element.24.share_ref, bf16[4,32,128]{2,1,0:T(8,128)(2,1)S(1)} %get-tuple-element.25.stats_ref), custom_call_target="tpu_custom_call" | custom-call | flops 268435456 | bytes 3383296 | tf_op jit(solution)/shard_map/pallas_call | solution.py:180
  2.5 0.5 %shard_map.84.refs_0_ = bf16[32,1152]{1,0:T(8,128)(2,1)S(1)} custom-call(bf16[4,4,32,1024]{3,2,1,0:T(8,128)(2,1)S(1)} %get-tuple-element.22.x_ref, bf16[1024,1024]{1,0:T(8,128)(2,1)S(1)} %get-tuple-element.23.wv_ref, bf16[4,4,32,128]{3,2,1,0:T(8,128)(2,1)S(1)} %get-tuple-element.24.share_ref, bf16[4,32,128]{2,1,0:T(8,128)(2,1)S(1)} %get-tuple-element.25.stats_ref, ...), custom_call_target="tpu_custom_call" | custom-call | flops 268435456 | bytes 3457024 | tf_op jit(solution)/shard_map/pallas_call | solution.py:180
  3.0 0.0 copy-start.4
  3.0 0.0 copy-start.2
  3.0 0.5 %shard_map.85.refs_0_ = bf16[32,1152]{1,0:T(8,128)(2,1)S(1)} custom-call(bf16[4,4,32,1024]{3,2,1,0:T(8,128)(2,1)S(1)} %get-tuple-element.22.x_ref, bf16[1024,1024]{1,0:T(8,128)(2,1)S(1)} %get-tuple-element.23.wv_ref, bf16[4,4,32,128]{3,2,1,0:T(8,128)(2,1)S(1)} %get-tuple-element.24.share_ref, bf16[4,32,128]{2,1,0:T(8,128)(2,1)S(1)} %get-tuple-element.25.stats_ref, ...), custom_call_target="tpu_custom_call" | custom-call | flops 268435456 | bytes 3457024 | tf_op jit(solution)/shard_map/pallas_call | solution.py:180
  3.5 3.1 %collective-permute-start.2 = (bf16[32,1152]{1,0:T(8,128)(2,1)S(1)}, bf16[32,1152]{1,0:T(8,128)(2,1)S(1)}, u32[]{:S(2)}, u32[]{:S(2)}) collective-permute-start(bf16[32,1152]{1,0:T(8,128)(2,1)S(1)} %shard_map.85.refs_0_), channel_id=1, source_target_pairs={{0,1},{1,0},{2,3},{3,2},{4,5},{5,4},{6,7},{7,6},{8,9},{9,8},{10,11... | collective-permute-start | bytes 221192 | tf_op jit(solution)/shard_map/ppermute | solution.py:194
  6.6 2.6 %collective-permute-start.1 = (bf16[32,1152]{1,0:T(8,128)(2,1)S(1)}, bf16[32,1152]{1,0:T(8,128)(2,1)S(1)}, u32[]{:S(2)}, u32[]{:S(2)}) collective-permute-start(bf16[32,1152]{1,0:T(8,128)(2,1)S(1)} %shard_map.84.refs_0_), channel_id=1, source_target_pairs={{0,2},{1,3},{2,0},{3,1},{4,6},{5,7},{6,4},{7,5},{8,10},{9,11},{10,... | collective-permute-start | bytes 221192 | tf_op jit(solution)/shard_map/ppermute | solution.py:194
  9.2 0.0 collective-permute-start
  9.2 0.0 copy-done.4
  9.2 0.0 copy-start
  9.2 0.0 copy-start.1
  9.2 0.5 %shard_map.86.refs_3_ = bf16[32,1152]{1,0:T(8,128)(2,1)S(1)} custom-call(bf16[4,4,32,1024]{3,2,1,0:T(8,128)(2,1)S(1)} %get-tuple-element.22.x_ref, bf16[1024,1024]{1,0:T(8,128)(2,1)S(1)} %get-tuple-element.23.wv_ref, bf16[4,4,32,128]{3,2,1,0:T(8,128)(2,1)S(1)} %get-tuple-element.24.share_ref, bf16[4,32,128]{2,1,0:T(8,128)(2,1)S(1)} %get-tuple-element.25.stats_ref, ...), custom_call_target="tpu_custom_call" | custom-call | flops 268435456 | bytes 3457024 | tf_op jit(solution)/shard_map/pallas_call | solution.py:180
  9.7 0.0 collective-permute-done.2.refs_2_
  9.7 4.7 %collective-permute-done.1.refs_1_ = bf16[32,1152]{1,0:T(8,128)(2,1)S(1)} collective-permute-done((bf16[32,1152]{1,0:T(8,128)(2,1)S(1)}, bf16[32,1152]{1,0:T(8,128)(2,1)S(1)}, u32[]{:S(2)}, u32[]{:S(2)}) %collective-permute-start.1) | collective-permute-done | bytes 73760 | tf_op jit(solution)/shard_map/ppermute | solution.py:194
  14.5 1.0 %collective-permute-done.refs_0_ = bf16[32,1152]{1,0:T(8,128)(2,1)S(1)} collective-permute-done((bf16[32,1152]{1,0:T(8,128)(2,1)S(1)}, bf16[32,1152]{1,0:T(8,128)(2,1)S(1)}, u32[]{:S(2)}, u32[]{:S(2)}) %collective-permute-start) | collective-permute-done | bytes 73760 | tf_op jit(solution)/shard_map/ppermute | solution.py:194
  15.5 0.6 %shard_map.87 = (bf16[32,1024]{1,0:T(8,128)(2,1)S(1)}, bf16[32,1024]{1,0:T(8,128)(2,1)S(1)}) custom-call(bf16[1,1024]{1,0:T(2,128)(2,1)S(1)} %reshape.6.gain_ref, bf16[32,1152]{1,0:T(8,128)(2,1)S(1)} %collective-permute-done.refs_0_, bf16[32,1152]{1,0:T(8,128)(2,1)S(1)} %collective-permute-done.1.refs_1_, ...), custom_call_target="tpu_custom_call" | custom-call | bytes 428032 | tf_op jit(solution)/shard_map/pallas_call | solution.py:180
  16.0 2.3 %collective-permute-start.3 = (bf16[32,1024]{1,0:T(8,128)(2,1)S(1)}, bf16[32,1024]{1,0:T(8,128)(2,1)S(1)}, u32[]{:S(2)}, u32[]{:S(2)}) collective-permute-start(bf16[32,1024]{1,0:T(8,128)(2,1)S(1)} %get-tuple-element.27.refs_3_), channel_id=1, source_target_pairs={{0,3},{1,2},{2,1},{3,0},{4,7},{5,6},{6,5},{7,4},{8,11},{9,10},{10,... | collective-permute-start | bytes 196616 | tf_op jit(solution)/shard_map/ppermute | solution.py:194
  18.3 0.4 collective-permute-start.4
  18.7 1.8 %collective-permute-start.5 = (bf16[32,1024]{1,0:T(8,128)(2,1)S(1)}, bf16[32,1024]{1,0:T(8,128)(2,1)S(1)}, u32[]{:S(2)}, u32[]{:S(2)}) collective-permute-start(bf16[32,1024]{1,0:T(8,128)(2,1)S(1)} %get-tuple-element.27.refs_3_), channel_id=1, source_target_pairs={{0,1},{1,0},{2,3},{3,2},{4,5},{5,4},{6,7},{7,6},{8,9},{9,8},{10,11... | collective-permute-start | bytes 196616 | tf_op jit(solution)/shard_map/ppermute | solution.py:194
  20.5 1.7 %collective-permute-done.3.refs_0_ = bf16[32,1024]{1,0:T(8,128)(2,1)S(1)} collective-permute-done((bf16[32,1024]{1,0:T(8,128)(2,1)S(1)}, bf16[32,1024]{1,0:T(8,128)(2,1)S(1)}, u32[]{:S(2)}, u32[]{:S(2)}) %collective-permute-start.3) | collective-permute-done | bytes 65568 | tf_op jit(solution)/shard_map/ppermute | solution.py:194
  22.2 1.9 %collective-permute-done.4.refs_1_ = bf16[32,1024]{1,0:T(8,128)(2,1)S(1)} collective-permute-done((bf16[32,1024]{1,0:T(8,128)(2,1)S(1)}, bf16[32,1024]{1,0:T(8,128)(2,1)S(1)}, u32[]{:S(2)}, u32[]{:S(2)}) %collective-permute-start.4) | collective-permute-done | bytes 65568 | tf_op jit(solution)/shard_map/ppermute | solution.py:194
  24.1 0.0 collective-permute-done.5.refs_2_
  24.1 0.0 copy-done.2
  24.1 0.4 shard_map.88
  24.5 0.0 copy-start.3
  24.5 2.5 %collective-permute-start.6 = (bf16[128,512]{1,0:T(8,128)(2,1)S(1)}, bf16[128,512]{1,0:T(8,128)(2,1)S(1)}, u32[]{:S(2)}, u32[]{:S(2)}) collective-permute-start(bf16[128,512]{1,0:T(8,128)(2,1)S(1)} %get-tuple-element.29.refs_0_), channel_id=1, source_target_pairs={{0,24},{4,28},{8,16},{12,20},{16,8},{20,12},{24,0},{28,4},{1,25},{... | collective-permute-start | bytes 393224 | tf_op jit(solution)/shard_map/ppermute | solution.py:206
  27.0 0.5 %collective-permute-start.7 = (bf16[128,512]{1,0:T(8,128)(2,1)S(1)}, bf16[128,512]{1,0:T(8,128)(2,1)S(1)}, u32[]{:S(2)}, u32[]{:S(2)}) collective-permute-start(bf16[128,512]{1,0:T(8,128)(2,1)S(1)} %get-tuple-element.29.refs_0_), channel_id=1, source_target_pairs={{0,16},{4,20},{8,24},{12,28},{16,0},{20,4},{24,8},{28,12},{1,17},{... | collective-permute-start | bytes 393224 | tf_op jit(solution)/shard_map/ppermute | solution.py:206
  27.5 0.6 %collective-permute-start.8 = (bf16[128,512]{1,0:T(8,128)(2,1)S(1)}, bf16[128,512]{1,0:T(8,128)(2,1)S(1)}, u32[]{:S(2)}, u32[]{:S(2)}) collective-permute-start(bf16[128,512]{1,0:T(8,128)(2,1)S(1)} %get-tuple-element.29.refs_0_), channel_id=1, source_target_pairs={{0,8},{4,12},{8,0},{12,4},{16,24},{20,28},{24,16},{28,20},{1,9},{5... | collective-permute-start | bytes 393224 | tf_op jit(solution)/shard_map/ppermute | solution.py:206
  28.0 0.0 collective-permute-start.9
  28.0 2.4 %collective-permute-done.6.refs_4_ = bf16[128,512]{1,0:T(8,128)(2,1)S(1)} collective-permute-done((bf16[128,512]{1,0:T(8,128)(2,1)S(1)}, bf16[128,512]{1,0:T(8,128)(2,1)S(1)}, u32[]{:S(2)}, u32[]{:S(2)}) %collective-permute-start.6) | collective-permute-done | bytes 131104 | tf_op jit(solution)/shard_map/ppermute | solution.py:206
  30.4 0.0 copy-done
  30.4 0.0 copy-done.1
  30.4 0.8 %shard_map.89 = (f32[128,1024]{1,0:T(8,128)S(1)}, bf16[128,512]{1,0:T(8,128)(2,1)S(1)}) custom-call(bf16[1024,1024]{1,0:T(8,128)(2,1)S(1)} %copy-done, bf16[1024,1024]{1,0:T(8,128)(2,1)S(1)} %copy-done.1, bf16[32,1024]{1,0:T(8,128)(2,1)S(1)} %collective-permute-done.3.refs_0_, ...), custom_call_target="tpu_custom_call", output_to_operand_aliasing={{1}: (6, {})} | custom-call | flops 536870912 | bytes 5242880 | tf_op jit(solution)/shard_map/pallas_call | solution.py:180
  31.3 0.1 collective-permute-start.10
  31.3 0.6 %collective-permute-done.7.refs_2_ = bf16[128,512]{1,0:T(8,128)(2,1)S(1)} collective-permute-done((bf16[128,512]{1,0:T(8,128)(2,1)S(1)}, bf16[128,512]{1,0:T(8,128)(2,1)S(1)}, u32[]{:S(2)}, u32[]{:S(2)}) %collective-permute-start.7) | collective-permute-done | bytes 131104 | tf_op jit(solution)/shard_map/ppermute | solution.py:206
  31.9 0.0 collective-permute-start.11
  31.9 0.5 %collective-permute-done.8.refs_3_ = bf16[128,512]{1,0:T(8,128)(2,1)S(1)} collective-permute-done((bf16[128,512]{1,0:T(8,128)(2,1)S(1)}, bf16[128,512]{1,0:T(8,128)(2,1)S(1)}, u32[]{:S(2)}, u32[]{:S(2)}) %collective-permute-start.8) | collective-permute-done | bytes 131104 | tf_op jit(solution)/shard_map/ppermute | solution.py:206
  32.4 0.0 collective-permute-start.12
  32.5 0.0 collective-permute-done.9.refs_4_
  32.5 0.2 collective-permute-done.10.refs_5_
  32.7 1.2 %shard_map.90 = (f32[128,256]{1,0:T(8,128)S(1)}, f32[128,256]{1,0:T(8,128)S(1)}, f32[128,256]{1,0:T(8,128)S(1)}) custom-call(bf16[128,256]{1,0:T(8,128)(2,1)S(1)} %get-tuple-element.28.q_ref, bf16[128,512]{1,0:T(8,128)(2,1)S(1)} %get-tuple-element.29.refs_0_, bf16[128,512]{1,0:T(8,128)(2,1)S(1)} %get-tuple-element.31.refs_1_, ...), custom_call_target="tpu_custom_call" | custom-call | flops 402653184 | bytes 1245184 | tf_op jit(solution)/shard_map/pallas_call | solution.py:180
  33.8 0.0 collective-permute-done.11.refs_0_
  33.9 0.0 collective-permute-done.12.refs_1_
  33.9 0.0 copy-done.3
  33.9 0.7 %shard_map.91 = (bf16[32,1024]{1,0:T(8,128)(2,1)S(1)}, bf16[32,1024]{1,0:T(8,128)(2,1)S(1)}, bf16[32,1024]{1,0:T(8,128)(2,1)S(1)}, bf16[32,1024]{1,0:T(8,128)(2,1)S(1)}) custom-call(bf16[128,256]{1,0:T(8,128)(2,1)S(1)} %get-tuple-element.28.q_ref, f32[128,1024]{1,0:T(8,128)S(1)} %get-tuple-element.30.ffn_ref, bf16[256,1024]{1,0:T(8,128)(2,1)S(1)} %copy-done.3, ...), custom_call_target="tpu_custom_call" | custom-call | flops 134217728 | bytes 2031616 | tf_op jit(solution)/shard_map/pallas_call | solution.py:180
  34.6 2.0 %collective-permute-start.13 = (bf16[32,1024]{1,0:T(8,128)(2,1)S(1)}, bf16[32,1024]{1,0:T(8,128)(2,1)S(1)}, u32[]{:S(2)}, u32[]{:S(2)}) collective-permute-start(bf16[32,1024]{1,0:T(8,128)(2,1)S(1)} %get-tuple-element.35), channel_id=1, source_target_pairs={{0,3},{1,2},{2,1},{3,0},{4,7},{5,6},{6,5},{7,4},{8,11},{9,10},{10,... | collective-permute-start | bytes 196616 | tf_op jit(solution)/shard_map/ppermute | solution.py:194
  36.7 0.1 collective-permute-start.14
  36.8 2.3 %collective-permute-start.15 = (bf16[32,1024]{1,0:T(8,128)(2,1)S(1)}, bf16[32,1024]{1,0:T(8,128)(2,1)S(1)}, u32[]{:S(2)}, u32[]{:S(2)}) collective-permute-start(bf16[32,1024]{1,0:T(8,128)(2,1)S(1)} %get-tuple-element.37), channel_id=1, source_target_pairs={{0,1},{1,0},{2,3},{3,2},{4,5},{5,4},{6,7},{7,6},{8,9},{9,8},{10,11... | collective-permute-start | bytes 196616 | tf_op jit(solution)/shard_map/ppermute | solution.py:194
  39.1 2.4 %collective-permute-done.13.refs_1_ = bf16[32,1024]{1,0:T(8,128)(2,1)S(1)} collective-permute-done((bf16[32,1024]{1,0:T(8,128)(2,1)S(1)}, bf16[32,1024]{1,0:T(8,128)(2,1)S(1)}, u32[]{:S(2)}, u32[]{:S(2)}) %collective-permute-start.13) | collective-permute-done | bytes 65568 | tf_op jit(solution)/shard_map/ppermute | solution.py:194
  41.5 2.1 %collective-permute-done.14.refs_2_ = bf16[32,1024]{1,0:T(8,128)(2,1)S(1)} collective-permute-done((bf16[32,1024]{1,0:T(8,128)(2,1)S(1)}, bf16[32,1024]{1,0:T(8,128)(2,1)S(1)}, u32[]{:S(2)}, u32[]{:S(2)}) %collective-permute-start.14) | collective-permute-done | bytes 65568 | tf_op jit(solution)/shard_map/ppermute | solution.py:194
  43.6 0.0 collective-permute-done.15.refs_3_
  43.6 0.7 %shard_map.92 = bf16[32,1024]{1,0:T(8,128)(2,1)} custom-call(bf16[32,1024]{1,0:T(8,128)(2,1)S(1)} %get-tuple-element.26.refs_0_, bf16[32,1024]{1,0:T(8,128)(2,1)S(1)} %collective-permute-done.13.refs_1_, bf16[32,1024]{1,0:T(8,128)(2,1)S(1)} %collective-permute-done.14.refs_2_, bf16[32,1024]{1,0:T(8,128)(2,1)S(1)} %collective-permute-done.15.refs_3_, ...), custom_call_target="tpu_custom_call" | custom-call | bytes 393216 | tf_op jit(solution)/shard_map/pallas_call | solution.py:180
  (1 shorter events, 0.0 us)
Async XLA Ops:
  3.0 6.2 %copy-start.4 = (bf16[1024]{0:T(1024)(128)(2,1)S(1)}, bf16[1024]{0:T(1024)(128)(2,1)}, u32[]{:S(2)}) copy-start(bf16[1024]{0:T(1024)(128)(2,1)} %param.15) | copy-start | bytes 6148
  3.0 21.1 %copy-start.2 = (bf16[1024,3,256]{2,0,1:T(8,128)(2,1)S(1)}, bf16[1024,3,256]{2,0,1:T(8,128)(2,1)}, u32[]{:S(2)}) copy-start(bf16[1024,3,256]{2,0,1:T(8,128)(2,1)} %param.11) | copy-start | bytes 4718596
  3.5 6.2 %collective-permute-start.2 = (bf16[32,1152]{1,0:T(8,128)(2,1)S(1)}, bf16[32,1152]{1,0:T(8,128)(2,1)S(1)}, u32[]{:S(2)}, u32[]{:S(2)}) collective-permute-start(bf16[32,1152]{1,0:T(8,128)(2,1)S(1)} %shard_map.85.refs_0_), channel_id=1, source_target_pairs={{0,1},{1,0},{2,3},{3,2},{4,5},{5,4},{6,7},{7,6},{8,9},{9,8},{10,11... | collective-permute-start | bytes 221192 | tf_op jit(solution)/shard_map/ppermute | solution.py:194
  6.6 7.8 %collective-permute-start.1 = (bf16[32,1152]{1,0:T(8,128)(2,1)S(1)}, bf16[32,1152]{1,0:T(8,128)(2,1)S(1)}, u32[]{:S(2)}, u32[]{:S(2)}) collective-permute-start(bf16[32,1152]{1,0:T(8,128)(2,1)S(1)} %shard_map.84.refs_0_), channel_id=1, source_target_pairs={{0,2},{1,3},{2,0},{3,1},{4,6},{5,7},{6,4},{7,5},{8,10},{9,11},{10,... | collective-permute-start | bytes 221192 | tf_op jit(solution)/shard_map/ppermute | solution.py:194
  9.2 6.3 %collective-permute-start = (bf16[32,1152]{1,0:T(8,128)(2,1)S(1)}, bf16[32,1152]{1,0:T(8,128)(2,1)S(1)}, u32[]{:S(2)}, u32[]{:S(2)}) collective-permute-start(bf16[32,1152]{1,0:T(8,128)(2,1)S(1)} %shard_map.83.refs_0_), channel_id=1, source_target_pairs={{0,3},{1,2},{2,1},{3,0},{4,7},{5,6},{6,5},{7,4},{8,11},{9,10},{10,... | collective-permute-start | bytes 221192 | tf_op jit(solution)/shard_map/ppermute | solution.py:194
  9.2 21.2 %copy-start = (bf16[1024,1024]{1,0:T(8,128)(2,1)S(1)}, bf16[1024,1024]{1,0:T(8,128)(2,1)}, u32[]{:S(2)}) copy-start(bf16[1024,1024]{1,0:T(8,128)(2,1)} %up_ref.1) | copy-start | bytes 6291460
  9.2 21.2 %copy-start.1 = (bf16[1024,1024]{1,0:T(8,128)(2,1)S(1)}, bf16[1024,1024]{1,0:T(8,128)(2,1)}, u32[]{:S(2)}) copy-start(bf16[1024,1024]{1,0:T(8,128)(2,1)} %down_ref.1) | copy-start | bytes 6291460
  16.0 6.2 %collective-permute-start.3 = (bf16[32,1024]{1,0:T(8,128)(2,1)S(1)}, bf16[32,1024]{1,0:T(8,128)(2,1)S(1)}, u32[]{:S(2)}, u32[]{:S(2)}) collective-permute-start(bf16[32,1024]{1,0:T(8,128)(2,1)S(1)} %get-tuple-element.27.refs_3_), channel_id=1, source_target_pairs={{0,3},{1,2},{2,1},{3,0},{4,7},{5,6},{6,5},{7,4},{8,11},{9,10},{10,... | collective-permute-start | bytes 196616 | tf_op jit(solution)/shard_map/ppermute | solution.py:194
  18.3 5.8 %collective-permute-start.4 = (bf16[32,1024]{1,0:T(8,128)(2,1)S(1)}, bf16[32,1024]{1,0:T(8,128)(2,1)S(1)}, u32[]{:S(2)}, u32[]{:S(2)}) collective-permute-start(bf16[32,1024]{1,0:T(8,128)(2,1)S(1)} %get-tuple-element.27.refs_3_), channel_id=1, source_target_pairs={{0,2},{1,3},{2,0},{3,1},{4,6},{5,7},{6,4},{7,5},{8,10},{9,11},{10,... | collective-permute-start | bytes 196616 | tf_op jit(solution)/shard_map/ppermute | solution.py:194
  18.7 5.4 %collective-permute-start.5 = (bf16[32,1024]{1,0:T(8,128)(2,1)S(1)}, bf16[32,1024]{1,0:T(8,128)(2,1)S(1)}, u32[]{:S(2)}, u32[]{:S(2)}) collective-permute-start(bf16[32,1024]{1,0:T(8,128)(2,1)S(1)} %get-tuple-element.27.refs_3_), channel_id=1, source_target_pairs={{0,1},{1,0},{2,3},{3,2},{4,5},{5,4},{6,7},{7,6},{8,9},{9,8},{10,11... | collective-permute-start | bytes 196616 | tf_op jit(solution)/shard_map/ppermute | solution.py:194
  24.5 9.4 %copy-start.3 = (bf16[256,1024]{1,0:T(8,128)(2,1)S(1)}, bf16[256,1024]{1,0:T(8,128)(2,1)}, u32[]{:S(2)}) copy-start(bf16[256,1024]{1,0:T(8,128)(2,1)} %wo_ref.1) | copy-start | bytes 1572868
  24.5 5.9 %collective-permute-start.6 = (bf16[128,512]{1,0:T(8,128)(2,1)S(1)}, bf16[128,512]{1,0:T(8,128)(2,1)S(1)}, u32[]{:S(2)}, u32[]{:S(2)}) collective-permute-start(bf16[128,512]{1,0:T(8,128)(2,1)S(1)} %get-tuple-element.29.refs_0_), channel_id=1, source_target_pairs={{0,24},{4,28},{8,16},{12,20},{16,8},{20,12},{24,0},{28,4},{1,25},{... | collective-permute-start | bytes 393224 | tf_op jit(solution)/shard_map/ppermute | solution.py:206
  27.0 5.0 %collective-permute-start.7 = (bf16[128,512]{1,0:T(8,128)(2,1)S(1)}, bf16[128,512]{1,0:T(8,128)(2,1)S(1)}, u32[]{:S(2)}, u32[]{:S(2)}) collective-permute-start(bf16[128,512]{1,0:T(8,128)(2,1)S(1)} %get-tuple-element.29.refs_0_), channel_id=1, source_target_pairs={{0,16},{4,20},{8,24},{12,28},{16,0},{20,4},{24,8},{28,12},{1,17},{... | collective-permute-start | bytes 393224 | tf_op jit(solution)/shard_map/ppermute | solution.py:206
  27.5 5.0 %collective-permute-start.8 = (bf16[128,512]{1,0:T(8,128)(2,1)S(1)}, bf16[128,512]{1,0:T(8,128)(2,1)S(1)}, u32[]{:S(2)}, u32[]{:S(2)}) collective-permute-start(bf16[128,512]{1,0:T(8,128)(2,1)S(1)} %get-tuple-element.29.refs_0_), channel_id=1, source_target_pairs={{0,8},{4,12},{8,0},{12,4},{16,24},{20,28},{24,16},{28,20},{1,9},{5... | collective-permute-start | bytes 393224 | tf_op jit(solution)/shard_map/ppermute | solution.py:206
  28.0 4.4 %collective-permute-start.9 = (bf16[128,512]{1,0:T(8,128)(2,1)S(1)}, bf16[128,512]{1,0:T(8,128)(2,1)S(1)}, u32[]{:S(2)}, u32[]{:S(2)}) collective-permute-start(bf16[128,512]{1,0:T(8,128)(2,1)S(1)} %get-tuple-element.29.refs_0_), channel_id=1, source_target_pairs={{0,4},{4,0},{8,12},{12,8},{16,20},{20,16},{24,28},{28,24},{1,5},{5... | collective-permute-start | bytes 393224 | tf_op jit(solution)/shard_map/ppermute | solution.py:210
  31.3 1.4 %collective-permute-start.10 = (bf16[128,512]{1,0:T(8,128)(2,1)S(1)}, bf16[128,512]{1,0:T(8,128)(2,1)S(1)}, u32[]{:S(2)}, u32[]{:S(2)}) collective-permute-start(bf16[128,512]{1,0:T(8,128)(2,1)S(1)} %get-tuple-element.31.refs_1_), channel_id=1, source_target_pairs={{0,4},{4,0},{8,12},{12,8},{16,20},{20,16},{24,28},{28,24},{1,5},{5... | collective-permute-start | bytes 393224 | tf_op jit(solution)/shard_map/ppermute | solution.py:210
  31.9 1.9 %collective-permute-start.11 = (bf16[128,512]{1,0:T(8,128)(2,1)S(1)}, bf16[128,512]{1,0:T(8,128)(2,1)S(1)}, u32[]{:S(2)}, u32[]{:S(2)}) collective-permute-start(bf16[128,512]{1,0:T(8,128)(2,1)S(1)} %collective-permute-done.7.refs_2_), channel_id=1, source_target_pairs={{0,4},{4,0},{8,12},{12,8},{16,20},{20,16},{24,28},{28,24},{1,5},{5... | collective-permute-start | bytes 393224 | tf_op jit(solution)/shard_map/ppermute | solution.py:210
  32.4 1.4 %collective-permute-start.12 = (bf16[128,512]{1,0:T(8,128)(2,1)S(1)}, bf16[128,512]{1,0:T(8,128)(2,1)S(1)}, u32[]{:S(2)}, u32[]{:S(2)}) collective-permute-start(bf16[128,512]{1,0:T(8,128)(2,1)S(1)} %collective-permute-done.8.refs_3_), channel_id=1, source_target_pairs={{0,4},{4,0},{8,12},{12,8},{16,20},{20,16},{24,28},{28,24},{1,5},{5... | collective-permute-start | bytes 393224 | tf_op jit(solution)/shard_map/ppermute | solution.py:210
  34.6 6.9 %collective-permute-start.13 = (bf16[32,1024]{1,0:T(8,128)(2,1)S(1)}, bf16[32,1024]{1,0:T(8,128)(2,1)S(1)}, u32[]{:S(2)}, u32[]{:S(2)}) collective-permute-start(bf16[32,1024]{1,0:T(8,128)(2,1)S(1)} %get-tuple-element.35), channel_id=1, source_target_pairs={{0,3},{1,2},{2,1},{3,0},{4,7},{5,6},{6,5},{7,4},{8,11},{9,10},{10,... | collective-permute-start | bytes 196616 | tf_op jit(solution)/shard_map/ppermute | solution.py:194
  36.7 6.9 %collective-permute-start.14 = (bf16[32,1024]{1,0:T(8,128)(2,1)S(1)}, bf16[32,1024]{1,0:T(8,128)(2,1)S(1)}, u32[]{:S(2)}, u32[]{:S(2)}) collective-permute-start(bf16[32,1024]{1,0:T(8,128)(2,1)S(1)} %get-tuple-element.36), channel_id=1, source_target_pairs={{0,2},{1,3},{2,0},{3,1},{4,6},{5,7},{6,4},{7,5},{8,10},{9,11},{10,... | collective-permute-start | bytes 196616 | tf_op jit(solution)/shard_map/ppermute | solution.py:194
  36.8 6.8 %collective-permute-start.15 = (bf16[32,1024]{1,0:T(8,128)(2,1)S(1)}, bf16[32,1024]{1,0:T(8,128)(2,1)S(1)}, u32[]{:S(2)}, u32[]{:S(2)}) collective-permute-start(bf16[32,1024]{1,0:T(8,128)(2,1)S(1)} %get-tuple-element.37), channel_id=1, source_target_pairs={{0,1},{1,0},{2,3},{3,2},{4,5},{5,4},{6,7},{7,6},{8,9},{9,8},{10,11... | collective-permute-start | bytes 196616 | tf_op jit(solution)/shard_map/ppermute | solution.py:194

commit v4 on v3

--- a/solution.py
+++ b/solution.py
@@ -69,8 +69,7 @@
     weights.wait()
 
 
-def pool_kernel(slot, x_ref, wv_ref, share_ref, stats_ref, *refs):
-    out_ref = refs[-1]
+def pool_kernel(slot, x_ref, wv_ref, share_ref, stats_ref, out_ref):
     n_vars, rows, width = x_ref.shape[1:]
     share = below([share_ref[slot, v] for v in range(n_vars)])
     share = jnp.dot(share, head_spread(0, 1, width), preferred_element_type=f32)
@@ -102,12 +101,13 @@
 
 
 def qkv_kernel(w_ref, *refs):
-    blocks, (q_ref, kv_ref) = refs[:-2], refs[-2:]
+    blocks, (q_ref, kv_ref, kept_ref) = refs[:-3], refs[-3:]
     x = rows_of(blocks)
     width = q_ref.shape[1]
     q_ref[...] = jnp.dot(x, w_ref[0], preferred_element_type=f32).astype(bf16)
     kv_ref[:, :width] = jnp.dot(x, w_ref[1], preferred_element_type=f32).astype(bf16)
     kv_ref[:, width:] = jnp.dot(x, w_ref[2], preferred_element_type=f32).astype(bf16)
+    kept_ref[...] = kv_ref[...]
 
 
 def ffn_kernel(up_ref, down_ref, *refs):
@@ -189,25 +189,17 @@
     )(*args)
 
 
-def exchange(parts, axis, size):
-    got = [
-        lax.ppermute(parts[k], axis, [(i, i ^ k) for i in range(size)])
-        for k in reversed(range(1, size))
-    ]
-    return [*got, parts[0]]
-
-
-def gather_space(block, size, between):
+def exchange(parts, axis, size, partners):
+    return [lax.ppermute(parts[k], axis, [(i, i ^ k) for i in range(size)]) for k in partners]
+
+
+def gather_space(block, kept, size):
     if size > 8:
-        blocks = between(lax.all_gather(block, "space", axis=0, tiled=True))
+        blocks = lax.all_gather(block, "space", axis=0, tiled=True)
         half = blocks.shape[0] // 2
         return [blocks[:half]], [blocks[half:]]
-    blocks = [block] + [
-        lax.ppermute(block, "space", [(i, i ^ k) for i in range(size)]) for k in reversed(range(2, size, 2))
-    ]
-    blocks[1] = between(blocks[1])
-    twin = [(i, i ^ 1) for i in range(size)]
-    twins = [lax.ppermute(b, "space", twin) for b in blocks]
+    blocks = [kept, *exchange([block] * size, "space", size, range(size - 2, 0, -2))]
+    twins = [twin for b in blocks for twin in exchange([b, b], "space", size, (1,))]
     return blocks + twins[:2], twins[2:]
 
 
@@ -219,6 +211,9 @@
     n_vars, rows, width = var_tokens.shape
     part = rows // groups
     local = qkv_weight.shape[2]
+    partners = [range(groups - 1, 0, -1)] * 3
+    if groups == 4:
+        partners = (3, 2, 1), (1, 3, 2), (2, 1, 3)
 
     shape = pltpu.VMEM
     kept = (groups, n_vars, part)
@@ -242,17 +237,17 @@
     for slot in reversed(range(groups)):
         sent += call(
             functools.partial(pool_kernel, slot), [shape((part, width + LANES), bf16)],
-            *loaded, *sent[-1:],
+            *loaded,
             flops=2 * n_vars * part * width * width,
         )
-    got = exchange(sent[::-1], "var", groups)
+    got = exchange(sent[::-1], "var", groups, partners[0])
     normed, pooled = call(
-        norm_kernel, [shape((part, width), bf16)] * 2, norm_gain.reshape(1, width), *got
-    )
-    blocks = exchange([normed] * groups, "var", groups)
-    q, kv = call(
+        norm_kernel, [shape((part, width), bf16)] * 2, norm_gain.reshape(1, width), *got, sent[-1]
+    )
+    blocks = [*exchange([normed] * groups, "var", groups, partners[1]), normed]
+    q, kv, kept = call(
         qkv_kernel,
-        [shape((rows, local), bf16), shape((rows, 2 * local), bf16)],
+        [shape((rows, local), bf16)] + [shape((rows, 2 * local), bf16)] * 2,
         qkv_weight.transpose(1, 0, 2), *blocks,
         flops=6 * rows * width * local,
     )
@@ -267,7 +262,7 @@
         ffn.append(made[0])
         return made[1]
 
-    early, late = gather_space(kv, spaces, feed_forward)
+    early, late = gather_space(kv, feed_forward(kept), spaces)
     heads = H // groups
     state = call(
         functools.partial(early_kernel, heads), [shape((rows, local), f32)] * 3, q, *early,
@@ -279,7 +274,11 @@
         q, *ffn, out_weight, *state, *late,
         flops=4 * rows * rows * len(late) * local * heads, vmem=32,
     )
-    (out,) = call(add_kernel, [jax.ShapeDtypeStruct((part, width), bf16)], pooled, *exchange(sums[::-1], "var", groups))
+    by_partner = dict(zip([*partners[1], 0], sums))
+    got = exchange(by_partner, "var", groups, partners[2])
+    (out,) = call(
+        add_kernel, [jax.ShapeDtypeStruct((part, width), bf16)], pooled, *got, by_partner[0]
+    )
     return out
 
 

time: 44.4 us -> 43.4 us (0.977)
  starting transfers between devices: 18.2 us -> 17.4 us
    ppermute x7 -> x0, waiting for transfers between devices: 3.68 us -> none  [the longest x3 3.46 us: gather_space(): lax.ppermute(block, 'space', [(i, i ^ k) for i in range(size)])]
    ppermute x7 -> x0, starting transfers between devices: 3.66 us -> none  [the longest x3 3.55 us: gather_space(): lax.ppermute(block, 'space', [(i, i ^ k) for i in range(size)])]
    ppermute x9 -> x16, waiting for transfers between devices: 13.8 us -> 17.3 us  [exchange(): lax.ppermute(parts[k], axis, [(i, i ^ k) for i in range(size)])]
    ppermute x9 -> x16, starting transfers between devices: 14.6 us -> 17.4 us  [exchange(): lax.ppermute(parts[k], axis, [(i, i ^ k) for i in range(size)])]
  transfers between devices with their start and end apart: 16 -> 16, of which waited for: 10 -> 12; matrix products, arithmetic and copies ran while one was open for 0% -> 0% of each run, Pallas kernels for 6% -> 8%
where the time goes in v4:
time: 43.4 us; the launch traced here: 43.3 us
  starting transfers between devices  17.4 us (40%)
  waiting for transfers between devices  17.3 us (40%)
  Pallas kernels  8.31 us (19%)
    ppermute x16, starting transfers between devices, exchange(): lax.ppermute(parts[k], axis, [(i, i ^ k) for i in range(size)])  17.4 us
    ppermute x16, waiting for transfers between devices, exchange(): lax.ppermute(parts[k], axis, [(i, i ^ k) for i in range(size)])  17.3 us
    pallas_call x11, Pallas kernels, call(): pl.pallas_call(kernel, out_shape=out_shapes, in_specs=in_specs, out_specs...  8.31 us
  transfers between devices with their start and end apart: 16, of which 12 were waited for; matrix products, arithmetic and copies ran while one was open for 0% of the time, Pallas kernels for 8%

profile of v4, /device:TPU:0, one launch (start us, length us, event | category | flops | bytes accessed | tf_op | source)
XLA Modules:
  0.0 43.3 jit_solution(15730618597230513309)
XLA Ops:
  0.0 2.0 %shard_map.82 = (bf16[4,4,32,1024]{3,2,1,0:T(8,128)(2,1)S(1)}, bf16[1024,1024]{1,0:T(8,128)(2,1)S(1)}, bf16[4,4,32,128]{3,2,1,0:T(8,128)(2,1)S(1)}, bf16[4,32,128]{2,1,0:T(8,128)(2,1)S(1)}) custom-call(bf16[4,4,32,1024]{3,2,1,0:T(8,128)(2,1)} %bitcast.4, bf16[16,1024]{1,0:T(8,128)(2,1)} %bitcast.5, bf16[1024,1024]{1,0:T(8,128)(2,1)} %wv_hbm.1), custom_call_target="tpu_custom_call" | custom-call | flops 134217728 | bytes 6488064 | tf_op jit(solution)/shard_map/pallas_call | solution.py:180
  2.0 0.5 %shard_map.83 = bf16[32,1152]{1,0:T(8,128)(2,1)S(1)} custom-call(bf16[4,4,32,1024]{3,2,1,0:T(8,128)(2,1)S(1)} %get-tuple-element.23.x_ref, bf16[1024,1024]{1,0:T(8,128)(2,1)S(1)} %get-tuple-element.24.wv_ref, bf16[4,4,32,128]{3,2,1,0:T(8,128)(2,1)S(1)} %get-tuple-element.25.share_ref, bf16[4,32,128]{2,1,0:T(8,128)(2,1)S(1)} %get-tuple-element.26.stats_ref), custom_call_target="tpu_custom_call" | custom-call | flops 268435456 | bytes 3383296 | tf_op jit(solution)/shard_map/pallas_call | solution.py:180
  2.5 5.1 %collective-permute-start = (bf16[32,1152]{1,0:T(8,128)(2,1)S(1)}, bf16[32,1152]{1,0:T(8,128)(2,1)S(1)}, u32[]{:S(2)}, u32[]{:S(2)}) collective-permute-start(bf16[32,1152]{1,0:T(8,128)(2,1)S(1)} %shard_map.83), channel_id=1, source_target_pairs={{0,3},{1,2},{2,1},{3,0},{4,7},{5,6},{6,5},{7,4},{8,11},{9,10},{10,... | collective-permute-start | bytes 221192 | tf_op jit(solution)/shard_map/ppermute | solution.py:193
  7.6 0.5 %shard_map.84 = bf16[32,1152]{1,0:T(8,128)(2,1)S(1)} custom-call(bf16[4,4,32,1024]{3,2,1,0:T(8,128)(2,1)S(1)} %get-tuple-element.23.x_ref, bf16[1024,1024]{1,0:T(8,128)(2,1)S(1)} %get-tuple-element.24.wv_ref, bf16[4,4,32,128]{3,2,1,0:T(8,128)(2,1)S(1)} %get-tuple-element.25.share_ref, bf16[4,32,128]{2,1,0:T(8,128)(2,1)S(1)} %get-tuple-element.26.stats_ref), custom_call_target="tpu_custom_call" | custom-call | flops 268435456 | bytes 3383296 | tf_op jit(solution)/shard_map/pallas_call | solution.py:180
  8.1 0.0 copy-start.4
  8.1 0.1 collective-permute-start.1
  8.2 0.0 copy-start.2
  8.2 0.5 %shard_map.85 = bf16[32,1152]{1,0:T(8,128)(2,1)S(1)} custom-call(bf16[4,4,32,1024]{3,2,1,0:T(8,128)(2,1)S(1)} %get-tuple-element.23.x_ref, bf16[1024,1024]{1,0:T(8,128)(2,1)S(1)} %get-tuple-element.24.wv_ref, bf16[4,4,32,128]{3,2,1,0:T(8,128)(2,1)S(1)} %get-tuple-element.25.share_ref, bf16[4,32,128]{2,1,0:T(8,128)(2,1)S(1)} %get-tuple-element.26.stats_ref), custom_call_target="tpu_custom_call" | custom-call | flops 268435456 | bytes 3383296 | tf_op jit(solution)/shard_map/pallas_call | solution.py:180
  8.7 0.6 %collective-permute-start.2 = (bf16[32,1152]{1,0:T(8,128)(2,1)S(1)}, bf16[32,1152]{1,0:T(8,128)(2,1)S(1)}, u32[]{:S(2)}, u32[]{:S(2)}) collective-permute-start(bf16[32,1152]{1,0:T(8,128)(2,1)S(1)} %shard_map.85), channel_id=1, source_target_pairs={{0,1},{1,0},{2,3},{3,2},{4,5},{5,4},{6,7},{7,6},{8,9},{9,8},{10,11... | collective-permute-start | bytes 221192 | tf_op jit(solution)/shard_map/ppermute | solution.py:193
  9.3 0.0 copy-done.4
  9.3 0.0 copy-start
  9.3 0.0 copy-start.1
  9.4 0.5 %shard_map.86.refs_3_ = bf16[32,1152]{1,0:T(8,128)(2,1)S(1)} custom-call(bf16[4,4,32,1024]{3,2,1,0:T(8,128)(2,1)S(1)} %get-tuple-element.23.x_ref, bf16[1024,1024]{1,0:T(8,128)(2,1)S(1)} %get-tuple-element.24.wv_ref, bf16[4,4,32,128]{3,2,1,0:T(8,128)(2,1)S(1)} %get-tuple-element.25.share_ref, bf16[4,32,128]{2,1,0:T(8,128)(2,1)S(1)} %get-tuple-element.26.stats_ref), custom_call_target="tpu_custom_call" | custom-call | flops 268435456 | bytes 3383296 | tf_op jit(solution)/shard_map/pallas_call | solution.py:180
  9.8 0.4 %collective-permute-done.refs_0_ = bf16[32,1152]{1,0:T(8,128)(2,1)S(1)} collective-permute-done((bf16[32,1152]{1,0:T(8,128)(2,1)S(1)}, bf16[32,1152]{1,0:T(8,128)(2,1)S(1)}, u32[]{:S(2)}, u32[]{:S(2)}) %collective-permute-start) | collective-permute-done | bytes 73760 | tf_op jit(solution)/shard_map/ppermute | solution.py:193
  10.3 3.7 %collective-permute-done.1.refs_1_ = bf16[32,1152]{1,0:T(8,128)(2,1)S(1)} collective-permute-done((bf16[32,1152]{1,0:T(8,128)(2,1)S(1)}, bf16[32,1152]{1,0:T(8,128)(2,1)S(1)}, u32[]{:S(2)}, u32[]{:S(2)}) %collective-permute-start.1) | collective-permute-done | bytes 73760 | tf_op jit(solution)/shard_map/ppermute | solution.py:193
  14.0 0.5 %collective-permute-done.2.refs_2_ = bf16[32,1152]{1,0:T(8,128)(2,1)S(1)} collective-permute-done((bf16[32,1152]{1,0:T(8,128)(2,1)S(1)}, bf16[32,1152]{1,0:T(8,128)(2,1)S(1)}, u32[]{:S(2)}, u32[]{:S(2)}) %collective-permute-start.2) | collective-permute-done | bytes 73760 | tf_op jit(solution)/shard_map/ppermute | solution.py:193
  14.5 0.6 %shard_map.87 = (bf16[32,1024]{1,0:T(8,128)(2,1)S(1)}, bf16[32,1024]{1,0:T(8,128)(2,1)S(1)}) custom-call(bf16[1,1024]{1,0:T(2,128)(2,1)S(1)} %reshape.6.gain_ref, bf16[32,1152]{1,0:T(8,128)(2,1)S(1)} %collective-permute-done.refs_0_, bf16[32,1152]{1,0:T(8,128)(2,1)S(1)} %collective-permute-done.1.refs_1_, ...), custom_call_target="tpu_custom_call" | custom-call | bytes 428032 | tf_op jit(solution)/shard_map/pallas_call | solution.py:180
  15.0 1.6 %collective-permute-start.5 = (bf16[32,1024]{1,0:T(8,128)(2,1)S(1)}, bf16[32,1024]{1,0:T(8,128)(2,1)S(1)}, u32[]{:S(2)}, u32[]{:S(2)}) collective-permute-start(bf16[32,1024]{1,0:T(8,128)(2,1)S(1)} %get-tuple-element.28.refs_3_), channel_id=1, source_target_pairs={{0,2},{1,3},{2,0},{3,1},{4,6},{5,7},{6,4},{7,5},{8,10},{9,11},{10,... | collective-permute-start | bytes 196616 | tf_op jit(solution)/shard_map/ppermute | solution.py:193
  16.7 1.2 %collective-permute-start.4 = (bf16[32,1024]{1,0:T(8,128)(2,1)S(1)}, bf16[32,1024]{1,0:T(8,128)(2,1)S(1)}, u32[]{:S(2)}, u32[]{:S(2)}) collective-permute-start(bf16[32,1024]{1,0:T(8,128)(2,1)S(1)} %get-tuple-element.28.refs_3_), channel_id=1, source_target_pairs={{0,3},{1,2},{2,1},{3,0},{4,7},{5,6},{6,5},{7,4},{8,11},{9,10},{10,... | collective-permute-start | bytes 196616 | tf_op jit(solution)/shard_map/ppermute | solution.py:193
  17.8 0.8 %collective-permute-start.3 = (bf16[32,1024]{1,0:T(8,128)(2,1)S(1)}, bf16[32,1024]{1,0:T(8,128)(2,1)S(1)}, u32[]{:S(2)}, u32[]{:S(2)}) collective-permute-start(bf16[32,1024]{1,0:T(8,128)(2,1)S(1)} %get-tuple-element.28.refs_3_), channel_id=1, source_target_pairs={{0,1},{1,0},{2,3},{3,2},{4,5},{5,4},{6,7},{7,6},{8,9},{9,8},{10,11... | collective-permute-start | bytes 196616 | tf_op jit(solution)/shard_map/ppermute | solution.py:193
  18.6 3.4 %collective-permute-done.5.refs_2_ = bf16[32,1024]{1,0:T(8,128)(2,1)S(1)} collective-permute-done((bf16[32,1024]{1,0:T(8,128)(2,1)S(1)}, bf16[32,1024]{1,0:T(8,128)(2,1)S(1)}, u32[]{:S(2)}, u32[]{:S(2)}) %collective-permute-start.5) | collective-permute-done | bytes 65568 | tf_op jit(solution)/shard_map/ppermute | solution.py:193
  22.0 0.9 %collective-permute-done.4.refs_1_ = bf16[32,1024]{1,0:T(8,128)(2,1)S(1)} collective-permute-done((bf16[32,1024]{1,0:T(8,128)(2,1)S(1)}, bf16[32,1024]{1,0:T(8,128)(2,1)S(1)}, u32[]{:S(2)}, u32[]{:S(2)}) %collective-permute-start.4) | collective-permute-done | bytes 65568 | tf_op jit(solution)/shard_map/ppermute | solution.py:193
  22.9 0.2 collective-permute-done.3.refs_0_
  23.1 0.0 copy-done.2
  23.1 0.4 shard_map.88
  23.5 2.5 %collective-permute-start.6 = (bf16[128,512]{1,0:T(8,128)(2,1)S(1)}, bf16[128,512]{1,0:T(8,128)(2,1)S(1)}, u32[]{:S(2)}, u32[]{:S(2)}) collective-permute-start(bf16[128,512]{1,0:T(8,128)(2,1)S(1)} %get-tuple-element.33), channel_id=1, source_target_pairs={{0,24},{4,28},{8,16},{12,20},{16,8},{20,12},{24,0},{28,4},{1,25},{... | collective-permute-start | bytes 393224 | tf_op jit(solution)/shard_map/ppermute | solution.py:193
  26.0 0.5 %collective-permute-start.8 = (bf16[128,512]{1,0:T(8,128)(2,1)S(1)}, bf16[128,512]{1,0:T(8,128)(2,1)S(1)}, u32[]{:S(2)}, u32[]{:S(2)}) collective-permute-start(bf16[128,512]{1,0:T(8,128)(2,1)S(1)} %get-tuple-element.33), channel_id=1, source_target_pairs={{0,8},{4,12},{8,0},{12,4},{16,24},{20,28},{24,16},{28,20},{1,9},{5... | collective-permute-start | bytes 393224 | tf_op jit(solution)/shard_map/ppermute | solution.py:193
  26.5 0.5 %collective-permute-start.7 = (bf16[128,512]{1,0:T(8,128)(2,1)S(1)}, bf16[128,512]{1,0:T(8,128)(2,1)S(1)}, u32[]{:S(2)}, u32[]{:S(2)}) collective-permute-start(bf16[128,512]{1,0:T(8,128)(2,1)S(1)} %get-tuple-element.33), channel_id=1, source_target_pairs={{0,16},{4,20},{8,24},{12,28},{16,0},{20,4},{24,8},{28,12},{1,17},{... | collective-permute-start | bytes 393224 | tf_op jit(solution)/shard_map/ppermute | solution.py:193
  27.1 0.0 copy-done
  27.1 0.0 copy-done.1
  27.1 0.0 copy-start.3
  27.1 0.8 %shard_map.89 = (f32[128,1024]{1,0:T(8,128)S(1)}, bf16[128,512]{1,0:T(8,128)(2,1)S(1)}) custom-call(bf16[1024,1024]{1,0:T(8,128)(2,1)S(1)} %copy-done, bf16[1024,1024]{1,0:T(8,128)(2,1)S(1)} %copy-done.1, bf16[32,1024]{1,0:T(8,128)(2,1)S(1)} %collective-permute-done.3.refs_0_, ...), custom_call_target="tpu_custom_call", output_to_operand_aliasing={{1}: (6, {})} | custom-call | flops 536870912 | bytes 5242880 | tf_op jit(solution)/shard_map/pallas_call | solution.py:180
  27.9 0.1 collective-permute-start.9
  28.0 1.4 %collective-permute-done.6.refs_1_ = bf16[128,512]{1,0:T(8,128)(2,1)S(1)} collective-permute-done((bf16[128,512]{1,0:T(8,128)(2,1)S(1)}, bf16[128,512]{1,0:T(8,128)(2,1)S(1)}, u32[]{:S(2)}, u32[]{:S(2)}) %collective-permute-start.6) | collective-permute-done | bytes 131104 | tf_op jit(solution)/shard_map/ppermute | solution.py:193
  29.5 0.0 collective-permute-start.10
  29.5 1.5 %collective-permute-done.8.refs_3_ = bf16[128,512]{1,0:T(8,128)(2,1)S(1)} collective-permute-done((bf16[128,512]{1,0:T(8,128)(2,1)S(1)}, bf16[128,512]{1,0:T(8,128)(2,1)S(1)}, u32[]{:S(2)}, u32[]{:S(2)}) %collective-permute-start.8) | collective-permute-done | bytes 131104 | tf_op jit(solution)/shard_map/ppermute | solution.py:193
  31.0 0.0 collective-permute-start.12
  31.0 0.5 %collective-permute-done.7.refs_2_ = bf16[128,512]{1,0:T(8,128)(2,1)S(1)} collective-permute-done((bf16[128,512]{1,0:T(8,128)(2,1)S(1)}, bf16[128,512]{1,0:T(8,128)(2,1)S(1)}, u32[]{:S(2)}, u32[]{:S(2)}) %collective-permute-start.7) | collective-permute-done | bytes 131104 | tf_op jit(solution)/shard_map/ppermute | solution.py:193
  31.5 0.0 collective-permute-start.11
  31.5 0.0 collective-permute-done.9.refs_4_
  31.5 0.0 collective-permute-done.10.refs_5_
  31.5 1.2 %shard_map.90 = (f32[128,256]{1,0:T(8,128)S(1)}, f32[128,256]{1,0:T(8,128)S(1)}, f32[128,256]{1,0:T(8,128)S(1)}) custom-call(bf16[128,256]{1,0:T(8,128)(2,1)S(1)} %get-tuple-element.29.q_ref, bf16[128,512]{1,0:T(8,128)(2,1)S(1)} %get-tuple-element.32.refs_0_, bf16[128,512]{1,0:T(8,128)(2,1)S(1)} %collective-permute-done.6.refs_1_, ...), custom_call_target="tpu_custom_call" | custom-call | flops 402653184 | bytes 1245184 | tf_op jit(solution)/shard_map/pallas_call | solution.py:180
  32.7 0.0 collective-permute-done.12.refs_1_
  32.7 0.2 collective-permute-done.11.refs_0_
  32.9 0.0 copy-done.3
  32.9 0.7 %shard_map.91 = (bf16[32,1024]{1,0:T(8,128)(2,1)S(1)}, bf16[32,1024]{1,0:T(8,128)(2,1)S(1)}, bf16[32,1024]{1,0:T(8,128)(2,1)S(1)}, bf16[32,1024]{1,0:T(8,128)(2,1)S(1)}) custom-call(bf16[128,256]{1,0:T(8,128)(2,1)S(1)} %get-tuple-element.29.q_ref, f32[128,1024]{1,0:T(8,128)S(1)} %get-tuple-element.31.ffn_ref, bf16[256,1024]{1,0:T(8,128)(2,1)S(1)} %copy-done.3, ...), custom_call_target="tpu_custom_call" | custom-call | flops 134217728 | bytes 2031616 | tf_op jit(solution)/shard_map/pallas_call | solution.py:180
  33.6 1.4 %collective-permute-start.13 = (bf16[32,1024]{1,0:T(8,128)(2,1)S(1)}, bf16[32,1024]{1,0:T(8,128)(2,1)S(1)}, u32[]{:S(2)}, u32[]{:S(2)}) collective-permute-start(bf16[32,1024]{1,0:T(8,128)(2,1)S(1)} %get-tuple-element.37), channel_id=1, source_target_pairs={{0,2},{1,3},{2,0},{3,1},{4,6},{5,7},{6,4},{7,5},{8,10},{9,11},{10,... | collective-permute-start | bytes 196616 | tf_op jit(solution)/shard_map/ppermute | solution.py:193
  35.0 1.5 %collective-permute-start.14 = (bf16[32,1024]{1,0:T(8,128)(2,1)S(1)}, bf16[32,1024]{1,0:T(8,128)(2,1)S(1)}, u32[]{:S(2)}, u32[]{:S(2)}) collective-permute-start(bf16[32,1024]{1,0:T(8,128)(2,1)S(1)} %get-tuple-element.38), channel_id=1, source_target_pairs={{0,1},{1,0},{2,3},{3,2},{4,5},{5,4},{6,7},{7,6},{8,9},{9,8},{10,11... | collective-permute-start | bytes 196616 | tf_op jit(solution)/shard_map/ppermute | solution.py:193
  36.5 1.6 %collective-permute-start.15 = (bf16[32,1024]{1,0:T(8,128)(2,1)S(1)}, bf16[32,1024]{1,0:T(8,128)(2,1)S(1)}, u32[]{:S(2)}, u32[]{:S(2)}) collective-permute-start(bf16[32,1024]{1,0:T(8,128)(2,1)S(1)} %get-tuple-element.39), channel_id=1, source_target_pairs={{0,3},{1,2},{2,1},{3,0},{4,7},{5,6},{6,5},{7,4},{8,11},{9,10},{10,... | collective-permute-start | bytes 196616 | tf_op jit(solution)/shard_map/ppermute | solution.py:193
  38.1 2.6 %collective-permute-done.13.refs_1_ = bf16[32,1024]{1,0:T(8,128)(2,1)S(1)} collective-permute-done((bf16[32,1024]{1,0:T(8,128)(2,1)S(1)}, bf16[32,1024]{1,0:T(8,128)(2,1)S(1)}, u32[]{:S(2)}, u32[]{:S(2)}) %collective-permute-start.13) | collective-permute-done | bytes 65568 | tf_op jit(solution)/shard_map/ppermute | solution.py:193
  40.7 0.0 collective-permute-done.14.refs_2_
  40.7 1.9 %collective-permute-done.15.refs_3_ = bf16[32,1024]{1,0:T(8,128)(2,1)S(1)} collective-permute-done((bf16[32,1024]{1,0:T(8,128)(2,1)S(1)}, bf16[32,1024]{1,0:T(8,128)(2,1)S(1)}, u32[]{:S(2)}, u32[]{:S(2)}) %collective-permute-start.15) | collective-permute-done | bytes 65568 | tf_op jit(solution)/shard_map/ppermute | solution.py:193
  42.6 0.7 %shard_map.92 = bf16[32,1024]{1,0:T(8,128)(2,1)} custom-call(bf16[32,1024]{1,0:T(8,128)(2,1)S(1)} %get-tuple-element.27.refs_0_, bf16[32,1024]{1,0:T(8,128)(2,1)S(1)} %collective-permute-done.13.refs_1_, bf16[32,1024]{1,0:T(8,128)(2,1)S(1)} %collective-permute-done.14.refs_2_, bf16[32,1024]{1,0:T(8,128)(2,1)S(1)} %collective-permute-done.15.refs_3_, ...), custom_call_target="tpu_custom_call" | custom-call | bytes 393216 | tf_op jit(solution)/shard_map/pallas_call | solution.py:180
  (1 shorter events, 0.0 us)
Async XLA Ops:
  2.5 7.8 %collective-permute-start = (bf16[32,1152]{1,0:T(8,128)(2,1)S(1)}, bf16[32,1152]{1,0:T(8,128)(2,1)S(1)}, u32[]{:S(2)}, u32[]{:S(2)}) collective-permute-start(bf16[32,1152]{1,0:T(8,128)(2,1)S(1)} %shard_map.83), channel_id=1, source_target_pairs={{0,3},{1,2},{2,1},{3,0},{4,7},{5,6},{6,5},{7,4},{8,11},{9,10},{10,... | collective-permute-start | bytes 221192 | tf_op jit(solution)/shard_map/ppermute | solution.py:193
  8.1 1.2 %copy-start.4 = (bf16[1024]{0:T(1024)(128)(2,1)S(1)}, bf16[1024]{0:T(1024)(128)(2,1)}, u32[]{:S(2)}) copy-start(bf16[1024]{0:T(1024)(128)(2,1)} %param.15) | copy-start | bytes 6148
  8.1 5.8 %collective-permute-start.1 = (bf16[32,1152]{1,0:T(8,128)(2,1)S(1)}, bf16[32,1152]{1,0:T(8,128)(2,1)S(1)}, u32[]{:S(2)}, u32[]{:S(2)}) collective-permute-start(bf16[32,1152]{1,0:T(8,128)(2,1)S(1)} %shard_map.84), channel_id=1, source_target_pairs={{0,2},{1,3},{2,0},{3,1},{4,6},{5,7},{6,4},{7,5},{8,10},{9,11},{10,... | collective-permute-start | bytes 221192 | tf_op jit(solution)/shard_map/ppermute | solution.py:193
  8.2 14.9 %copy-start.2 = (bf16[1024,3,256]{2,0,1:T(8,128)(2,1)S(1)}, bf16[1024,3,256]{2,0,1:T(8,128)(2,1)}, u32[]{:S(2)}) copy-start(bf16[1024,3,256]{2,0,1:T(8,128)(2,1)} %param.11) | copy-start | bytes 4718596
  8.7 5.7 %collective-permute-start.2 = (bf16[32,1152]{1,0:T(8,128)(2,1)S(1)}, bf16[32,1152]{1,0:T(8,128)(2,1)S(1)}, u32[]{:S(2)}, u32[]{:S(2)}) collective-permute-start(bf16[32,1152]{1,0:T(8,128)(2,1)S(1)} %shard_map.85), channel_id=1, source_target_pairs={{0,1},{1,0},{2,3},{3,2},{4,5},{5,4},{6,7},{7,6},{8,9},{9,8},{10,11... | collective-permute-start | bytes 221192 | tf_op jit(solution)/shard_map/ppermute | solution.py:193
  9.3 17.7 %copy-start = (bf16[1024,1024]{1,0:T(8,128)(2,1)S(1)}, bf16[1024,1024]{1,0:T(8,128)(2,1)}, u32[]{:S(2)}) copy-start(bf16[1024,1024]{1,0:T(8,128)(2,1)} %up_ref.1) | copy-start | bytes 6291460
  9.3 17.7 %copy-start.1 = (bf16[1024,1024]{1,0:T(8,128)(2,1)S(1)}, bf16[1024,1024]{1,0:T(8,128)(2,1)}, u32[]{:S(2)}) copy-start(bf16[1024,1024]{1,0:T(8,128)(2,1)} %down_ref.1) | copy-start | bytes 6291460
  15.0 7.0 %collective-permute-start.5 = (bf16[32,1024]{1,0:T(8,128)(2,1)S(1)}, bf16[32,1024]{1,0:T(8,128)(2,1)S(1)}, u32[]{:S(2)}, u32[]{:S(2)}) collective-permute-start(bf16[32,1024]{1,0:T(8,128)(2,1)S(1)} %get-tuple-element.28.refs_3_), channel_id=1, source_target_pairs={{0,2},{1,3},{2,0},{3,1},{4,6},{5,7},{6,4},{7,5},{8,10},{9,11},{10,... | collective-permute-start | bytes 196616 | tf_op jit(solution)/shard_map/ppermute | solution.py:193
  16.7 6.2 %collective-permute-start.4 = (bf16[32,1024]{1,0:T(8,128)(2,1)S(1)}, bf16[32,1024]{1,0:T(8,128)(2,1)S(1)}, u32[]{:S(2)}, u32[]{:S(2)}) collective-permute-start(bf16[32,1024]{1,0:T(8,128)(2,1)S(1)} %get-tuple-element.28.refs_3_), channel_id=1, source_target_pairs={{0,3},{1,2},{2,1},{3,0},{4,7},{5,6},{6,5},{7,4},{8,11},{9,10},{10,... | collective-permute-start | bytes 196616 | tf_op jit(solution)/shard_map/ppermute | solution.py:193
  17.8 5.3 %collective-permute-start.3 = (bf16[32,1024]{1,0:T(8,128)(2,1)S(1)}, bf16[32,1024]{1,0:T(8,128)(2,1)S(1)}, u32[]{:S(2)}, u32[]{:S(2)}) collective-permute-start(bf16[32,1024]{1,0:T(8,128)(2,1)S(1)} %get-tuple-element.28.refs_3_), channel_id=1, source_target_pairs={{0,1},{1,0},{2,3},{3,2},{4,5},{5,4},{6,7},{7,6},{8,9},{9,8},{10,11... | collective-permute-start | bytes 196616 | tf_op jit(solution)/shard_map/ppermute | solution.py:193
  23.5 5.9 %collective-permute-start.6 = (bf16[128,512]{1,0:T(8,128)(2,1)S(1)}, bf16[128,512]{1,0:T(8,128)(2,1)S(1)}, u32[]{:S(2)}, u32[]{:S(2)}) collective-permute-start(bf16[128,512]{1,0:T(8,128)(2,1)S(1)} %get-tuple-element.33), channel_id=1, source_target_pairs={{0,24},{4,28},{8,16},{12,20},{16,8},{20,12},{24,0},{28,4},{1,25},{... | collective-permute-start | bytes 393224 | tf_op jit(solution)/shard_map/ppermute | solution.py:193
  26.0 5.0 %collective-permute-start.8 = (bf16[128,512]{1,0:T(8,128)(2,1)S(1)}, bf16[128,512]{1,0:T(8,128)(2,1)S(1)}, u32[]{:S(2)}, u32[]{:S(2)}) collective-permute-start(bf16[128,512]{1,0:T(8,128)(2,1)S(1)} %get-tuple-element.33), channel_id=1, source_target_pairs={{0,8},{4,12},{8,0},{12,4},{16,24},{20,28},{24,16},{28,20},{1,9},{5... | collective-permute-start | bytes 393224 | tf_op jit(solution)/shard_map/ppermute | solution.py:193
  26.5 5.0 %collective-permute-start.7 = (bf16[128,512]{1,0:T(8,128)(2,1)S(1)}, bf16[128,512]{1,0:T(8,128)(2,1)S(1)}, u32[]{:S(2)}, u32[]{:S(2)}) collective-permute-start(bf16[128,512]{1,0:T(8,128)(2,1)S(1)} %get-tuple-element.33), channel_id=1, source_target_pairs={{0,16},{4,20},{8,24},{12,28},{16,0},{20,4},{24,8},{28,12},{1,17},{... | collective-permute-start | bytes 393224 | tf_op jit(solution)/shard_map/ppermute | solution.py:193
  27.1 5.8 %copy-start.3 = (bf16[256,1024]{1,0:T(8,128)(2,1)S(1)}, bf16[256,1024]{1,0:T(8,128)(2,1)}, u32[]{:S(2)}) copy-start(bf16[256,1024]{1,0:T(8,128)(2,1)} %wo_ref.1) | copy-start | bytes 1572868
  27.9 3.6 %collective-permute-start.9 = (bf16[128,512]{1,0:T(8,128)(2,1)S(1)}, bf16[128,512]{1,0:T(8,128)(2,1)S(1)}, u32[]{:S(2)}, u32[]{:S(2)}) collective-permute-start(bf16[128,512]{1,0:T(8,128)(2,1)S(1)} %get-tuple-element.32.refs_0_), channel_id=1, source_target_pairs={{0,4},{4,0},{8,12},{12,8},{16,20},{20,16},{24,28},{28,24},{1,5},{5... | collective-permute-start | bytes 393224 | tf_op jit(solution)/shard_map/ppermute | solution.py:193
  29.5 2.1 %collective-permute-start.10 = (bf16[128,512]{1,0:T(8,128)(2,1)S(1)}, bf16[128,512]{1,0:T(8,128)(2,1)S(1)}, u32[]{:S(2)}, u32[]{:S(2)}) collective-permute-start(bf16[128,512]{1,0:T(8,128)(2,1)S(1)} %collective-permute-done.6.refs_1_), channel_id=1, source_target_pairs={{0,4},{4,0},{8,12},{12,8},{16,20},{20,16},{24,28},{28,24},{1,5},{5... | collective-permute-start | bytes 393224 | tf_op jit(solution)/shard_map/ppermute | solution.py:193
  31.0 1.7 %collective-permute-start.12 = (bf16[128,512]{1,0:T(8,128)(2,1)S(1)}, bf16[128,512]{1,0:T(8,128)(2,1)S(1)}, u32[]{:S(2)}, u32[]{:S(2)}) collective-permute-start(bf16[128,512]{1,0:T(8,128)(2,1)S(1)} %collective-permute-done.8.refs_3_), channel_id=1, source_target_pairs={{0,4},{4,0},{8,12},{12,8},{16,20},{20,16},{24,28},{28,24},{1,5},{5... | collective-permute-start | bytes 393224 | tf_op jit(solution)/shard_map/ppermute | solution.py:193
  31.5 1.3 %collective-permute-start.11 = (bf16[128,512]{1,0:T(8,128)(2,1)S(1)}, bf16[128,512]{1,0:T(8,128)(2,1)S(1)}, u32[]{:S(2)}, u32[]{:S(2)}) collective-permute-start(bf16[128,512]{1,0:T(8,128)(2,1)S(1)} %collective-permute-done.7.refs_2_), channel_id=1, source_target_pairs={{0,4},{4,0},{8,12},{12,8},{16,20},{20,16},{24,28},{28,24},{1,5},{5... | collective-permute-start | bytes 393224 | tf_op jit(solution)/shard_map/ppermute | solution.py:193
  33.6 7.1 %collective-permute-start.13 = (bf16[32,1024]{1,0:T(8,128)(2,1)S(1)}, bf16[32,1024]{1,0:T(8,128)(2,1)S(1)}, u32[]{:S(2)}, u32[]{:S(2)}) collective-permute-start(bf16[32,1024]{1,0:T(8,128)(2,1)S(1)} %get-tuple-element.37), channel_id=1, source_target_pairs={{0,2},{1,3},{2,0},{3,1},{4,6},{5,7},{6,4},{7,5},{8,10},{9,11},{10,... | collective-permute-start | bytes 196616 | tf_op jit(solution)/shard_map/ppermute | solution.py:193
  35.0 5.7 %collective-permute-start.14 = (bf16[32,1024]{1,0:T(8,128)(2,1)S(1)}, bf16[32,1024]{1,0:T(8,128)(2,1)S(1)}, u32[]{:S(2)}, u32[]{:S(2)}) collective-permute-start(bf16[32,1024]{1,0:T(8,128)(2,1)S(1)} %get-tuple-element.38), channel_id=1, source_target_pairs={{0,1},{1,0},{2,3},{3,2},{4,5},{5,4},{6,7},{7,6},{8,9},{9,8},{10,11... | collective-permute-start | bytes 196616 | tf_op jit(solution)/shard_map/ppermute | solution.py:193
  36.5 6.1 %collective-permute-start.15 = (bf16[32,1024]{1,0:T(8,128)(2,1)S(1)}, bf16[32,1024]{1,0:T(8,128)(2,1)S(1)}, u32[]{:S(2)}, u32[]{:S(2)}) collective-permute-start(bf16[32,1024]{1,0:T(8,128)(2,1)S(1)} %get-tuple-element.39), channel_id=1, source_target_pairs={{0,3},{1,2},{2,1},{3,0},{4,7},{5,6},{6,5},{7,4},{8,11},{9,10},{10,... | collective-permute-start | bytes 196616 | tf_op jit(solution)/shard_map/ppermute | solution.py:193

commit v5 on v4

--- a/solution.py
+++ b/solution.py
@@ -118,39 +118,43 @@
     out_ref[...] = jnp.dot(hidden, down_ref[...], preferred_element_type=f32)
 
 
-def attend(heads, q_ref, blocks):
+def attend(heads, q_ref, blocks, span):
     rows, width = q_ref.shape
     head_dim = width // heads
-    q = q_ref[...].astype(f32) * head_dim ** (-0.5)
-    owner = lax.broadcasted_iota(jnp.int32, (rows, width), 1) // head_dim
-    stacked = jnp.concatenate([jnp.where(owner == h, q, 0.0) for h in range(heads)], axis=0)
-    stacked = stacked.astype(bf16)
-    keys = jnp.concatenate([b[:, :width] for b in blocks], axis=0)
-    vals = jnp.concatenate([b[:, width:] for b in blocks], axis=0)
-    logits = lax.dot_general(stacked, keys, (((1,), (1,)), ((), ())), preferred_element_type=f32)
-    top = jnp.max(logits, axis=1, keepdims=True)
-    terms = jnp.exp(logits - top)
-    total = jnp.sum(terms, axis=1, keepdims=True)
-    mixed = jnp.dot(terms.astype(bf16), vals, preferred_element_type=f32)
-
-    def own_head(stack):
-        out = jnp.broadcast_to(stack[:rows], (rows, width))
-        for h in range(1, heads):
-            out = jnp.where(owner == h, stack[h * rows : (h + 1) * rows], out)
-        return out
-
-    return own_head(mixed), own_head(top), own_head(total)
+    span = min(width, span)
+    owner = lax.broadcasted_iota(jnp.int32, (rows, span), 1) // head_dim
+    together = span // head_dim
+    results = []
+    for first in range(0, width, span):
+        own = slice(first, first + span)
+        q = q_ref[:, own].astype(f32) * head_dim ** (-0.5)
+        q = jnp.concatenate([jnp.where(owner == h, q, 0.0) for h in range(together)], axis=0)
+        keys = jnp.concatenate([b[:, own] for b in blocks], axis=0)
+        vals = jnp.concatenate([b[:, width + first : width + first + span] for b in blocks], axis=0)
+        logits = lax.dot_general(
+            q.astype(bf16), keys, (((1,), (1,)), ((), ())), preferred_element_type=f32
+        )
+        top = jnp.max(logits, axis=1, keepdims=True)
+        terms = jnp.exp(logits - top)
+        total = jnp.sum(terms, axis=1, keepdims=True)
+        mixed = jnp.dot(terms.astype(bf16), vals, preferred_element_type=f32)
+        for i, stack in enumerate((mixed, top, total)):
+            out = jnp.broadcast_to(stack[:rows], (rows, span))
+            for h in range(1, together):
+                out = jnp.where(owner == h, stack[h * rows : (h + 1) * rows], out)
+            results.append(out)
+    return [jnp.concatenate(results[i::3], axis=1) for i in range(3)]
 
 
 def early_kernel(heads, q_ref, *refs):
     blocks, out_refs = refs[:-3], refs[-3:]
-    for ref, value in zip(out_refs, attend(heads, q_ref, blocks)):
+    for ref, value in zip(out_refs, attend(heads, q_ref, blocks, LANES)):
         ref[...] = value
 
 
 def attend_kernel(heads, groups, q_ref, ffn_ref, wo_ref, mixed_ref, top_ref, total_ref, *refs):
     blocks, out_refs = refs[:-groups], refs[-groups:]
-    mixed, top, total = attend(heads, q_ref, blocks)
+    mixed, top, total = attend(heads, q_ref, blocks, q_ref.shape[1])
     both = jnp.maximum(top, top_ref[...])
     late, early = jnp.exp(top - both), jnp.exp(top_ref[...] - both)
     attended = (mixed * late + mixed_ref[...] * early) / (total * late + total_ref[...] * early)

time: 43.4 us -> 43.4 us (level)
  no operation moved by 1% of the time
where the time goes in v5:
time: 43.4 us; the launch traced here: 43.2 us
  waiting for transfers between devices  17.5 us (40%)
  starting transfers between devices  17.4 us (40%)
  Pallas kernels  8.15 us (19%)
    ppermute x16, waiting for transfers between devices, exchange(): lax.ppermute(parts[k], axis, [(i, i ^ k) for i in range(size)])  17.5 us
    ppermute x16, starting transfers between devices, exchange(): lax.ppermute(parts[k], axis, [(i, i ^ k) for i in range(size)])  17.4 us
    pallas_call x11, Pallas kernels, call(): pl.pallas_call(kernel, out_shape=out_shapes, in_specs=in_specs, out_specs...  8.15 us
  transfers between devices with their start and end apart: 16, of which 12 were waited for; matrix products, arithmetic and copies ran while one was open for 0% of the time, Pallas kernels for 8%

profile of v5, /device:TPU:0, one launch (start us, length us, event | category | flops | bytes accessed | tf_op | source)
XLA Modules:
  0.0 43.2 jit_solution(5381913263884517249)
XLA Ops:
  0.0 2.0 %shard_map.82 = (bf16[4,4,32,1024]{3,2,1,0:T(8,128)(2,1)S(1)}, bf16[1024,1024]{1,0:T(8,128)(2,1)S(1)}, bf16[4,4,32,128]{3,2,1,0:T(8,128)(2,1)S(1)}, bf16[4,32,128]{2,1,0:T(8,128)(2,1)S(1)}) custom-call(bf16[4,4,32,1024]{3,2,1,0:T(8,128)(2,1)} %bitcast.4, bf16[16,1024]{1,0:T(8,128)(2,1)} %bitcast.5, bf16[1024,1024]{1,0:T(8,128)(2,1)} %wv_hbm.1), custom_call_target="tpu_custom_call" | custom-call | flops 134217728 | bytes 6488064 | tf_op jit(solution)/shard_map/pallas_call | solution.py:184
  2.0 0.5 %shard_map.83 = bf16[32,1152]{1,0:T(8,128)(2,1)S(1)} custom-call(bf16[4,4,32,1024]{3,2,1,0:T(8,128)(2,1)S(1)} %get-tuple-element.23.x_ref, bf16[1024,1024]{1,0:T(8,128)(2,1)S(1)} %get-tuple-element.24.wv_ref, bf16[4,4,32,128]{3,2,1,0:T(8,128)(2,1)S(1)} %get-tuple-element.25.share_ref, bf16[4,32,128]{2,1,0:T(8,128)(2,1)S(1)} %get-tuple-element.26.stats_ref), custom_call_target="tpu_custom_call" | custom-call | flops 268435456 | bytes 3383296 | tf_op jit(solution)/shard_map/pallas_call | solution.py:184
  2.5 5.1 %collective-permute-start = (bf16[32,1152]{1,0:T(8,128)(2,1)S(1)}, bf16[32,1152]{1,0:T(8,128)(2,1)S(1)}, u32[]{:S(2)}, u32[]{:S(2)}) collective-permute-start(bf16[32,1152]{1,0:T(8,128)(2,1)S(1)} %shard_map.83), channel_id=1, source_target_pairs={{0,3},{1,2},{2,1},{3,0},{4,7},{5,6},{6,5},{7,4},{8,11},{9,10},{10,... | collective-permute-start | bytes 221192 | tf_op jit(solution)/shard_map/ppermute | solution.py:197
  7.6 0.5 %shard_map.84 = bf16[32,1152]{1,0:T(8,128)(2,1)S(1)} custom-call(bf16[4,4,32,1024]{3,2,1,0:T(8,128)(2,1)S(1)} %get-tuple-element.23.x_ref, bf16[1024,1024]{1,0:T(8,128)(2,1)S(1)} %get-tuple-element.24.wv_ref, bf16[4,4,32,128]{3,2,1,0:T(8,128)(2,1)S(1)} %get-tuple-element.25.share_ref, bf16[4,32,128]{2,1,0:T(8,128)(2,1)S(1)} %get-tuple-element.26.stats_ref), custom_call_target="tpu_custom_call" | custom-call | flops 268435456 | bytes 3383296 | tf_op jit(solution)/shard_map/pallas_call | solution.py:184
  8.1 0.0 copy-start.4
  8.1 0.1 collective-permute-start.1
  8.2 0.0 copy-start.2
  8.2 0.5 %shard_map.85 = bf16[32,1152]{1,0:T(8,128)(2,1)S(1)} custom-call(bf16[4,4,32,1024]{3,2,1,0:T(8,128)(2,1)S(1)} %get-tuple-element.23.x_ref, bf16[1024,1024]{1,0:T(8,128)(2,1)S(1)} %get-tuple-element.24.wv_ref, bf16[4,4,32,128]{3,2,1,0:T(8,128)(2,1)S(1)} %get-tuple-element.25.share_ref, bf16[4,32,128]{2,1,0:T(8,128)(2,1)S(1)} %get-tuple-element.26.stats_ref), custom_call_target="tpu_custom_call" | custom-call | flops 268435456 | bytes 3383296 | tf_op jit(solution)/shard_map/pallas_call | solution.py:184
  8.7 0.6 %collective-permute-start.2 = (bf16[32,1152]{1,0:T(8,128)(2,1)S(1)}, bf16[32,1152]{1,0:T(8,128)(2,1)S(1)}, u32[]{:S(2)}, u32[]{:S(2)}) collective-permute-start(bf16[32,1152]{1,0:T(8,128)(2,1)S(1)} %shard_map.85), channel_id=1, source_target_pairs={{0,1},{1,0},{2,3},{3,2},{4,5},{5,4},{6,7},{7,6},{8,9},{9,8},{10,11... | collective-permute-start | bytes 221192 | tf_op jit(solution)/shard_map/ppermute | solution.py:197
  9.3 0.0 copy-done.4
  9.3 0.0 copy-start
  9.3 0.0 copy-start.1
  9.4 0.5 %shard_map.86.refs_3_ = bf16[32,1152]{1,0:T(8,128)(2,1)S(1)} custom-call(bf16[4,4,32,1024]{3,2,1,0:T(8,128)(2,1)S(1)} %get-tuple-element.23.x_ref, bf16[1024,1024]{1,0:T(8,128)(2,1)S(1)} %get-tuple-element.24.wv_ref, bf16[4,4,32,128]{3,2,1,0:T(8,128)(2,1)S(1)} %get-tuple-element.25.share_ref, bf16[4,32,128]{2,1,0:T(8,128)(2,1)S(1)} %get-tuple-element.26.stats_ref), custom_call_target="tpu_custom_call" | custom-call | flops 268435456 | bytes 3383296 | tf_op jit(solution)/shard_map/pallas_call | solution.py:184
  9.8 0.4 %collective-permute-done.refs_0_ = bf16[32,1152]{1,0:T(8,128)(2,1)S(1)} collective-permute-done((bf16[32,1152]{1,0:T(8,128)(2,1)S(1)}, bf16[32,1152]{1,0:T(8,128)(2,1)S(1)}, u32[]{:S(2)}, u32[]{:S(2)}) %collective-permute-start) | collective-permute-done | bytes 73760 | tf_op jit(solution)/shard_map/ppermute | solution.py:197
  10.3 3.7 %collective-permute-done.1.refs_1_ = bf16[32,1152]{1,0:T(8,128)(2,1)S(1)} collective-permute-done((bf16[32,1152]{1,0:T(8,128)(2,1)S(1)}, bf16[32,1152]{1,0:T(8,128)(2,1)S(1)}, u32[]{:S(2)}, u32[]{:S(2)}) %collective-permute-start.1) | collective-permute-done | bytes 73760 | tf_op jit(solution)/shard_map/ppermute | solution.py:197
  14.0 0.5 %collective-permute-done.2.refs_2_ = bf16[32,1152]{1,0:T(8,128)(2,1)S(1)} collective-permute-done((bf16[32,1152]{1,0:T(8,128)(2,1)S(1)}, bf16[32,1152]{1,0:T(8,128)(2,1)S(1)}, u32[]{:S(2)}, u32[]{:S(2)}) %collective-permute-start.2) | collective-permute-done | bytes 73760 | tf_op jit(solution)/shard_map/ppermute | solution.py:197
  14.5 0.6 %shard_map.87 = (bf16[32,1024]{1,0:T(8,128)(2,1)S(1)}, bf16[32,1024]{1,0:T(8,128)(2,1)S(1)}) custom-call(bf16[1,1024]{1,0:T(2,128)(2,1)S(1)} %reshape.6.gain_ref, bf16[32,1152]{1,0:T(8,128)(2,1)S(1)} %collective-permute-done.refs_0_, bf16[32,1152]{1,0:T(8,128)(2,1)S(1)} %collective-permute-done.1.refs_1_, ...), custom_call_target="tpu_custom_call" | custom-call | bytes 428032 | tf_op jit(solution)/shard_map/pallas_call | solution.py:184
  15.0 1.6 %collective-permute-start.5 = (bf16[32,1024]{1,0:T(8,128)(2,1)S(1)}, bf16[32,1024]{1,0:T(8,128)(2,1)S(1)}, u32[]{:S(2)}, u32[]{:S(2)}) collective-permute-start(bf16[32,1024]{1,0:T(8,128)(2,1)S(1)} %get-tuple-element.28.refs_3_), channel_id=1, source_target_pairs={{0,2},{1,3},{2,0},{3,1},{4,6},{5,7},{6,4},{7,5},{8,10},{9,11},{10,... | collective-permute-start | bytes 196616 | tf_op jit(solution)/shard_map/ppermute | solution.py:197
  16.7 1.2 %collective-permute-start.4 = (bf16[32,1024]{1,0:T(8,128)(2,1)S(1)}, bf16[32,1024]{1,0:T(8,128)(2,1)S(1)}, u32[]{:S(2)}, u32[]{:S(2)}) collective-permute-start(bf16[32,1024]{1,0:T(8,128)(2,1)S(1)} %get-tuple-element.28.refs_3_), channel_id=1, source_target_pairs={{0,3},{1,2},{2,1},{3,0},{4,7},{5,6},{6,5},{7,4},{8,11},{9,10},{10,... | collective-permute-start | bytes 196616 | tf_op jit(solution)/shard_map/ppermute | solution.py:197
  17.8 0.8 %collective-permute-start.3 = (bf16[32,1024]{1,0:T(8,128)(2,1)S(1)}, bf16[32,1024]{1,0:T(8,128)(2,1)S(1)}, u32[]{:S(2)}, u32[]{:S(2)}) collective-permute-start(bf16[32,1024]{1,0:T(8,128)(2,1)S(1)} %get-tuple-element.28.refs_3_), channel_id=1, source_target_pairs={{0,1},{1,0},{2,3},{3,2},{4,5},{5,4},{6,7},{7,6},{8,9},{9,8},{10,11... | collective-permute-start | bytes 196616 | tf_op jit(solution)/shard_map/ppermute | solution.py:197
  18.6 3.4 %collective-permute-done.5.refs_2_ = bf16[32,1024]{1,0:T(8,128)(2,1)S(1)} collective-permute-done((bf16[32,1024]{1,0:T(8,128)(2,1)S(1)}, bf16[32,1024]{1,0:T(8,128)(2,1)S(1)}, u32[]{:S(2)}, u32[]{:S(2)}) %collective-permute-start.5) | collective-permute-done | bytes 65568 | tf_op jit(solution)/shard_map/ppermute | solution.py:197
  22.0 0.9 %collective-permute-done.4.refs_1_ = bf16[32,1024]{1,0:T(8,128)(2,1)S(1)} collective-permute-done((bf16[32,1024]{1,0:T(8,128)(2,1)S(1)}, bf16[32,1024]{1,0:T(8,128)(2,1)S(1)}, u32[]{:S(2)}, u32[]{:S(2)}) %collective-permute-start.4) | collective-permute-done | bytes 65568 | tf_op jit(solution)/shard_map/ppermute | solution.py:197
  22.9 0.2 collective-permute-done.3.refs_0_
  23.1 0.0 copy-done.2
  23.1 0.4 shard_map.88
  23.5 2.5 %collective-permute-start.6 = (bf16[128,512]{1,0:T(8,128)(2,1)S(1)}, bf16[128,512]{1,0:T(8,128)(2,1)S(1)}, u32[]{:S(2)}, u32[]{:S(2)}) collective-permute-start(bf16[128,512]{1,0:T(8,128)(2,1)S(1)} %get-tuple-element.33), channel_id=1, source_target_pairs={{0,24},{4,28},{8,16},{12,20},{16,8},{20,12},{24,0},{28,4},{1,25},{... | collective-permute-start | bytes 393224 | tf_op jit(solution)/shard_map/ppermute | solution.py:197
  26.0 0.5 %collective-permute-start.8 = (bf16[128,512]{1,0:T(8,128)(2,1)S(1)}, bf16[128,512]{1,0:T(8,128)(2,1)S(1)}, u32[]{:S(2)}, u32[]{:S(2)}) collective-permute-start(bf16[128,512]{1,0:T(8,128)(2,1)S(1)} %get-tuple-element.33), channel_id=1, source_target_pairs={{0,8},{4,12},{8,0},{12,4},{16,24},{20,28},{24,16},{28,20},{1,9},{5... | collective-permute-start | bytes 393224 | tf_op jit(solution)/shard_map/ppermute | solution.py:197
  26.5 0.5 %collective-permute-start.7 = (bf16[128,512]{1,0:T(8,128)(2,1)S(1)}, bf16[128,512]{1,0:T(8,128)(2,1)S(1)}, u32[]{:S(2)}, u32[]{:S(2)}) collective-permute-start(bf16[128,512]{1,0:T(8,128)(2,1)S(1)} %get-tuple-element.33), channel_id=1, source_target_pairs={{0,16},{4,20},{8,24},{12,28},{16,0},{20,4},{24,8},{28,12},{1,17},{... | collective-permute-start | bytes 393224 | tf_op jit(solution)/shard_map/ppermute | solution.py:197
  27.1 0.0 copy-done
  27.1 0.0 copy-done.1
  27.1 0.0 copy-start.3
  27.1 0.8 %shard_map.89 = (f32[128,1024]{1,0:T(8,128)S(1)}, bf16[128,512]{1,0:T(8,128)(2,1)S(1)}) custom-call(bf16[1024,1024]{1,0:T(8,128)(2,1)S(1)} %copy-done, bf16[1024,1024]{1,0:T(8,128)(2,1)S(1)} %copy-done.1, bf16[32,1024]{1,0:T(8,128)(2,1)S(1)} %collective-permute-done.3.refs_0_, ...), custom_call_target="tpu_custom_call", output_to_operand_aliasing={{1}: (6, {})} | custom-call | flops 536870912 | bytes 5242880 | tf_op jit(solution)/shard_map/pallas_call | solution.py:184
  27.9 0.1 collective-permute-start.9
  28.0 1.4 %collective-permute-done.6.refs_1_ = bf16[128,512]{1,0:T(8,128)(2,1)S(1)} collective-permute-done((bf16[128,512]{1,0:T(8,128)(2,1)S(1)}, bf16[128,512]{1,0:T(8,128)(2,1)S(1)}, u32[]{:S(2)}, u32[]{:S(2)}) %collective-permute-start.6) | collective-permute-done | bytes 131104 | tf_op jit(solution)/shard_map/ppermute | solution.py:197
  29.5 0.0 collective-permute-start.10
  29.5 1.5 %collective-permute-done.8.refs_3_ = bf16[128,512]{1,0:T(8,128)(2,1)S(1)} collective-permute-done((bf16[128,512]{1,0:T(8,128)(2,1)S(1)}, bf16[128,512]{1,0:T(8,128)(2,1)S(1)}, u32[]{:S(2)}, u32[]{:S(2)}) %collective-permute-start.8) | collective-permute-done | bytes 131104 | tf_op jit(solution)/shard_map/ppermute | solution.py:197
  31.0 0.0 collective-permute-start.12
  31.0 0.5 %collective-permute-done.7.refs_2_ = bf16[128,512]{1,0:T(8,128)(2,1)S(1)} collective-permute-done((bf16[128,512]{1,0:T(8,128)(2,1)S(1)}, bf16[128,512]{1,0:T(8,128)(2,1)S(1)}, u32[]{:S(2)}, u32[]{:S(2)}) %collective-permute-start.7) | collective-permute-done | bytes 131104 | tf_op jit(solution)/shard_map/ppermute | solution.py:197
  31.5 0.0 collective-permute-start.11
  31.5 0.0 collective-permute-done.9.refs_4_
  31.5 0.0 collective-permute-done.10.refs_5_
  31.5 1.0 %shard_map.90 = (f32[128,256]{1,0:T(8,128)S(1)}, f32[128,256]{1,0:T(8,128)S(1)}, f32[128,256]{1,0:T(8,128)S(1)}) custom-call(bf16[128,256]{1,0:T(8,128)(2,1)S(1)} %get-tuple-element.29.q_ref, bf16[128,512]{1,0:T(8,128)(2,1)S(1)} %get-tuple-element.32.refs_0_, bf16[128,512]{1,0:T(8,128)(2,1)S(1)} %collective-permute-done.6.refs_1_, ...), custom_call_target="tpu_custom_call" | custom-call | flops 402653184 | bytes 1245184 | tf_op jit(solution)/shard_map/pallas_call | solution.py:184
  32.5 0.0 collective-permute-done.12.refs_1_
  32.5 0.3 collective-permute-done.11.refs_0_
  32.9 0.0 copy-done.3
  32.9 0.7 %shard_map.91 = (bf16[32,1024]{1,0:T(8,128)(2,1)S(1)}, bf16[32,1024]{1,0:T(8,128)(2,1)S(1)}, bf16[32,1024]{1,0:T(8,128)(2,1)S(1)}, bf16[32,1024]{1,0:T(8,128)(2,1)S(1)}) custom-call(bf16[128,256]{1,0:T(8,128)(2,1)S(1)} %get-tuple-element.29.q_ref, f32[128,1024]{1,0:T(8,128)S(1)} %get-tuple-element.31.ffn_ref, bf16[256,1024]{1,0:T(8,128)(2,1)S(1)} %copy-done.3, ...), custom_call_target="tpu_custom_call" | custom-call | flops 134217728 | bytes 2031616 | tf_op jit(solution)/shard_map/pallas_call | solution.py:184
  33.6 1.4 %collective-permute-start.13 = (bf16[32,1024]{1,0:T(8,128)(2,1)S(1)}, bf16[32,1024]{1,0:T(8,128)(2,1)S(1)}, u32[]{:S(2)}, u32[]{:S(2)}) collective-permute-start(bf16[32,1024]{1,0:T(8,128)(2,1)S(1)} %get-tuple-element.37), channel_id=1, source_target_pairs={{0,2},{1,3},{2,0},{3,1},{4,6},{5,7},{6,4},{7,5},{8,10},{9,11},{10,... | collective-permute-start | bytes 196616 | tf_op jit(solution)/shard_map/ppermute | solution.py:197
  35.0 1.5 %collective-permute-start.14 = (bf16[32,1024]{1,0:T(8,128)(2,1)S(1)}, bf16[32,1024]{1,0:T(8,128)(2,1)S(1)}, u32[]{:S(2)}, u32[]{:S(2)}) collective-permute-start(bf16[32,1024]{1,0:T(8,128)(2,1)S(1)} %get-tuple-element.38), channel_id=1, source_target_pairs={{0,1},{1,0},{2,3},{3,2},{4,5},{5,4},{6,7},{7,6},{8,9},{9,8},{10,11... | collective-permute-start | bytes 196616 | tf_op jit(solution)/shard_map/ppermute | solution.py:197
  36.5 1.6 %collective-permute-start.15 = (bf16[32,1024]{1,0:T(8,128)(2,1)S(1)}, bf16[32,1024]{1,0:T(8,128)(2,1)S(1)}, u32[]{:S(2)}, u32[]{:S(2)}) collective-permute-start(bf16[32,1024]{1,0:T(8,128)(2,1)S(1)} %get-tuple-element.39), channel_id=1, source_target_pairs={{0,3},{1,2},{2,1},{3,0},{4,7},{5,6},{6,5},{7,4},{8,11},{9,10},{10,... | collective-permute-start | bytes 196616 | tf_op jit(solution)/shard_map/ppermute | solution.py:197
  38.0 2.8 %collective-permute-done.13.refs_1_ = bf16[32,1024]{1,0:T(8,128)(2,1)S(1)} collective-permute-done((bf16[32,1024]{1,0:T(8,128)(2,1)S(1)}, bf16[32,1024]{1,0:T(8,128)(2,1)S(1)}, u32[]{:S(2)}, u32[]{:S(2)}) %collective-permute-start.13) | collective-permute-done | bytes 65568 | tf_op jit(solution)/shard_map/ppermute | solution.py:197
  40.8 0.0 collective-permute-done.14.refs_2_
  40.8 1.7 %collective-permute-done.15.refs_3_ = bf16[32,1024]{1,0:T(8,128)(2,1)S(1)} collective-permute-done((bf16[32,1024]{1,0:T(8,128)(2,1)S(1)}, bf16[32,1024]{1,0:T(8,128)(2,1)S(1)}, u32[]{:S(2)}, u32[]{:S(2)}) %collective-permute-start.15) | collective-permute-done | bytes 65568 | tf_op jit(solution)/shard_map/ppermute | solution.py:197
  42.6 0.7 %shard_map.92 = bf16[32,1024]{1,0:T(8,128)(2,1)} custom-call(bf16[32,1024]{1,0:T(8,128)(2,1)S(1)} %get-tuple-element.27.refs_0_, bf16[32,1024]{1,0:T(8,128)(2,1)S(1)} %collective-permute-done.13.refs_1_, bf16[32,1024]{1,0:T(8,128)(2,1)S(1)} %collective-permute-done.14.refs_2_, bf16[32,1024]{1,0:T(8,128)(2,1)S(1)} %collective-permute-done.15.refs_3_, ...), custom_call_target="tpu_custom_call" | custom-call | bytes 393216 | tf_op jit(solution)/shard_map/pallas_call | solution.py:184
  (1 shorter events, 0.0 us)
Async XLA Ops:
  2.5 7.8 %collective-permute-start = (bf16[32,1152]{1,0:T(8,128)(2,1)S(1)}, bf16[32,1152]{1,0:T(8,128)(2,1)S(1)}, u32[]{:S(2)}, u32[]{:S(2)}) collective-permute-start(bf16[32,1152]{1,0:T(8,128)(2,1)S(1)} %shard_map.83), channel_id=1, source_target_pairs={{0,3},{1,2},{2,1},{3,0},{4,7},{5,6},{6,5},{7,4},{8,11},{9,10},{10,... | collective-permute-start | bytes 221192 | tf_op jit(solution)/shard_map/ppermute | solution.py:197
  8.1 1.2 %copy-start.4 = (bf16[1024]{0:T(1024)(128)(2,1)S(1)}, bf16[1024]{0:T(1024)(128)(2,1)}, u32[]{:S(2)}) copy-start(bf16[1024]{0:T(1024)(128)(2,1)} %param.15) | copy-start | bytes 6148
  8.1 5.8 %collective-permute-start.1 = (bf16[32,1152]{1,0:T(8,128)(2,1)S(1)}, bf16[32,1152]{1,0:T(8,128)(2,1)S(1)}, u32[]{:S(2)}, u32[]{:S(2)}) collective-permute-start(bf16[32,1152]{1,0:T(8,128)(2,1)S(1)} %shard_map.84), channel_id=1, source_target_pairs={{0,2},{1,3},{2,0},{3,1},{4,6},{5,7},{6,4},{7,5},{8,10},{9,11},{10,... | collective-permute-start | bytes 221192 | tf_op jit(solution)/shard_map/ppermute | solution.py:197
  8.2 14.9 %copy-start.2 = (bf16[1024,3,256]{2,0,1:T(8,128)(2,1)S(1)}, bf16[1024,3,256]{2,0,1:T(8,128)(2,1)}, u32[]{:S(2)}) copy-start(bf16[1024,3,256]{2,0,1:T(8,128)(2,1)} %param.11) | copy-start | bytes 4718596
  8.7 5.7 %collective-permute-start.2 = (bf16[32,1152]{1,0:T(8,128)(2,1)S(1)}, bf16[32,1152]{1,0:T(8,128)(2,1)S(1)}, u32[]{:S(2)}, u32[]{:S(2)}) collective-permute-start(bf16[32,1152]{1,0:T(8,128)(2,1)S(1)} %shard_map.85), channel_id=1, source_target_pairs={{0,1},{1,0},{2,3},{3,2},{4,5},{5,4},{6,7},{7,6},{8,9},{9,8},{10,11... | collective-permute-start | bytes 221192 | tf_op jit(solution)/shard_map/ppermute | solution.py:197
  9.3 17.7 %copy-start = (bf16[1024,1024]{1,0:T(8,128)(2,1)S(1)}, bf16[1024,1024]{1,0:T(8,128)(2,1)}, u32[]{:S(2)}) copy-start(bf16[1024,1024]{1,0:T(8,128)(2,1)} %up_ref.1) | copy-start | bytes 6291460
  9.3 17.7 %copy-start.1 = (bf16[1024,1024]{1,0:T(8,128)(2,1)S(1)}, bf16[1024,1024]{1,0:T(8,128)(2,1)}, u32[]{:S(2)}) copy-start(bf16[1024,1024]{1,0:T(8,128)(2,1)} %down_ref.1) | copy-start | bytes 6291460
  15.0 7.0 %collective-permute-start.5 = (bf16[32,1024]{1,0:T(8,128)(2,1)S(1)}, bf16[32,1024]{1,0:T(8,128)(2,1)S(1)}, u32[]{:S(2)}, u32[]{:S(2)}) collective-permute-start(bf16[32,1024]{1,0:T(8,128)(2,1)S(1)} %get-tuple-element.28.refs_3_), channel_id=1, source_target_pairs={{0,2},{1,3},{2,0},{3,1},{4,6},{5,7},{6,4},{7,5},{8,10},{9,11},{10,... | collective-permute-start | bytes 196616 | tf_op jit(solution)/shard_map/ppermute | solution.py:197
  16.7 6.2 %collective-permute-start.4 = (bf16[32,1024]{1,0:T(8,128)(2,1)S(1)}, bf16[32,1024]{1,0:T(8,128)(2,1)S(1)}, u32[]{:S(2)}, u32[]{:S(2)}) collective-permute-start(bf16[32,1024]{1,0:T(8,128)(2,1)S(1)} %get-tuple-element.28.refs_3_), channel_id=1, source_target_pairs={{0,3},{1,2},{2,1},{3,0},{4,7},{5,6},{6,5},{7,4},{8,11},{9,10},{10,... | collective-permute-start | bytes 196616 | tf_op jit(solution)/shard_map/ppermute | solution.py:197
  17.8 5.3 %collective-permute-start.3 = (bf16[32,1024]{1,0:T(8,128)(2,1)S(1)}, bf16[32,1024]{1,0:T(8,128)(2,1)S(1)}, u32[]{:S(2)}, u32[]{:S(2)}) collective-permute-start(bf16[32,1024]{1,0:T(8,128)(2,1)S(1)} %get-tuple-element.28.refs_3_), channel_id=1, source_target_pairs={{0,1},{1,0},{2,3},{3,2},{4,5},{5,4},{6,7},{7,6},{8,9},{9,8},{10,11... | collective-permute-start | bytes 196616 | tf_op jit(solution)/shard_map/ppermute | solution.py:197
  23.5 5.9 %collective-permute-start.6 = (bf16[128,512]{1,0:T(8,128)(2,1)S(1)}, bf16[128,512]{1,0:T(8,128)(2,1)S(1)}, u32[]{:S(2)}, u32[]{:S(2)}) collective-permute-start(bf16[128,512]{1,0:T(8,128)(2,1)S(1)} %get-tuple-element.33), channel_id=1, source_target_pairs={{0,24},{4,28},{8,16},{12,20},{16,8},{20,12},{24,0},{28,4},{1,25},{... | collective-permute-start | bytes 393224 | tf_op jit(solution)/shard_map/ppermute | solution.py:197
  26.0 5.0 %collective-permute-start.8 = (bf16[128,512]{1,0:T(8,128)(2,1)S(1)}, bf16[128,512]{1,0:T(8,128)(2,1)S(1)}, u32[]{:S(2)}, u32[]{:S(2)}) collective-permute-start(bf16[128,512]{1,0:T(8,128)(2,1)S(1)} %get-tuple-element.33), channel_id=1, source_target_pairs={{0,8},{4,12},{8,0},{12,4},{16,24},{20,28},{24,16},{28,20},{1,9},{5... | collective-permute-start | bytes 393224 | tf_op jit(solution)/shard_map/ppermute | solution.py:197
  26.5 5.0 %collective-permute-start.7 = (bf16[128,512]{1,0:T(8,128)(2,1)S(1)}, bf16[128,512]{1,0:T(8,128)(2,1)S(1)}, u32[]{:S(2)}, u32[]{:S(2)}) collective-permute-start(bf16[128,512]{1,0:T(8,128)(2,1)S(1)} %get-tuple-element.33), channel_id=1, source_target_pairs={{0,16},{4,20},{8,24},{12,28},{16,0},{20,4},{24,8},{28,12},{1,17},{... | collective-permute-start | bytes 393224 | tf_op jit(solution)/shard_map/ppermute | solution.py:197
  27.1 5.8 %copy-start.3 = (bf16[256,1024]{1,0:T(8,128)(2,1)S(1)}, bf16[256,1024]{1,0:T(8,128)(2,1)}, u32[]{:S(2)}) copy-start(bf16[256,1024]{1,0:T(8,128)(2,1)} %wo_ref.1) | copy-start | bytes 1572868
  27.9 3.6 %collective-permute-start.9 = (bf16[128,512]{1,0:T(8,128)(2,1)S(1)}, bf16[128,512]{1,0:T(8,128)(2,1)S(1)}, u32[]{:S(2)}, u32[]{:S(2)}) collective-permute-start(bf16[128,512]{1,0:T(8,128)(2,1)S(1)} %get-tuple-element.32.refs_0_), channel_id=1, source_target_pairs={{0,4},{4,0},{8,12},{12,8},{16,20},{20,16},{24,28},{28,24},{1,5},{5... | collective-permute-start | bytes 393224 | tf_op jit(solution)/shard_map/ppermute | solution.py:197
  29.5 2.1 %collective-permute-start.10 = (bf16[128,512]{1,0:T(8,128)(2,1)S(1)}, bf16[128,512]{1,0:T(8,128)(2,1)S(1)}, u32[]{:S(2)}, u32[]{:S(2)}) collective-permute-start(bf16[128,512]{1,0:T(8,128)(2,1)S(1)} %collective-permute-done.6.refs_1_), channel_id=1, source_target_pairs={{0,4},{4,0},{8,12},{12,8},{16,20},{20,16},{24,28},{28,24},{1,5},{5... | collective-permute-start | bytes 393224 | tf_op jit(solution)/shard_map/ppermute | solution.py:197
  31.0 1.5 %collective-permute-start.12 = (bf16[128,512]{1,0:T(8,128)(2,1)S(1)}, bf16[128,512]{1,0:T(8,128)(2,1)S(1)}, u32[]{:S(2)}, u32[]{:S(2)}) collective-permute-start(bf16[128,512]{1,0:T(8,128)(2,1)S(1)} %collective-permute-done.8.refs_3_), channel_id=1, source_target_pairs={{0,4},{4,0},{8,12},{12,8},{16,20},{20,16},{24,28},{28,24},{1,5},{5... | collective-permute-start | bytes 393224 | tf_op jit(solution)/shard_map/ppermute | solution.py:197
  31.5 1.3 %collective-permute-start.11 = (bf16[128,512]{1,0:T(8,128)(2,1)S(1)}, bf16[128,512]{1,0:T(8,128)(2,1)S(1)}, u32[]{:S(2)}, u32[]{:S(2)}) collective-permute-start(bf16[128,512]{1,0:T(8,128)(2,1)S(1)} %collective-permute-done.7.refs_2_), channel_id=1, source_target_pairs={{0,4},{4,0},{8,12},{12,8},{16,20},{20,16},{24,28},{28,24},{1,5},{5... | collective-permute-start | bytes 393224 | tf_op jit(solution)/shard_map/ppermute | solution.py:197
  33.6 7.3 %collective-permute-start.13 = (bf16[32,1024]{1,0:T(8,128)(2,1)S(1)}, bf16[32,1024]{1,0:T(8,128)(2,1)S(1)}, u32[]{:S(2)}, u32[]{:S(2)}) collective-permute-start(bf16[32,1024]{1,0:T(8,128)(2,1)S(1)} %get-tuple-element.37), channel_id=1, source_target_pairs={{0,2},{1,3},{2,0},{3,1},{4,6},{5,7},{6,4},{7,5},{8,10},{9,11},{10,... | collective-permute-start | bytes 196616 | tf_op jit(solution)/shard_map/ppermute | solution.py:197
  35.0 5.9 %collective-permute-start.14 = (bf16[32,1024]{1,0:T(8,128)(2,1)S(1)}, bf16[32,1024]{1,0:T(8,128)(2,1)S(1)}, u32[]{:S(2)}, u32[]{:S(2)}) collective-permute-start(bf16[32,1024]{1,0:T(8,128)(2,1)S(1)} %get-tuple-element.38), channel_id=1, source_target_pairs={{0,1},{1,0},{2,3},{3,2},{4,5},{5,4},{6,7},{7,6},{8,9},{9,8},{10,11... | collective-permute-start | bytes 196616 | tf_op jit(solution)/shard_map/ppermute | solution.py:197
  36.5 6.1 %collective-permute-start.15 = (bf16[32,1024]{1,0:T(8,128)(2,1)S(1)}, bf16[32,1024]{1,0:T(8,128)(2,1)S(1)}, u32[]{:S(2)}, u32[]{:S(2)}) collective-permute-start(bf16[32,1024]{1,0:T(8,128)(2,1)S(1)} %get-tuple-element.39), channel_id=1, source_target_pairs={{0,3},{1,2},{2,1},{3,0},{4,7},{5,6},{6,5},{7,4},{8,11},{9,10},{10,... | collective-permute-start | bytes 196616 | tf_op jit(solution)/shard_map/ppermute | solution.py:197

commit v6 on v5

--- a/solution.py
+++ b/solution.py
@@ -100,19 +100,19 @@
     normed_ref[...] = (centered * lax.rsqrt(spread + EPS) * gain_ref[...].astype(f32)).astype(bf16)
 
 
-def qkv_kernel(w_ref, *refs):
-    blocks, (q_ref, kv_ref, kept_ref) = refs[:-3], refs[-3:]
+def key_value_kernel(w_ref, *refs):
+    blocks, kv_ref = refs[:-1], refs[-1]
     x = rows_of(blocks)
-    width = q_ref.shape[1]
-    q_ref[...] = jnp.dot(x, w_ref[0], preferred_element_type=f32).astype(bf16)
+    width = w_ref.shape[2]
     kv_ref[:, :width] = jnp.dot(x, w_ref[1], preferred_element_type=f32).astype(bf16)
     kv_ref[:, width:] = jnp.dot(x, w_ref[2], preferred_element_type=f32).astype(bf16)
+
+
+def ffn_kernel(up_ref, down_ref, w_ref, kv_ref, *refs):
+    blocks, (out_ref, q_ref, kept_ref) = refs[:-3], refs[-3:]
     kept_ref[...] = kv_ref[...]
-
-
-def ffn_kernel(up_ref, down_ref, *refs):
-    blocks, out_ref = refs[:-3], refs[-2]
     x = rows_of(blocks)
+    q_ref[...] = jnp.dot(x, w_ref[0], preferred_element_type=f32).astype(bf16)
     hidden = jnp.dot(x, up_ref[...], preferred_element_type=f32)
     hidden = jax.nn.gelu(hidden, approximate=True).astype(bf16)
     out_ref[...] = jnp.dot(hidden, down_ref[...], preferred_element_type=f32)
@@ -249,24 +249,18 @@
         norm_kernel, [shape((part, width), bf16)] * 2, norm_gain.reshape(1, width), *got, sent[-1]
     )
     blocks = [*exchange([normed] * groups, "var", groups, partners[1]), normed]
-    q, kv, kept = call(
-        qkv_kernel,
-        [shape((rows, local), bf16)] + [shape((rows, 2 * local), bf16)] * 2,
-        qkv_weight.transpose(1, 0, 2), *blocks,
-        flops=6 * rows * width * local,
-    )
-    ffn = []
-
-    def feed_forward(arrived):
-        made = call(
-            ffn_kernel, [shape((rows, width), f32), shape(arrived.shape, bf16)],
-            up_weight, down_weight, *blocks, arrived,
-            flops=4 * rows * width * up_weight.shape[1], aliases={2 + len(blocks): 1},
-        )
-        ffn.append(made[0])
-        return made[1]
-
-    early, late = gather_space(kv, feed_forward(kept), spaces)
+    weights = qkv_weight.transpose(1, 0, 2)
+    (kv,) = call(
+        key_value_kernel, [shape((rows, 2 * local), bf16)], weights, *blocks,
+        flops=4 * rows * width * local,
+    )
+    ffn, q, kept = call(
+        ffn_kernel,
+        [shape((rows, width), f32), shape((rows, local), bf16), shape(kv.shape, bf16)],
+        up_weight, down_weight, weights, kv, *blocks,
+        flops=2 * rows * width * (2 * up_weight.shape[1] + local),
+    )
+    early, late = gather_space(kv, kept, spaces)
     heads = H // groups
     state = call(
         functools.partial(early_kernel, heads), [shape((rows, local), f32)] * 3, q, *early,
@@ -275,7 +269,7 @@
     sums = call(
         functools.partial(attend_kernel, heads, groups),
         [shape((part, width), bf16)] * groups,
-        q, *ffn, out_weight, *state, *late,
+        q, ffn, out_weight, *state, *late,
         flops=4 * rows * rows * len(late) * local * heads, vmem=32,
     )
     by_partner = dict(zip([*partners[1], 0], sums))

time: 43.4 us -> 43.3 us (level)
  no operation moved by 1% of the time
where the time goes in v6:
time: 43.3 us; the launch traced here: 43.2 us
  waiting for transfers between devices  17.5 us (40%)
  starting transfers between devices  17.4 us (40%)
  Pallas kernels  8.14 us (19%)
    ppermute x16, waiting for transfers between devices, exchange(): lax.ppermute(parts[k], axis, [(i, i ^ k) for i in range(size)])  17.5 us
    ppermute x16, starting transfers between devices, exchange(): lax.ppermute(parts[k], axis, [(i, i ^ k) for i in range(size)])  17.4 us
    pallas_call x11, Pallas kernels, call(): pl.pallas_call(kernel, out_shape=out_shapes, in_specs=in_specs, out_specs...  8.14 us
  transfers between devices with their start and end apart: 16, of which 12 were waited for; matrix products, arithmetic and copies ran while one was open for 0% of the time, Pallas kernels for 8%

profile of v6, /device:TPU:0, one launch (start us, length us, event | category | flops | bytes accessed | tf_op | source)
XLA Modules:
  0.0 43.2 jit_solution(7735848959256134222)
XLA Ops:
  0.0 2.0 %shard_map.82 = (bf16[4,4,32,1024]{3,2,1,0:T(8,128)(2,1)S(1)}, bf16[1024,1024]{1,0:T(8,128)(2,1)S(1)}, bf16[4,4,32,128]{3,2,1,0:T(8,128)(2,1)S(1)}, bf16[4,32,128]{2,1,0:T(8,128)(2,1)S(1)}) custom-call(bf16[4,4,32,1024]{3,2,1,0:T(8,128)(2,1)} %bitcast.5, bf16[16,1024]{1,0:T(8,128)(2,1)} %bitcast.6, bf16[1024,1024]{1,0:T(8,128)(2,1)} %wv_hbm.1), custom_call_target="tpu_custom_call" | custom-call | flops 134217728 | bytes 6488064 | tf_op jit(solution)/shard_map/pallas_call | solution.py:184
  2.0 0.5 %shard_map.83 = bf16[32,1152]{1,0:T(8,128)(2,1)S(1)} custom-call(bf16[4,4,32,1024]{3,2,1,0:T(8,128)(2,1)S(1)} %get-tuple-element.21.x_ref, bf16[1024,1024]{1,0:T(8,128)(2,1)S(1)} %get-tuple-element.22.wv_ref, bf16[4,4,32,128]{3,2,1,0:T(8,128)(2,1)S(1)} %get-tuple-element.23.share_ref, bf16[4,32,128]{2,1,0:T(8,128)(2,1)S(1)} %get-tuple-element.24.stats_ref), custom_call_target="tpu_custom_call" | custom-call | flops 268435456 | bytes 3383296 | tf_op jit(solution)/shard_map/pallas_call | solution.py:184
  2.5 5.1 %collective-permute-start = (bf16[32,1152]{1,0:T(8,128)(2,1)S(1)}, bf16[32,1152]{1,0:T(8,128)(2,1)S(1)}, u32[]{:S(2)}, u32[]{:S(2)}) collective-permute-start(bf16[32,1152]{1,0:T(8,128)(2,1)S(1)} %shard_map.83), channel_id=1, source_target_pairs={{0,3},{1,2},{2,1},{3,0},{4,7},{5,6},{6,5},{7,4},{8,11},{9,10},{10,... | collective-permute-start | bytes 221192 | tf_op jit(solution)/shard_map/ppermute | solution.py:197
  7.6 0.5 %shard_map.84 = bf16[32,1152]{1,0:T(8,128)(2,1)S(1)} custom-call(bf16[4,4,32,1024]{3,2,1,0:T(8,128)(2,1)S(1)} %get-tuple-element.21.x_ref, bf16[1024,1024]{1,0:T(8,128)(2,1)S(1)} %get-tuple-element.22.wv_ref, bf16[4,4,32,128]{3,2,1,0:T(8,128)(2,1)S(1)} %get-tuple-element.23.share_ref, bf16[4,32,128]{2,1,0:T(8,128)(2,1)S(1)} %get-tuple-element.24.stats_ref), custom_call_target="tpu_custom_call" | custom-call | flops 268435456 | bytes 3383296 | tf_op jit(solution)/shard_map/pallas_call | solution.py:184
  8.1 0.0 copy-start.4
  8.1 0.1 collective-permute-start.1
  8.2 0.0 copy-start.2
  8.2 0.5 %shard_map.85 = bf16[32,1152]{1,0:T(8,128)(2,1)S(1)} custom-call(bf16[4,4,32,1024]{3,2,1,0:T(8,128)(2,1)S(1)} %get-tuple-element.21.x_ref, bf16[1024,1024]{1,0:T(8,128)(2,1)S(1)} %get-tuple-element.22.wv_ref, bf16[4,4,32,128]{3,2,1,0:T(8,128)(2,1)S(1)} %get-tuple-element.23.share_ref, bf16[4,32,128]{2,1,0:T(8,128)(2,1)S(1)} %get-tuple-element.24.stats_ref), custom_call_target="tpu_custom_call" | custom-call | flops 268435456 | bytes 3383296 | tf_op jit(solution)/shard_map/pallas_call | solution.py:184
  8.7 0.0 copy-start
  8.7 0.6 %collective-permute-start.2 = (bf16[32,1152]{1,0:T(8,128)(2,1)S(1)}, bf16[32,1152]{1,0:T(8,128)(2,1)S(1)}, u32[]{:S(2)}, u32[]{:S(2)}) collective-permute-start(bf16[32,1152]{1,0:T(8,128)(2,1)S(1)} %shard_map.85), channel_id=1, source_target_pairs={{0,1},{1,0},{2,3},{3,2},{4,5},{5,4},{6,7},{7,6},{8,9},{9,8},{10,11... | collective-permute-start | bytes 221192 | tf_op jit(solution)/shard_map/ppermute | solution.py:197
  9.3 0.0 copy-done.4
  9.4 0.0 copy-start.1
  9.4 0.5 %shard_map.86.refs_3_ = bf16[32,1152]{1,0:T(8,128)(2,1)S(1)} custom-call(bf16[4,4,32,1024]{3,2,1,0:T(8,128)(2,1)S(1)} %get-tuple-element.21.x_ref, bf16[1024,1024]{1,0:T(8,128)(2,1)S(1)} %get-tuple-element.22.wv_ref, bf16[4,4,32,128]{3,2,1,0:T(8,128)(2,1)S(1)} %get-tuple-element.23.share_ref, bf16[4,32,128]{2,1,0:T(8,128)(2,1)S(1)} %get-tuple-element.24.stats_ref), custom_call_target="tpu_custom_call" | custom-call | flops 268435456 | bytes 3383296 | tf_op jit(solution)/shard_map/pallas_call | solution.py:184
  9.8 0.4 %collective-permute-done.refs_0_ = bf16[32,1152]{1,0:T(8,128)(2,1)S(1)} collective-permute-done((bf16[32,1152]{1,0:T(8,128)(2,1)S(1)}, bf16[32,1152]{1,0:T(8,128)(2,1)S(1)}, u32[]{:S(2)}, u32[]{:S(2)}) %collective-permute-start) | collective-permute-done | bytes 73760 | tf_op jit(solution)/shard_map/ppermute | solution.py:197
  10.3 3.7 %collective-permute-done.1.refs_1_ = bf16[32,1152]{1,0:T(8,128)(2,1)S(1)} collective-permute-done((bf16[32,1152]{1,0:T(8,128)(2,1)S(1)}, bf16[32,1152]{1,0:T(8,128)(2,1)S(1)}, u32[]{:S(2)}, u32[]{:S(2)}) %collective-permute-start.1) | collective-permute-done | bytes 73760 | tf_op jit(solution)/shard_map/ppermute | solution.py:197
  14.0 0.5 %collective-permute-done.2.refs_2_ = bf16[32,1152]{1,0:T(8,128)(2,1)S(1)} collective-permute-done((bf16[32,1152]{1,0:T(8,128)(2,1)S(1)}, bf16[32,1152]{1,0:T(8,128)(2,1)S(1)}, u32[]{:S(2)}, u32[]{:S(2)}) %collective-permute-start.2) | collective-permute-done | bytes 73760 | tf_op jit(solution)/shard_map/ppermute | solution.py:197
  14.5 0.6 %shard_map.87 = (bf16[32,1024]{1,0:T(8,128)(2,1)S(1)}, bf16[32,1024]{1,0:T(8,128)(2,1)S(1)}) custom-call(bf16[1,1024]{1,0:T(2,128)(2,1)S(1)} %reshape.6.gain_ref, bf16[32,1152]{1,0:T(8,128)(2,1)S(1)} %collective-permute-done.refs_0_, bf16[32,1152]{1,0:T(8,128)(2,1)S(1)} %collective-permute-done.1.refs_1_, ...), custom_call_target="tpu_custom_call" | custom-call | bytes 428032 | tf_op jit(solution)/shard_map/pallas_call | solution.py:184
  15.0 1.6 %collective-permute-start.5 = (bf16[32,1024]{1,0:T(8,128)(2,1)S(1)}, bf16[32,1024]{1,0:T(8,128)(2,1)S(1)}, u32[]{:S(2)}, u32[]{:S(2)}) collective-permute-start(bf16[32,1024]{1,0:T(8,128)(2,1)S(1)} %get-tuple-element.26.refs_3_), channel_id=1, source_target_pairs={{0,2},{1,3},{2,0},{3,1},{4,6},{5,7},{6,4},{7,5},{8,10},{9,11},{10,... | collective-permute-start | bytes 196616 | tf_op jit(solution)/shard_map/ppermute | solution.py:197
  16.7 1.1 %collective-permute-start.4 = (bf16[32,1024]{1,0:T(8,128)(2,1)S(1)}, bf16[32,1024]{1,0:T(8,128)(2,1)S(1)}, u32[]{:S(2)}, u32[]{:S(2)}) collective-permute-start(bf16[32,1024]{1,0:T(8,128)(2,1)S(1)} %get-tuple-element.26.refs_3_), channel_id=1, source_target_pairs={{0,3},{1,2},{2,1},{3,0},{4,7},{5,6},{6,5},{7,4},{8,11},{9,10},{10,... | collective-permute-start | bytes 196616 | tf_op jit(solution)/shard_map/ppermute | solution.py:197
  17.8 0.8 %collective-permute-start.3 = (bf16[32,1024]{1,0:T(8,128)(2,1)S(1)}, bf16[32,1024]{1,0:T(8,128)(2,1)S(1)}, u32[]{:S(2)}, u32[]{:S(2)}) collective-permute-start(bf16[32,1024]{1,0:T(8,128)(2,1)S(1)} %get-tuple-element.26.refs_3_), channel_id=1, source_target_pairs={{0,1},{1,0},{2,3},{3,2},{4,5},{5,4},{6,7},{7,6},{8,9},{9,8},{10,11... | collective-permute-start | bytes 196616 | tf_op jit(solution)/shard_map/ppermute | solution.py:197
  18.6 3.4 %collective-permute-done.5.refs_2_ = bf16[32,1024]{1,0:T(8,128)(2,1)S(1)} collective-permute-done((bf16[32,1024]{1,0:T(8,128)(2,1)S(1)}, bf16[32,1024]{1,0:T(8,128)(2,1)S(1)}, u32[]{:S(2)}, u32[]{:S(2)}) %collective-permute-start.5) | collective-permute-done | bytes 65568 | tf_op jit(solution)/shard_map/ppermute | solution.py:197
  22.0 0.9 %collective-permute-done.4.refs_1_ = bf16[32,1024]{1,0:T(8,128)(2,1)S(1)} collective-permute-done((bf16[32,1024]{1,0:T(8,128)(2,1)S(1)}, bf16[32,1024]{1,0:T(8,128)(2,1)S(1)}, u32[]{:S(2)}, u32[]{:S(2)}) %collective-permute-start.4) | collective-permute-done | bytes 65568 | tf_op jit(solution)/shard_map/ppermute | solution.py:197
  22.9 0.2 collective-permute-done.3.refs_0_
  23.1 0.0 copy-done
  23.1 0.3 shard_map.88.kv_ref
  23.5 0.0 copy-start.3
  23.5 2.5 %collective-permute-start.6 = (bf16[128,512]{1,0:T(8,128)(2,1)S(1)}, bf16[128,512]{1,0:T(8,128)(2,1)S(1)}, u32[]{:S(2)}, u32[]{:S(2)}) collective-permute-start(bf16[128,512]{1,0:T(8,128)(2,1)S(1)} %shard_map.88.kv_ref), channel_id=1, source_target_pairs={{0,24},{4,28},{8,16},{12,20},{16,8},{20,12},{24,0},{28,4},{1,25},{... | collective-permute-start | bytes 393224 | tf_op jit(solution)/shard_map/ppermute | solution.py:197
  26.0 0.5 %collective-permute-start.8 = (bf16[128,512]{1,0:T(8,128)(2,1)S(1)}, bf16[128,512]{1,0:T(8,128)(2,1)S(1)}, u32[]{:S(2)}, u32[]{:S(2)}) collective-permute-start(bf16[128,512]{1,0:T(8,128)(2,1)S(1)} %shard_map.88.kv_ref), channel_id=1, source_target_pairs={{0,8},{4,12},{8,0},{12,4},{16,24},{20,28},{24,16},{28,20},{1,9},{5... | collective-permute-start | bytes 393224 | tf_op jit(solution)/shard_map/ppermute | solution.py:197
  26.5 0.5 %collective-permute-start.7 = (bf16[128,512]{1,0:T(8,128)(2,1)S(1)}, bf16[128,512]{1,0:T(8,128)(2,1)S(1)}, u32[]{:S(2)}, u32[]{:S(2)}) collective-permute-start(bf16[128,512]{1,0:T(8,128)(2,1)S(1)} %shard_map.88.kv_ref), channel_id=1, source_target_pairs={{0,16},{4,20},{8,24},{12,28},{16,0},{20,4},{24,8},{28,12},{1,17},{... | collective-permute-start | bytes 393224 | tf_op jit(solution)/shard_map/ppermute | solution.py:197
  27.0 0.0 copy-done.2
  27.0 0.0 copy-done.1
  27.0 0.9 %shard_map.89 = (f32[128,1024]{1,0:T(8,128)S(1)}, bf16[128,256]{1,0:T(8,128)(2,1)S(1)}, bf16[128,512]{1,0:T(8,128)(2,1)S(1)}) custom-call(bf16[1024,1024]{1,0:T(8,128)(2,1)S(1)} %copy-done.1, bf16[1024,1024]{1,0:T(8,128)(2,1)S(1)} %copy-done.2, bf16[3,1024,256]{2,1,0:T(8,128)(2,1)S(1)} %bitcast.4, bf16[128,512]{1,0:T(8,128)(2,1)S(1)} %shard_map.88.kv_ref, ...), custom_call_target="tpu_custom_call" | custom-call | flops 603979776 | bytes 6881280 | tf_op jit(solution)/shard_map/pallas_call | solution.py:184
  27.9 0.1 collective-permute-start.9
  28.0 1.4 %collective-permute-done.6.refs_1_ = bf16[128,512]{1,0:T(8,128)(2,1)S(1)} collective-permute-done((bf16[128,512]{1,0:T(8,128)(2,1)S(1)}, bf16[128,512]{1,0:T(8,128)(2,1)S(1)}, u32[]{:S(2)}, u32[]{:S(2)}) %collective-permute-start.6) | collective-permute-done | bytes 131104 | tf_op jit(solution)/shard_map/ppermute | solution.py:197
  29.4 0.0 collective-permute-start.10
  29.4 1.5 %collective-permute-done.8.refs_3_ = bf16[128,512]{1,0:T(8,128)(2,1)S(1)} collective-permute-done((bf16[128,512]{1,0:T(8,128)(2,1)S(1)}, bf16[128,512]{1,0:T(8,128)(2,1)S(1)}, u32[]{:S(2)}, u32[]{:S(2)}) %collective-permute-start.8) | collective-permute-done | bytes 131104 | tf_op jit(solution)/shard_map/ppermute | solution.py:197
  30.9 0.0 collective-permute-start.12
  30.9 0.5 %collective-permute-done.7.refs_2_ = bf16[128,512]{1,0:T(8,128)(2,1)S(1)} collective-permute-done((bf16[128,512]{1,0:T(8,128)(2,1)S(1)}, bf16[128,512]{1,0:T(8,128)(2,1)S(1)}, u32[]{:S(2)}, u32[]{:S(2)}) %collective-permute-start.7) | collective-permute-done | bytes 131104 | tf_op jit(solution)/shard_map/ppermute | solution.py:197
  31.5 0.0 collective-permute-start.11
  31.5 0.0 collective-permute-done.9.refs_4_
  31.5 0.0 collective-permute-done.10.refs_5_
  31.5 1.0 %shard_map.90 = (f32[128,256]{1,0:T(8,128)S(1)}, f32[128,256]{1,0:T(8,128)S(1)}, f32[128,256]{1,0:T(8,128)S(1)}) custom-call(bf16[128,256]{1,0:T(8,128)(2,1)S(1)} %get-tuple-element.27.q_ref, bf16[128,512]{1,0:T(8,128)(2,1)S(1)} %get-tuple-element.29.refs_0_, bf16[128,512]{1,0:T(8,128)(2,1)S(1)} %collective-permute-done.6.refs_1_, ...), custom_call_target="tpu_custom_call" | custom-call | flops 402653184 | bytes 1245184 | tf_op jit(solution)/shard_map/pallas_call | solution.py:184
  32.5 0.0 collective-permute-done.12.refs_1_
  32.5 0.3 collective-permute-done.11.refs_0_
  32.8 0.0 copy-done.3
  32.8 0.7 %shard_map.91 = (bf16[32,1024]{1,0:T(8,128)(2,1)S(1)}, bf16[32,1024]{1,0:T(8,128)(2,1)S(1)}, bf16[32,1024]{1,0:T(8,128)(2,1)S(1)}, bf16[32,1024]{1,0:T(8,128)(2,1)S(1)}) custom-call(bf16[128,256]{1,0:T(8,128)(2,1)S(1)} %get-tuple-element.27.q_ref, f32[128,1024]{1,0:T(8,128)S(1)} %get-tuple-element.28.ffn_ref, bf16[256,1024]{1,0:T(8,128)(2,1)S(1)} %copy-done.3, ...), custom_call_target="tpu_custom_call" | custom-call | flops 134217728 | bytes 2031616 | tf_op jit(solution)/shard_map/pallas_call | solution.py:184
  33.5 1.4 %collective-permute-start.13 = (bf16[32,1024]{1,0:T(8,128)(2,1)S(1)}, bf16[32,1024]{1,0:T(8,128)(2,1)S(1)}, u32[]{:S(2)}, u32[]{:S(2)}) collective-permute-start(bf16[32,1024]{1,0:T(8,128)(2,1)S(1)} %get-tuple-element.33), channel_id=1, source_target_pairs={{0,2},{1,3},{2,0},{3,1},{4,6},{5,7},{6,4},{7,5},{8,10},{9,11},{10,... | collective-permute-start | bytes 196616 | tf_op jit(solution)/shard_map/ppermute | solution.py:197
  34.9 1.5 %collective-permute-start.14 = (bf16[32,1024]{1,0:T(8,128)(2,1)S(1)}, bf16[32,1024]{1,0:T(8,128)(2,1)S(1)}, u32[]{:S(2)}, u32[]{:S(2)}) collective-permute-start(bf16[32,1024]{1,0:T(8,128)(2,1)S(1)} %get-tuple-element.34), channel_id=1, source_target_pairs={{0,1},{1,0},{2,3},{3,2},{4,5},{5,4},{6,7},{7,6},{8,9},{9,8},{10,11... | collective-permute-start | bytes 196616 | tf_op jit(solution)/shard_map/ppermute | solution.py:197
  36.4 1.6 %collective-permute-start.15 = (bf16[32,1024]{1,0:T(8,128)(2,1)S(1)}, bf16[32,1024]{1,0:T(8,128)(2,1)S(1)}, u32[]{:S(2)}, u32[]{:S(2)}) collective-permute-start(bf16[32,1024]{1,0:T(8,128)(2,1)S(1)} %get-tuple-element.35), channel_id=1, source_target_pairs={{0,3},{1,2},{2,1},{3,0},{4,7},{5,6},{6,5},{7,4},{8,11},{9,10},{10,... | collective-permute-start | bytes 196616 | tf_op jit(solution)/shard_map/ppermute | solution.py:197
  38.0 2.8 %collective-permute-done.13.refs_1_ = bf16[32,1024]{1,0:T(8,128)(2,1)S(1)} collective-permute-done((bf16[32,1024]{1,0:T(8,128)(2,1)S(1)}, bf16[32,1024]{1,0:T(8,128)(2,1)S(1)}, u32[]{:S(2)}, u32[]{:S(2)}) %collective-permute-start.13) | collective-permute-done | bytes 65568 | tf_op jit(solution)/shard_map/ppermute | solution.py:197
  40.8 0.0 collective-permute-done.14.refs_2_
  40.8 1.7 %collective-permute-done.15.refs_3_ = bf16[32,1024]{1,0:T(8,128)(2,1)S(1)} collective-permute-done((bf16[32,1024]{1,0:T(8,128)(2,1)S(1)}, bf16[32,1024]{1,0:T(8,128)(2,1)S(1)}, u32[]{:S(2)}, u32[]{:S(2)}) %collective-permute-start.15) | collective-permute-done | bytes 65568 | tf_op jit(solution)/shard_map/ppermute | solution.py:197
  42.5 0.7 %shard_map.92 = bf16[32,1024]{1,0:T(8,128)(2,1)} custom-call(bf16[32,1024]{1,0:T(8,128)(2,1)S(1)} %get-tuple-element.25.refs_0_, bf16[32,1024]{1,0:T(8,128)(2,1)S(1)} %collective-permute-done.13.refs_1_, bf16[32,1024]{1,0:T(8,128)(2,1)S(1)} %collective-permute-done.14.refs_2_, bf16[32,1024]{1,0:T(8,128)(2,1)S(1)} %collective-permute-done.15.refs_3_, ...), custom_call_target="tpu_custom_call" | custom-call | bytes 393216 | tf_op jit(solution)/shard_map/pallas_call | solution.py:184
  (1 shorter events, 0.0 us)
Async XLA Ops:
  2.5 7.8 %collective-permute-start = (bf16[32,1152]{1,0:T(8,128)(2,1)S(1)}, bf16[32,1152]{1,0:T(8,128)(2,1)S(1)}, u32[]{:S(2)}, u32[]{:S(2)}) collective-permute-start(bf16[32,1152]{1,0:T(8,128)(2,1)S(1)} %shard_map.83), channel_id=1, source_target_pairs={{0,3},{1,2},{2,1},{3,0},{4,7},{5,6},{6,5},{7,4},{8,11},{9,10},{10,... | collective-permute-start | bytes 221192 | tf_op jit(solution)/shard_map/ppermute | solution.py:197
  8.1 1.2 %copy-start.4 = (bf16[1024]{0:T(1024)(128)(2,1)S(1)}, bf16[1024]{0:T(1024)(128)(2,1)}, u32[]{:S(2)}) copy-start(bf16[1024]{0:T(1024)(128)(2,1)} %param.15) | copy-start | bytes 6148
  8.1 5.8 %collective-permute-start.1 = (bf16[32,1152]{1,0:T(8,128)(2,1)S(1)}, bf16[32,1152]{1,0:T(8,128)(2,1)S(1)}, u32[]{:S(2)}, u32[]{:S(2)}) collective-permute-start(bf16[32,1152]{1,0:T(8,128)(2,1)S(1)} %shard_map.84), channel_id=1, source_target_pairs={{0,2},{1,3},{2,0},{3,1},{4,6},{5,7},{6,4},{7,5},{8,10},{9,11},{10,... | collective-permute-start | bytes 221192 | tf_op jit(solution)/shard_map/ppermute | solution.py:197
  8.2 18.8 %copy-start.2 = (bf16[1024,1024]{1,0:T(8,128)(2,1)S(1)}, bf16[1024,1024]{1,0:T(8,128)(2,1)}, u32[]{:S(2)}) copy-start(bf16[1024,1024]{1,0:T(8,128)(2,1)} %down_ref.1) | copy-start | bytes 6291460
  8.7 14.4 %copy-start = (bf16[1024,3,256]{2,0,1:T(8,128)(2,1)S(1)}, bf16[1024,3,256]{2,0,1:T(8,128)(2,1)}, u32[]{:S(2)}) copy-start(bf16[1024,3,256]{2,0,1:T(8,128)(2,1)} %param.11) | copy-start | bytes 4718596
  8.7 5.7 %collective-permute-start.2 = (bf16[32,1152]{1,0:T(8,128)(2,1)S(1)}, bf16[32,1152]{1,0:T(8,128)(2,1)S(1)}, u32[]{:S(2)}, u32[]{:S(2)}) collective-permute-start(bf16[32,1152]{1,0:T(8,128)(2,1)S(1)} %shard_map.85), channel_id=1, source_target_pairs={{0,1},{1,0},{2,3},{3,2},{4,5},{5,4},{6,7},{7,6},{8,9},{9,8},{10,11... | collective-permute-start | bytes 221192 | tf_op jit(solution)/shard_map/ppermute | solution.py:197
  9.4 17.7 %copy-start.1 = (bf16[1024,1024]{1,0:T(8,128)(2,1)S(1)}, bf16[1024,1024]{1,0:T(8,128)(2,1)}, u32[]{:S(2)}) copy-start(bf16[1024,1024]{1,0:T(8,128)(2,1)} %up_ref.1) | copy-start | bytes 6291460
  15.0 7.0 %collective-permute-start.5 = (bf16[32,1024]{1,0:T(8,128)(2,1)S(1)}, bf16[32,1024]{1,0:T(8,128)(2,1)S(1)}, u32[]{:S(2)}, u32[]{:S(2)}) collective-permute-start(bf16[32,1024]{1,0:T(8,128)(2,1)S(1)} %get-tuple-element.26.refs_3_), channel_id=1, source_target_pairs={{0,2},{1,3},{2,0},{3,1},{4,6},{5,7},{6,4},{7,5},{8,10},{9,11},{10,... | collective-permute-start | bytes 196616 | tf_op jit(solution)/shard_map/ppermute | solution.py:197
  16.7 6.2 %collective-permute-start.4 = (bf16[32,1024]{1,0:T(8,128)(2,1)S(1)}, bf16[32,1024]{1,0:T(8,128)(2,1)S(1)}, u32[]{:S(2)}, u32[]{:S(2)}) collective-permute-start(bf16[32,1024]{1,0:T(8,128)(2,1)S(1)} %get-tuple-element.26.refs_3_), channel_id=1, source_target_pairs={{0,3},{1,2},{2,1},{3,0},{4,7},{5,6},{6,5},{7,4},{8,11},{9,10},{10,... | collective-permute-start | bytes 196616 | tf_op jit(solution)/shard_map/ppermute | solution.py:197
  17.8 5.3 %collective-permute-start.3 = (bf16[32,1024]{1,0:T(8,128)(2,1)S(1)}, bf16[32,1024]{1,0:T(8,128)(2,1)S(1)}, u32[]{:S(2)}, u32[]{:S(2)}) collective-permute-start(bf16[32,1024]{1,0:T(8,128)(2,1)S(1)} %get-tuple-element.26.refs_3_), channel_id=1, source_target_pairs={{0,1},{1,0},{2,3},{3,2},{4,5},{5,4},{6,7},{7,6},{8,9},{9,8},{10,11... | collective-permute-start | bytes 196616 | tf_op jit(solution)/shard_map/ppermute | solution.py:197
  23.5 9.3 %copy-start.3 = (bf16[256,1024]{1,0:T(8,128)(2,1)S(1)}, bf16[256,1024]{1,0:T(8,128)(2,1)}, u32[]{:S(2)}) copy-start(bf16[256,1024]{1,0:T(8,128)(2,1)} %wo_ref.1) | copy-start | bytes 1572868
  23.5 5.9 %collective-permute-start.6 = (bf16[128,512]{1,0:T(8,128)(2,1)S(1)}, bf16[128,512]{1,0:T(8,128)(2,1)S(1)}, u32[]{:S(2)}, u32[]{:S(2)}) collective-permute-start(bf16[128,512]{1,0:T(8,128)(2,1)S(1)} %shard_map.88.kv_ref), channel_id=1, source_target_pairs={{0,24},{4,28},{8,16},{12,20},{16,8},{20,12},{24,0},{28,4},{1,25},{... | collective-permute-start | bytes 393224 | tf_op jit(solution)/shard_map/ppermute | solution.py:197
  26.0 5.0 %collective-permute-start.8 = (bf16[128,512]{1,0:T(8,128)(2,1)S(1)}, bf16[128,512]{1,0:T(8,128)(2,1)S(1)}, u32[]{:S(2)}, u32[]{:S(2)}) collective-permute-start(bf16[128,512]{1,0:T(8,128)(2,1)S(1)} %shard_map.88.kv_ref), channel_id=1, source_target_pairs={{0,8},{4,12},{8,0},{12,4},{16,24},{20,28},{24,16},{28,20},{1,9},{5... | collective-permute-start | bytes 393224 | tf_op jit(solution)/shard_map/ppermute | solution.py:197
  26.5 5.0 %collective-permute-start.7 = (bf16[128,512]{1,0:T(8,128)(2,1)S(1)}, bf16[128,512]{1,0:T(8,128)(2,1)S(1)}, u32[]{:S(2)}, u32[]{:S(2)}) collective-permute-start(bf16[128,512]{1,0:T(8,128)(2,1)S(1)} %shard_map.88.kv_ref), channel_id=1, source_target_pairs={{0,16},{4,20},{8,24},{12,28},{16,0},{20,4},{24,8},{28,12},{1,17},{... | collective-permute-start | bytes 393224 | tf_op jit(solution)/shard_map/ppermute | solution.py:197
  27.9 3.5 %collective-permute-start.9 = (bf16[128,512]{1,0:T(8,128)(2,1)S(1)}, bf16[128,512]{1,0:T(8,128)(2,1)S(1)}, u32[]{:S(2)}, u32[]{:S(2)}) collective-permute-start(bf16[128,512]{1,0:T(8,128)(2,1)S(1)} %get-tuple-element.29.refs_0_), channel_id=1, source_target_pairs={{0,4},{4,0},{8,12},{12,8},{16,20},{20,16},{24,28},{28,24},{1,5},{5... | collective-permute-start | bytes 393224 | tf_op jit(solution)/shard_map/ppermute | solution.py:197
  29.4 2.1 %collective-permute-start.10 = (bf16[128,512]{1,0:T(8,128)(2,1)S(1)}, bf16[128,512]{1,0:T(8,128)(2,1)S(1)}, u32[]{:S(2)}, u32[]{:S(2)}) collective-permute-start(bf16[128,512]{1,0:T(8,128)(2,1)S(1)} %collective-permute-done.6.refs_1_), channel_id=1, source_target_pairs={{0,4},{4,0},{8,12},{12,8},{16,20},{20,16},{24,28},{28,24},{1,5},{5... | collective-permute-start | bytes 393224 | tf_op jit(solution)/shard_map/ppermute | solution.py:197
  30.9 1.6 %collective-permute-start.12 = (bf16[128,512]{1,0:T(8,128)(2,1)S(1)}, bf16[128,512]{1,0:T(8,128)(2,1)S(1)}, u32[]{:S(2)}, u32[]{:S(2)}) collective-permute-start(bf16[128,512]{1,0:T(8,128)(2,1)S(1)} %collective-permute-done.8.refs_3_), channel_id=1, source_target_pairs={{0,4},{4,0},{8,12},{12,8},{16,20},{20,16},{24,28},{28,24},{1,5},{5... | collective-permute-start | bytes 393224 | tf_op jit(solution)/shard_map/ppermute | solution.py:197
  31.5 1.3 %collective-permute-start.11 = (bf16[128,512]{1,0:T(8,128)(2,1)S(1)}, bf16[128,512]{1,0:T(8,128)(2,1)S(1)}, u32[]{:S(2)}, u32[]{:S(2)}) collective-permute-start(bf16[128,512]{1,0:T(8,128)(2,1)S(1)} %collective-permute-done.7.refs_2_), channel_id=1, source_target_pairs={{0,4},{4,0},{8,12},{12,8},{16,20},{20,16},{24,28},{28,24},{1,5},{5... | collective-permute-start | bytes 393224 | tf_op jit(solution)/shard_map/ppermute | solution.py:197
  33.5 7.3 %collective-permute-start.13 = (bf16[32,1024]{1,0:T(8,128)(2,1)S(1)}, bf16[32,1024]{1,0:T(8,128)(2,1)S(1)}, u32[]{:S(2)}, u32[]{:S(2)}) collective-permute-start(bf16[32,1024]{1,0:T(8,128)(2,1)S(1)} %get-tuple-element.33), channel_id=1, source_target_pairs={{0,2},{1,3},{2,0},{3,1},{4,6},{5,7},{6,4},{7,5},{8,10},{9,11},{10,... | collective-permute-start | bytes 196616 | tf_op jit(solution)/shard_map/ppermute | solution.py:197
  34.9 5.9 %collective-permute-start.14 = (bf16[32,1024]{1,0:T(8,128)(2,1)S(1)}, bf16[32,1024]{1,0:T(8,128)(2,1)S(1)}, u32[]{:S(2)}, u32[]{:S(2)}) collective-permute-start(bf16[32,1024]{1,0:T(8,128)(2,1)S(1)} %get-tuple-element.34), channel_id=1, source_target_pairs={{0,1},{1,0},{2,3},{3,2},{4,5},{5,4},{6,7},{7,6},{8,9},{9,8},{10,11... | collective-permute-start | bytes 196616 | tf_op jit(solution)/shard_map/ppermute | solution.py:197
  36.4 6.1 %collective-permute-start.15 = (bf16[32,1024]{1,0:T(8,128)(2,1)S(1)}, bf16[32,1024]{1,0:T(8,128)(2,1)S(1)}, u32[]{:S(2)}, u32[]{:S(2)}) collective-permute-start(bf16[32,1024]{1,0:T(8,128)(2,1)S(1)} %get-tuple-element.35), channel_id=1, source_target_pairs={{0,3},{1,2},{2,1},{3,0},{4,7},{5,6},{6,5},{7,4},{8,11},{9,10},{10,... | collective-permute-start | bytes 196616 | tf_op jit(solution)/shard_map/ppermute | solution.py:197

commit v7 on v4

--- a/solution.py
+++ b/solution.py
@@ -100,9 +100,9 @@
     normed_ref[...] = (centered * lax.rsqrt(spread + EPS) * gain_ref[...].astype(f32)).astype(bf16)
 
 
-def qkv_kernel(w_ref, *refs):
+def qkv_kernel(order, w_ref, *refs):
     blocks, (q_ref, kv_ref, kept_ref) = refs[:-3], refs[-3:]
-    x = rows_of(blocks)
+    x = rows_of([blocks[i] for i in order])
     width = q_ref.shape[1]
     q_ref[...] = jnp.dot(x, w_ref[0], preferred_element_type=f32).astype(bf16)
     kv_ref[:, :width] = jnp.dot(x, w_ref[1], preferred_element_type=f32).astype(bf16)
@@ -110,18 +110,18 @@
     kept_ref[...] = kv_ref[...]
 
 
-def ffn_kernel(up_ref, down_ref, *refs):
+def ffn_kernel(order, up_ref, down_ref, *refs):
     blocks, out_ref = refs[:-3], refs[-2]
-    x = rows_of(blocks)
+    x = rows_of([blocks[i] for i in order])
     hidden = jnp.dot(x, up_ref[...], preferred_element_type=f32)
     hidden = jax.nn.gelu(hidden, approximate=True).astype(bf16)
     out_ref[...] = jnp.dot(hidden, down_ref[...], preferred_element_type=f32)
 
 
-def attend(heads, q_ref, blocks):
-    rows, width = q_ref.shape
+def attend(heads, q, blocks):
+    rows, width = q.shape
     head_dim = width // heads
-    q = q_ref[...].astype(f32) * head_dim ** (-0.5)
+    q = q.astype(f32) * head_dim ** (-0.5)
     owner = lax.broadcasted_iota(jnp.int32, (rows, width), 1) // head_dim
     stacked = jnp.concatenate([jnp.where(owner == h, q, 0.0) for h in range(heads)], axis=0)
     stacked = stacked.astype(bf16)
@@ -144,20 +144,22 @@
 
 def early_kernel(heads, q_ref, *refs):
     blocks, out_refs = refs[:-3], refs[-3:]
-    for ref, value in zip(out_refs, attend(heads, q_ref, blocks)):
+    for ref, value in zip(out_refs, attend(heads, q_ref[...], blocks)):
         ref[...] = value
 
 
-def attend_kernel(heads, groups, q_ref, ffn_ref, wo_ref, mixed_ref, top_ref, total_ref, *refs):
-    blocks, out_refs = refs[:-groups], refs[-groups:]
-    mixed, top, total = attend(heads, q_ref, blocks)
-    both = jnp.maximum(top, top_ref[...])
-    late, early = jnp.exp(top - both), jnp.exp(top_ref[...] - both)
-    attended = (mixed * late + mixed_ref[...] * early) / (total * late + total_ref[...] * early)
-    out = jnp.dot(attended.astype(bf16), wo_ref[...], preferred_element_type=f32) + ffn_ref[...]
-    part = out.shape[0] // groups
-    for k in range(groups):
-        out_refs[k][...] = out[k * part : (k + 1) * part].astype(bf16)
+def attend_kernel(heads, slots, q_ref, ffn_ref, wo_ref, mixed_ref, top_ref, total_ref, *refs):
+    n = len(slots)
+    blocks, out_refs = refs[:-n], refs[-n:]
+    part = out_refs[0].shape[0]
+    own = slice(slots[0] * part, (slots[-1] + 1) * part)
+    mixed, top, total = attend(heads, q_ref[own], blocks)
+    both = jnp.maximum(top, top_ref[own])
+    late, early = jnp.exp(top - both), jnp.exp(top_ref[own] - both)
+    attended = (mixed * late + mixed_ref[own] * early) / (total * late + total_ref[own] * early)
+    out = jnp.dot(attended.astype(bf16), wo_ref[...], preferred_element_type=f32) + ffn_ref[own]
+    for i, out_ref in enumerate(out_refs):
+        out_ref[...] = out[i * part : (i + 1) * part].astype(bf16)
 
 
 def add_kernel(*refs):
@@ -245,8 +247,9 @@
         norm_kernel, [shape((part, width), bf16)] * 2, norm_gain.reshape(1, width), *got, sent[-1]
     )
     blocks = [*exchange([normed] * groups, "var", groups, partners[1]), normed]
+    order = [[*partners[1], 0].index(k) for k in (*partners[2], 0)]
     q, kv, kept = call(
-        qkv_kernel,
+        functools.partial(qkv_kernel, order),
         [shape((rows, local), bf16)] + [shape((rows, 2 * local), bf16)] * 2,
         qkv_weight.transpose(1, 0, 2), *blocks,
         flops=6 * rows * width * local,
@@ -255,7 +258,8 @@
 
     def feed_forward(arrived):
         made = call(
-            ffn_kernel, [shape((rows, width), f32), shape(arrived.shape, bf16)],
+            functools.partial(ffn_kernel, order),
+            [shape((rows, width), f32), shape(arrived.shape, bf16)],
             up_weight, down_weight, *blocks, arrived,
             flops=4 * rows * width * up_weight.shape[1], aliases={2 + len(blocks): 1},
         )
@@ -268,13 +272,17 @@
         functools.partial(early_kernel, heads), [shape((rows, local), f32)] * 3, q, *early,
         flops=4 * rows * rows * len(early) * local * heads, vmem=32,
     )
-    sums = call(
-        functools.partial(attend_kernel, heads, groups),
-        [shape((part, width), bf16)] * groups,
-        q, *ffn, out_weight, *state, *late,
-        flops=4 * rows * rows * len(late) * local * heads, vmem=32,
-    )
-    by_partner = dict(zip([*partners[1], 0], sums))
+    sums = []
+    for slots in (range(groups // 2, groups), range(groups // 2)):
+        sums += call(
+            functools.partial(attend_kernel, heads, slots),
+            [shape((part, width), bf16)] * len(slots),
+            q, *ffn, out_weight, *state, *late,
+            flops=4 * part * len(slots) * sum(b.shape[0] for b in late) * local * heads, vmem=32,
+        )
+    rows_of_slots = [*partners[2], 0]
+    made_first = rows_of_slots[groups // 2 :]
+    by_partner = dict(zip(made_first + rows_of_slots[: groups // 2], sums))
     got = exchange(by_partner, "var", groups, partners[2])
     (out,) = call(
         add_kernel, [jax.ShapeDtypeStruct((part, width), bf16)], pooled, *got, by_partner[0]

time: 43.4 us -> 43.4 us (level)
  Pallas kernels: 8.31 us -> 8.87 us
  waiting for transfers between devices: 17.3 us -> 16.8 us
    pallas_call x11 -> x12, Pallas kernels: 8.31 us -> 8.87 us  [call(): pl.pallas_call(kernel, out_shape=out_shapes, in_specs=in_specs, out_specs...]
    ppermute x16, waiting for transfers between devices: 17.3 us -> 16.8 us  [exchange(): lax.ppermute(parts[k], axis, [(i, i ^ k) for i in range(size)])]
  transfers between devices with their start and end apart: 16 -> 16, of which waited for: 12 -> 12; matrix products, arithmetic and copies ran while one was open for 0% -> 0% of each run, Pallas kernels for 8% -> 10%
where the time goes in v7:
time: 43.4 us; the launch traced here: 43.3 us
  starting transfers between devices  17.5 us (40%)
  waiting for transfers between devices  16.8 us (39%)
  Pallas kernels  8.87 us (20%)
    ppermute x16, starting transfers between devices, exchange(): lax.ppermute(parts[k], axis, [(i, i ^ k) for i in range(size)])  17.5 us
    ppermute x16, waiting for transfers between devices, exchange(): lax.ppermute(parts[k], axis, [(i, i ^ k) for i in range(size)])  16.8 us
    pallas_call x12, Pallas kernels, call(): pl.pallas_call(kernel, out_shape=out_shapes, in_specs=in_specs, out_specs...  8.87 us
  transfers between devices with their start and end apart: 16, of which 12 were waited for; matrix products, arithmetic and copies ran while one was open for 0% of the time, Pallas kernels for 10%

profile of v7, /device:TPU:0, one launch (start us, length us, event | category | flops | bytes accessed | tf_op | source)
XLA Modules:
  0.0 43.3 jit_solution(9962774784070348083)
XLA Ops:
  0.0 2.0 %shard_map.82 = (bf16[4,4,32,1024]{3,2,1,0:T(8,128)(2,1)S(1)}, bf16[1024,1024]{1,0:T(8,128)(2,1)S(1)}, bf16[4,4,32,128]{3,2,1,0:T(8,128)(2,1)S(1)}, bf16[4,32,128]{2,1,0:T(8,128)(2,1)S(1)}) custom-call(bf16[4,4,32,1024]{3,2,1,0:T(8,128)(2,1)} %bitcast.4, bf16[16,1024]{1,0:T(8,128)(2,1)} %bitcast.5, bf16[1024,1024]{1,0:T(8,128)(2,1)} %wv_hbm.1), custom_call_target="tpu_custom_call" | custom-call | flops 134217728 | bytes 6488064 | tf_op jit(solution)/shard_map/pallas_call | solution.py:182
  2.0 0.5 %shard_map.83 = bf16[32,1152]{1,0:T(8,128)(2,1)S(1)} custom-call(bf16[4,4,32,1024]{3,2,1,0:T(8,128)(2,1)S(1)} %get-tuple-element.23.x_ref, bf16[1024,1024]{1,0:T(8,128)(2,1)S(1)} %get-tuple-element.24.wv_ref, bf16[4,4,32,128]{3,2,1,0:T(8,128)(2,1)S(1)} %get-tuple-element.25.share_ref, bf16[4,32,128]{2,1,0:T(8,128)(2,1)S(1)} %get-tuple-element.26.stats_ref), custom_call_target="tpu_custom_call" | custom-call | flops 268435456 | bytes 3383296 | tf_op jit(solution)/shard_map/pallas_call | solution.py:182
  2.5 5.1 %collective-permute-start = (bf16[32,1152]{1,0:T(8,128)(2,1)S(1)}, bf16[32,1152]{1,0:T(8,128)(2,1)S(1)}, u32[]{:S(2)}, u32[]{:S(2)}) collective-permute-start(bf16[32,1152]{1,0:T(8,128)(2,1)S(1)} %shard_map.83), channel_id=1, source_target_pairs={{0,3},{1,2},{2,1},{3,0},{4,7},{5,6},{6,5},{7,4},{8,11},{9,10},{10,... | collective-permute-start | bytes 221192 | tf_op jit(solution)/shard_map/ppermute | solution.py:195
  7.6 0.5 %shard_map.84 = bf16[32,1152]{1,0:T(8,128)(2,1)S(1)} custom-call(bf16[4,4,32,1024]{3,2,1,0:T(8,128)(2,1)S(1)} %get-tuple-element.23.x_ref, bf16[1024,1024]{1,0:T(8,128)(2,1)S(1)} %get-tuple-element.24.wv_ref, bf16[4,4,32,128]{3,2,1,0:T(8,128)(2,1)S(1)} %get-tuple-element.25.share_ref, bf16[4,32,128]{2,1,0:T(8,128)(2,1)S(1)} %get-tuple-element.26.stats_ref), custom_call_target="tpu_custom_call" | custom-call | flops 268435456 | bytes 3383296 | tf_op jit(solution)/shard_map/pallas_call | solution.py:182
  8.1 0.0 copy-start.4
  8.1 0.1 collective-permute-start.1
  8.2 0.0 copy-start.3
  8.2 0.5 %shard_map.85 = bf16[32,1152]{1,0:T(8,128)(2,1)S(1)} custom-call(bf16[4,4,32,1024]{3,2,1,0:T(8,128)(2,1)S(1)} %get-tuple-element.23.x_ref, bf16[1024,1024]{1,0:T(8,128)(2,1)S(1)} %get-tuple-element.24.wv_ref, bf16[4,4,32,128]{3,2,1,0:T(8,128)(2,1)S(1)} %get-tuple-element.25.share_ref, bf16[4,32,128]{2,1,0:T(8,128)(2,1)S(1)} %get-tuple-element.26.stats_ref), custom_call_target="tpu_custom_call" | custom-call | flops 268435456 | bytes 3383296 | tf_op jit(solution)/shard_map/pallas_call | solution.py:182
  8.7 0.6 %collective-permute-start.2 = (bf16[32,1152]{1,0:T(8,128)(2,1)S(1)}, bf16[32,1152]{1,0:T(8,128)(2,1)S(1)}, u32[]{:S(2)}, u32[]{:S(2)}) collective-permute-start(bf16[32,1152]{1,0:T(8,128)(2,1)S(1)} %shard_map.85), channel_id=1, source_target_pairs={{0,1},{1,0},{2,3},{3,2},{4,5},{5,4},{6,7},{7,6},{8,9},{9,8},{10,11... | collective-permute-start | bytes 221192 | tf_op jit(solution)/shard_map/ppermute | solution.py:195
  9.3 0.0 copy-done.4
  9.3 0.0 copy-start.1
  9.3 0.0 copy-start.2
  9.4 0.5 %shard_map.86.refs_3_ = bf16[32,1152]{1,0:T(8,128)(2,1)S(1)} custom-call(bf16[4,4,32,1024]{3,2,1,0:T(8,128)(2,1)S(1)} %get-tuple-element.23.x_ref, bf16[1024,1024]{1,0:T(8,128)(2,1)S(1)} %get-tuple-element.24.wv_ref, bf16[4,4,32,128]{3,2,1,0:T(8,128)(2,1)S(1)} %get-tuple-element.25.share_ref, bf16[4,32,128]{2,1,0:T(8,128)(2,1)S(1)} %get-tuple-element.26.stats_ref), custom_call_target="tpu_custom_call" | custom-call | flops 268435456 | bytes 3383296 | tf_op jit(solution)/shard_map/pallas_call | solution.py:182
  9.8 0.4 %collective-permute-done.refs_0_ = bf16[32,1152]{1,0:T(8,128)(2,1)S(1)} collective-permute-done((bf16[32,1152]{1,0:T(8,128)(2,1)S(1)}, bf16[32,1152]{1,0:T(8,128)(2,1)S(1)}, u32[]{:S(2)}, u32[]{:S(2)}) %collective-permute-start) | collective-permute-done | bytes 73760 | tf_op jit(solution)/shard_map/ppermute | solution.py:195
  10.3 3.7 %collective-permute-done.1.refs_1_ = bf16[32,1152]{1,0:T(8,128)(2,1)S(1)} collective-permute-done((bf16[32,1152]{1,0:T(8,128)(2,1)S(1)}, bf16[32,1152]{1,0:T(8,128)(2,1)S(1)}, u32[]{:S(2)}, u32[]{:S(2)}) %collective-permute-start.1) | collective-permute-done | bytes 73760 | tf_op jit(solution)/shard_map/ppermute | solution.py:195
  14.0 0.5 %collective-permute-done.2.refs_2_ = bf16[32,1152]{1,0:T(8,128)(2,1)S(1)} collective-permute-done((bf16[32,1152]{1,0:T(8,128)(2,1)S(1)}, bf16[32,1152]{1,0:T(8,128)(2,1)S(1)}, u32[]{:S(2)}, u32[]{:S(2)}) %collective-permute-start.2) | collective-permute-done | bytes 73760 | tf_op jit(solution)/shard_map/ppermute | solution.py:195
  14.5 0.6 %shard_map.87 = (bf16[32,1024]{1,0:T(8,128)(2,1)S(1)}, bf16[32,1024]{1,0:T(8,128)(2,1)S(1)}) custom-call(bf16[1,1024]{1,0:T(2,128)(2,1)S(1)} %reshape.6.gain_ref, bf16[32,1152]{1,0:T(8,128)(2,1)S(1)} %collective-permute-done.refs_0_, bf16[32,1152]{1,0:T(8,128)(2,1)S(1)} %collective-permute-done.1.refs_1_, ...), custom_call_target="tpu_custom_call" | custom-call | bytes 428032 | tf_op jit(solution)/shard_map/pallas_call | solution.py:182
  15.0 1.6 %collective-permute-start.5 = (bf16[32,1024]{1,0:T(8,128)(2,1)S(1)}, bf16[32,1024]{1,0:T(8,128)(2,1)S(1)}, u32[]{:S(2)}, u32[]{:S(2)}) collective-permute-start(bf16[32,1024]{1,0:T(8,128)(2,1)S(1)} %get-tuple-element.28.refs_3_), channel_id=1, source_target_pairs={{0,2},{1,3},{2,0},{3,1},{4,6},{5,7},{6,4},{7,5},{8,10},{9,11},{10,... | collective-permute-start | bytes 196616 | tf_op jit(solution)/shard_map/ppermute | solution.py:195
  16.7 1.2 %collective-permute-start.4 = (bf16[32,1024]{1,0:T(8,128)(2,1)S(1)}, bf16[32,1024]{1,0:T(8,128)(2,1)S(1)}, u32[]{:S(2)}, u32[]{:S(2)}) collective-permute-start(bf16[32,1024]{1,0:T(8,128)(2,1)S(1)} %get-tuple-element.28.refs_3_), channel_id=1, source_target_pairs={{0,3},{1,2},{2,1},{3,0},{4,7},{5,6},{6,5},{7,4},{8,11},{9,10},{10,... | collective-permute-start | bytes 196616 | tf_op jit(solution)/shard_map/ppermute | solution.py:195
  17.8 0.8 %collective-permute-start.3 = (bf16[32,1024]{1,0:T(8,128)(2,1)S(1)}, bf16[32,1024]{1,0:T(8,128)(2,1)S(1)}, u32[]{:S(2)}, u32[]{:S(2)}) collective-permute-start(bf16[32,1024]{1,0:T(8,128)(2,1)S(1)} %get-tuple-element.28.refs_3_), channel_id=1, source_target_pairs={{0,1},{1,0},{2,3},{3,2},{4,5},{5,4},{6,7},{7,6},{8,9},{9,8},{10,11... | collective-permute-start | bytes 196616 | tf_op jit(solution)/shard_map/ppermute | solution.py:195
  18.6 3.4 %collective-permute-done.5.refs_2_ = bf16[32,1024]{1,0:T(8,128)(2,1)S(1)} collective-permute-done((bf16[32,1024]{1,0:T(8,128)(2,1)S(1)}, bf16[32,1024]{1,0:T(8,128)(2,1)S(1)}, u32[]{:S(2)}, u32[]{:S(2)}) %collective-permute-start.5) | collective-permute-done | bytes 65568 | tf_op jit(solution)/shard_map/ppermute | solution.py:195
  22.0 0.9 %collective-permute-done.4.refs_1_ = bf16[32,1024]{1,0:T(8,128)(2,1)S(1)} collective-permute-done((bf16[32,1024]{1,0:T(8,128)(2,1)S(1)}, bf16[32,1024]{1,0:T(8,128)(2,1)S(1)}, u32[]{:S(2)}, u32[]{:S(2)}) %collective-permute-start.4) | collective-permute-done | bytes 65568 | tf_op jit(solution)/shard_map/ppermute | solution.py:195
  22.9 0.2 collective-permute-done.3.refs_0_
  23.1 0.0 copy-done.3
  23.1 0.4 shard_map.88
  23.5 2.5 %collective-permute-start.6 = (bf16[128,512]{1,0:T(8,128)(2,1)S(1)}, bf16[128,512]{1,0:T(8,128)(2,1)S(1)}, u32[]{:S(2)}, u32[]{:S(2)}) collective-permute-start(bf16[128,512]{1,0:T(8,128)(2,1)S(1)} %get-tuple-element.33), channel_id=1, source_target_pairs={{0,24},{4,28},{8,16},{12,20},{16,8},{20,12},{24,0},{28,4},{1,25},{... | collective-permute-start | bytes 393224 | tf_op jit(solution)/shard_map/ppermute | solution.py:195
  26.0 0.5 %collective-permute-start.8 = (bf16[128,512]{1,0:T(8,128)(2,1)S(1)}, bf16[128,512]{1,0:T(8,128)(2,1)S(1)}, u32[]{:S(2)}, u32[]{:S(2)}) collective-permute-start(bf16[128,512]{1,0:T(8,128)(2,1)S(1)} %get-tuple-element.33), channel_id=1, source_target_pairs={{0,8},{4,12},{8,0},{12,4},{16,24},{20,28},{24,16},{28,20},{1,9},{5... | collective-permute-start | bytes 393224 | tf_op jit(solution)/shard_map/ppermute | solution.py:195
  26.5 0.5 %collective-permute-start.7 = (bf16[128,512]{1,0:T(8,128)(2,1)S(1)}, bf16[128,512]{1,0:T(8,128)(2,1)S(1)}, u32[]{:S(2)}, u32[]{:S(2)}) collective-permute-start(bf16[128,512]{1,0:T(8,128)(2,1)S(1)} %get-tuple-element.33), channel_id=1, source_target_pairs={{0,16},{4,20},{8,24},{12,28},{16,0},{20,4},{24,8},{28,12},{1,17},{... | collective-permute-start | bytes 393224 | tf_op jit(solution)/shard_map/ppermute | solution.py:195
  27.1 0.0 copy-done.1
  27.1 0.0 copy-done.2
  27.1 0.0 copy-start
  27.1 0.8 %shard_map.89 = (f32[128,1024]{1,0:T(8,128)S(1)}, bf16[128,512]{1,0:T(8,128)(2,1)S(1)}) custom-call(bf16[1024,1024]{1,0:T(8,128)(2,1)S(1)} %copy-done.1, bf16[1024,1024]{1,0:T(8,128)(2,1)S(1)} %copy-done.2, bf16[32,1024]{1,0:T(8,128)(2,1)S(1)} %collective-permute-done.3.refs_0_, ...), custom_call_target="tpu_custom_call", output_to_operand_aliasing={{1}: (6, {})} | custom-call | flops 536870912 | bytes 5242880 | tf_op jit(solution)/shard_map/pallas_call | solution.py:182
  27.9 0.1 collective-permute-start.9
  28.0 1.4 %collective-permute-done.6.refs_1_ = bf16[128,512]{1,0:T(8,128)(2,1)S(1)} collective-permute-done((bf16[128,512]{1,0:T(8,128)(2,1)S(1)}, bf16[128,512]{1,0:T(8,128)(2,1)S(1)}, u32[]{:S(2)}, u32[]{:S(2)}) %collective-permute-start.6) | collective-permute-done | bytes 131104 | tf_op jit(solution)/shard_map/ppermute | solution.py:195
  29.5 0.0 collective-permute-start.10
  29.5 1.5 %collective-permute-done.8.refs_3_ = bf16[128,512]{1,0:T(8,128)(2,1)S(1)} collective-permute-done((bf16[128,512]{1,0:T(8,128)(2,1)S(1)}, bf16[128,512]{1,0:T(8,128)(2,1)S(1)}, u32[]{:S(2)}, u32[]{:S(2)}) %collective-permute-start.8) | collective-permute-done | bytes 131104 | tf_op jit(solution)/shard_map/ppermute | solution.py:195
  31.0 0.0 collective-permute-start.12
  31.0 0.5 %collective-permute-done.7.refs_2_ = bf16[128,512]{1,0:T(8,128)(2,1)S(1)} collective-permute-done((bf16[128,512]{1,0:T(8,128)(2,1)S(1)}, bf16[128,512]{1,0:T(8,128)(2,1)S(1)}, u32[]{:S(2)}, u32[]{:S(2)}) %collective-permute-start.7) | collective-permute-done | bytes 131104 | tf_op jit(solution)/shard_map/ppermute | solution.py:195
  31.5 0.0 collective-permute-start.11
  31.5 0.0 collective-permute-done.9.refs_4_
  31.5 0.0 collective-permute-done.10.refs_5_
  31.5 1.2 %shard_map.90 = (f32[128,256]{1,0:T(8,128)S(1)}, f32[128,256]{1,0:T(8,128)S(1)}, f32[128,256]{1,0:T(8,128)S(1)}) custom-call(bf16[128,256]{1,0:T(8,128)(2,1)S(1)} %get-tuple-element.29.q_ref, bf16[128,512]{1,0:T(8,128)(2,1)S(1)} %get-tuple-element.32.refs_0_, bf16[128,512]{1,0:T(8,128)(2,1)S(1)} %collective-permute-done.6.refs_1_, ...), custom_call_target="tpu_custom_call" | custom-call | flops 402653184 | bytes 1245184 | tf_op jit(solution)/shard_map/pallas_call | solution.py:182
  32.7 0.0 collective-permute-done.12.refs_1_
  32.7 0.2 collective-permute-done.11.refs_0_
  32.9 0.0 copy-done
  32.9 0.6 %shard_map.92 = (bf16[32,1024]{1,0:T(8,128)(2,1)S(1)}, bf16[32,1024]{1,0:T(8,128)(2,1)S(1)}) custom-call(bf16[128,256]{1,0:T(8,128)(2,1)S(1)} %get-tuple-element.29.q_ref, f32[128,1024]{1,0:T(8,128)S(1)} %get-tuple-element.31.ffn_ref, bf16[256,1024]{1,0:T(8,128)(2,1)S(1)} %copy-done, f32[128,256]{1,0:T(8,128)S(1)} %get-tuple-element.34.mixed_ref, ...), custom_call_target="tpu_custom_call" | custom-call | flops 67108864 | bytes 1900544 | tf_op jit(solution)/shard_map/pallas_call | solution.py:182
  33.5 2.3 %collective-permute-start.15 = (bf16[32,1024]{1,0:T(8,128)(2,1)S(1)}, bf16[32,1024]{1,0:T(8,128)(2,1)S(1)}, u32[]{:S(2)}, u32[]{:S(2)}) collective-permute-start(bf16[32,1024]{1,0:T(8,128)(2,1)S(1)} %get-tuple-element.39), channel_id=1, source_target_pairs={{0,3},{1,2},{2,1},{3,0},{4,7},{5,6},{6,5},{7,4},{8,11},{9,10},{10,... | collective-permute-start | bytes 196616 | tf_op jit(solution)/shard_map/ppermute | solution.py:195
  35.8 0.6 %shard_map.91 = (bf16[32,1024]{1,0:T(8,128)(2,1)S(1)}, bf16[32,1024]{1,0:T(8,128)(2,1)S(1)}) custom-call(bf16[128,256]{1,0:T(8,128)(2,1)S(1)} %get-tuple-element.29.q_ref, f32[128,1024]{1,0:T(8,128)S(1)} %get-tuple-element.31.ffn_ref, bf16[256,1024]{1,0:T(8,128)(2,1)S(1)} %copy-done, f32[128,256]{1,0:T(8,128)S(1)} %get-tuple-element.34.mixed_ref, ...), custom_call_target="tpu_custom_call" | custom-call | flops 67108864 | bytes 1900544 | tf_op jit(solution)/shard_map/pallas_call | solution.py:182
  36.4 0.4 collective-permute-start.13
  36.8 1.8 %collective-permute-start.14 = (bf16[32,1024]{1,0:T(8,128)(2,1)S(1)}, bf16[32,1024]{1,0:T(8,128)(2,1)S(1)}, u32[]{:S(2)}, u32[]{:S(2)}) collective-permute-start(bf16[32,1024]{1,0:T(8,128)(2,1)S(1)} %get-tuple-element.38), channel_id=1, source_target_pairs={{0,1},{1,0},{2,3},{3,2},{4,5},{5,4},{6,7},{7,6},{8,9},{9,8},{10,11... | collective-permute-start | bytes 196616 | tf_op jit(solution)/shard_map/ppermute | solution.py:195
  38.7 1.7 %collective-permute-done.15.refs_3_ = bf16[32,1024]{1,0:T(8,128)(2,1)S(1)} collective-permute-done((bf16[32,1024]{1,0:T(8,128)(2,1)S(1)}, bf16[32,1024]{1,0:T(8,128)(2,1)S(1)}, u32[]{:S(2)}, u32[]{:S(2)}) %collective-permute-start.15) | collective-permute-done | bytes 65568 | tf_op jit(solution)/shard_map/ppermute | solution.py:195
  40.4 2.3 %collective-permute-done.13.refs_1_ = bf16[32,1024]{1,0:T(8,128)(2,1)S(1)} collective-permute-done((bf16[32,1024]{1,0:T(8,128)(2,1)S(1)}, bf16[32,1024]{1,0:T(8,128)(2,1)S(1)}, u32[]{:S(2)}, u32[]{:S(2)}) %collective-permute-start.13) | collective-permute-done | bytes 65568 | tf_op jit(solution)/shard_map/ppermute | solution.py:195
  42.6 0.0 collective-permute-done.14.refs_2_
  42.6 0.7 %shard_map.93 = bf16[32,1024]{1,0:T(8,128)(2,1)} custom-call(bf16[32,1024]{1,0:T(8,128)(2,1)S(1)} %get-tuple-element.27.refs_0_, bf16[32,1024]{1,0:T(8,128)(2,1)S(1)} %collective-permute-done.13.refs_1_, bf16[32,1024]{1,0:T(8,128)(2,1)S(1)} %collective-permute-done.14.refs_2_, bf16[32,1024]{1,0:T(8,128)(2,1)S(1)} %collective-permute-done.15.refs_3_, ...), custom_call_target="tpu_custom_call" | custom-call | bytes 393216 | tf_op jit(solution)/shard_map/pallas_call | solution.py:182
  (1 shorter events, 0.0 us)
Async XLA Ops:
  2.5 7.8 %collective-permute-start = (bf16[32,1152]{1,0:T(8,128)(2,1)S(1)}, bf16[32,1152]{1,0:T(8,128)(2,1)S(1)}, u32[]{:S(2)}, u32[]{:S(2)}) collective-permute-start(bf16[32,1152]{1,0:T(8,128)(2,1)S(1)} %shard_map.83), channel_id=1, source_target_pairs={{0,3},{1,2},{2,1},{3,0},{4,7},{5,6},{6,5},{7,4},{8,11},{9,10},{10,... | collective-permute-start | bytes 221192 | tf_op jit(solution)/shard_map/ppermute | solution.py:195
  8.1 1.2 %copy-start.4 = (bf16[1024]{0:T(1024)(128)(2,1)S(1)}, bf16[1024]{0:T(1024)(128)(2,1)}, u32[]{:S(2)}) copy-start(bf16[1024]{0:T(1024)(128)(2,1)} %param.15) | copy-start | bytes 6148
  8.1 5.8 %collective-permute-start.1 = (bf16[32,1152]{1,0:T(8,128)(2,1)S(1)}, bf16[32,1152]{1,0:T(8,128)(2,1)S(1)}, u32[]{:S(2)}, u32[]{:S(2)}) collective-permute-start(bf16[32,1152]{1,0:T(8,128)(2,1)S(1)} %shard_map.84), channel_id=1, source_target_pairs={{0,2},{1,3},{2,0},{3,1},{4,6},{5,7},{6,4},{7,5},{8,10},{9,11},{10,... | collective-permute-start | bytes 221192 | tf_op jit(solution)/shard_map/ppermute | solution.py:195
  8.2 14.9 %copy-start.3 = (bf16[1024,3,256]{2,0,1:T(8,128)(2,1)S(1)}, bf16[1024,3,256]{2,0,1:T(8,128)(2,1)}, u32[]{:S(2)}) copy-start(bf16[1024,3,256]{2,0,1:T(8,128)(2,1)} %param.11) | copy-start | bytes 4718596
  8.7 5.7 %collective-permute-start.2 = (bf16[32,1152]{1,0:T(8,128)(2,1)S(1)}, bf16[32,1152]{1,0:T(8,128)(2,1)S(1)}, u32[]{:S(2)}, u32[]{:S(2)}) collective-permute-start(bf16[32,1152]{1,0:T(8,128)(2,1)S(1)} %shard_map.85), channel_id=1, source_target_pairs={{0,1},{1,0},{2,3},{3,2},{4,5},{5,4},{6,7},{7,6},{8,9},{9,8},{10,11... | collective-permute-start | bytes 221192 | tf_op jit(solution)/shard_map/ppermute | solution.py:195
  9.3 17.7 %copy-start.1 = (bf16[1024,1024]{1,0:T(8,128)(2,1)S(1)}, bf16[1024,1024]{1,0:T(8,128)(2,1)}, u32[]{:S(2)}) copy-start(bf16[1024,1024]{1,0:T(8,128)(2,1)} %up_ref.1) | copy-start | bytes 6291460
  9.3 17.7 %copy-start.2 = (bf16[1024,1024]{1,0:T(8,128)(2,1)S(1)}, bf16[1024,1024]{1,0:T(8,128)(2,1)}, u32[]{:S(2)}) copy-start(bf16[1024,1024]{1,0:T(8,128)(2,1)} %down_ref.1) | copy-start | bytes 6291460
  15.0 7.0 %collective-permute-start.5 = (bf16[32,1024]{1,0:T(8,128)(2,1)S(1)}, bf16[32,1024]{1,0:T(8,128)(2,1)S(1)}, u32[]{:S(2)}, u32[]{:S(2)}) collective-permute-start(bf16[32,1024]{1,0:T(8,128)(2,1)S(1)} %get-tuple-element.28.refs_3_), channel_id=1, source_target_pairs={{0,2},{1,3},{2,0},{3,1},{4,6},{5,7},{6,4},{7,5},{8,10},{9,11},{10,... | collective-permute-start | bytes 196616 | tf_op jit(solution)/shard_map/ppermute | solution.py:195
  16.7 6.2 %collective-permute-start.4 = (bf16[32,1024]{1,0:T(8,128)(2,1)S(1)}, bf16[32,1024]{1,0:T(8,128)(2,1)S(1)}, u32[]{:S(2)}, u32[]{:S(2)}) collective-permute-start(bf16[32,1024]{1,0:T(8,128)(2,1)S(1)} %get-tuple-element.28.refs_3_), channel_id=1, source_target_pairs={{0,3},{1,2},{2,1},{3,0},{4,7},{5,6},{6,5},{7,4},{8,11},{9,10},{10,... | collective-permute-start | bytes 196616 | tf_op jit(solution)/shard_map/ppermute | solution.py:195
  17.8 5.3 %collective-permute-start.3 = (bf16[32,1024]{1,0:T(8,128)(2,1)S(1)}, bf16[32,1024]{1,0:T(8,128)(2,1)S(1)}, u32[]{:S(2)}, u32[]{:S(2)}) collective-permute-start(bf16[32,1024]{1,0:T(8,128)(2,1)S(1)} %get-tuple-element.28.refs_3_), channel_id=1, source_target_pairs={{0,1},{1,0},{2,3},{3,2},{4,5},{5,4},{6,7},{7,6},{8,9},{9,8},{10,11... | collective-permute-start | bytes 196616 | tf_op jit(solution)/shard_map/ppermute | solution.py:195
  23.5 5.9 %collective-permute-start.6 = (bf16[128,512]{1,0:T(8,128)(2,1)S(1)}, bf16[128,512]{1,0:T(8,128)(2,1)S(1)}, u32[]{:S(2)}, u32[]{:S(2)}) collective-permute-start(bf16[128,512]{1,0:T(8,128)(2,1)S(1)} %get-tuple-element.33), channel_id=1, source_target_pairs={{0,24},{4,28},{8,16},{12,20},{16,8},{20,12},{24,0},{28,4},{1,25},{... | collective-permute-start | bytes 393224 | tf_op jit(solution)/shard_map/ppermute | solution.py:195
  26.0 5.0 %collective-permute-start.8 = (bf16[128,512]{1,0:T(8,128)(2,1)S(1)}, bf16[128,512]{1,0:T(8,128)(2,1)S(1)}, u32[]{:S(2)}, u32[]{:S(2)}) collective-permute-start(bf16[128,512]{1,0:T(8,128)(2,1)S(1)} %get-tuple-element.33), channel_id=1, source_target_pairs={{0,8},{4,12},{8,0},{12,4},{16,24},{20,28},{24,16},{28,20},{1,9},{5... | collective-permute-start | bytes 393224 | tf_op jit(solution)/shard_map/ppermute | solution.py:195
  26.5 5.0 %collective-permute-start.7 = (bf16[128,512]{1,0:T(8,128)(2,1)S(1)}, bf16[128,512]{1,0:T(8,128)(2,1)S(1)}, u32[]{:S(2)}, u32[]{:S(2)}) collective-permute-start(bf16[128,512]{1,0:T(8,128)(2,1)S(1)} %get-tuple-element.33), channel_id=1, source_target_pairs={{0,16},{4,20},{8,24},{12,28},{16,0},{20,4},{24,8},{28,12},{1,17},{... | collective-permute-start | bytes 393224 | tf_op jit(solution)/shard_map/ppermute | solution.py:195
  27.1 5.8 %copy-start = (bf16[256,1024]{1,0:T(8,128)(2,1)S(1)}, bf16[256,1024]{1,0:T(8,128)(2,1)}, u32[]{:S(2)}) copy-start(bf16[256,1024]{1,0:T(8,128)(2,1)} %wo_ref.3) | copy-start | bytes 1572868
  27.9 3.6 %collective-permute-start.9 = (bf16[128,512]{1,0:T(8,128)(2,1)S(1)}, bf16[128,512]{1,0:T(8,128)(2,1)S(1)}, u32[]{:S(2)}, u32[]{:S(2)}) collective-permute-start(bf16[128,512]{1,0:T(8,128)(2,1)S(1)} %get-tuple-element.32.refs_0_), channel_id=1, source_target_pairs={{0,4},{4,0},{8,12},{12,8},{16,20},{20,16},{24,28},{28,24},{1,5},{5... | collective-permute-start | bytes 393224 | tf_op jit(solution)/shard_map/ppermute | solution.py:195
  29.5 2.1 %collective-permute-start.10 = (bf16[128,512]{1,0:T(8,128)(2,1)S(1)}, bf16[128,512]{1,0:T(8,128)(2,1)S(1)}, u32[]{:S(2)}, u32[]{:S(2)}) collective-permute-start(bf16[128,512]{1,0:T(8,128)(2,1)S(1)} %collective-permute-done.6.refs_1_), channel_id=1, source_target_pairs={{0,4},{4,0},{8,12},{12,8},{16,20},{20,16},{24,28},{28,24},{1,5},{5... | collective-permute-start | bytes 393224 | tf_op jit(solution)/shard_map/ppermute | solution.py:195
  31.0 1.7 %collective-permute-start.12 = (bf16[128,512]{1,0:T(8,128)(2,1)S(1)}, bf16[128,512]{1,0:T(8,128)(2,1)S(1)}, u32[]{:S(2)}, u32[]{:S(2)}) collective-permute-start(bf16[128,512]{1,0:T(8,128)(2,1)S(1)} %collective-permute-done.8.refs_3_), channel_id=1, source_target_pairs={{0,4},{4,0},{8,12},{12,8},{16,20},{20,16},{24,28},{28,24},{1,5},{5... | collective-permute-start | bytes 393224 | tf_op jit(solution)/shard_map/ppermute | solution.py:195
  31.5 1.3 %collective-permute-start.11 = (bf16[128,512]{1,0:T(8,128)(2,1)S(1)}, bf16[128,512]{1,0:T(8,128)(2,1)S(1)}, u32[]{:S(2)}, u32[]{:S(2)}) collective-permute-start(bf16[128,512]{1,0:T(8,128)(2,1)S(1)} %collective-permute-done.7.refs_2_), channel_id=1, source_target_pairs={{0,4},{4,0},{8,12},{12,8},{16,20},{20,16},{24,28},{28,24},{1,5},{5... | collective-permute-start | bytes 393224 | tf_op jit(solution)/shard_map/ppermute | solution.py:195
  33.5 6.9 %collective-permute-start.15 = (bf16[32,1024]{1,0:T(8,128)(2,1)S(1)}, bf16[32,1024]{1,0:T(8,128)(2,1)S(1)}, u32[]{:S(2)}, u32[]{:S(2)}) collective-permute-start(bf16[32,1024]{1,0:T(8,128)(2,1)S(1)} %get-tuple-element.39), channel_id=1, source_target_pairs={{0,3},{1,2},{2,1},{3,0},{4,7},{5,6},{6,5},{7,4},{8,11},{9,10},{10,... | collective-permute-start | bytes 196616 | tf_op jit(solution)/shard_map/ppermute | solution.py:195
  36.4 6.2 %collective-permute-start.13 = (bf16[32,1024]{1,0:T(8,128)(2,1)S(1)}, bf16[32,1024]{1,0:T(8,128)(2,1)S(1)}, u32[]{:S(2)}, u32[]{:S(2)}) collective-permute-start(bf16[32,1024]{1,0:T(8,128)(2,1)S(1)} %get-tuple-element.37), channel_id=1, source_target_pairs={{0,2},{1,3},{2,0},{3,1},{4,6},{5,7},{6,4},{7,5},{8,10},{9,11},{10,... | collective-permute-start | bytes 196616 | tf_op jit(solution)/shard_map/ppermute | solution.py:195
  36.8 5.8 %collective-permute-start.14 = (bf16[32,1024]{1,0:T(8,128)(2,1)S(1)}, bf16[32,1024]{1,0:T(8,128)(2,1)S(1)}, u32[]{:S(2)}, u32[]{:S(2)}) collective-permute-start(bf16[32,1024]{1,0:T(8,128)(2,1)S(1)} %get-tuple-element.38), channel_id=1, source_target_pairs={{0,1},{1,0},{2,3},{3,2},{4,5},{5,4},{6,7},{7,6},{8,9},{9,8},{10,11... | collective-permute-start | bytes 196616 | tf_op jit(solution)/shard_map/ppermute | solution.py:195

commit v8 on v4

--- a/solution.py
+++ b/solution.py
@@ -198,7 +198,7 @@
         blocks = lax.all_gather(block, "space", axis=0, tiled=True)
         half = blocks.shape[0] // 2
         return [blocks[:half]], [blocks[half:]]
-    blocks = [kept, *exchange([block] * size, "space", size, range(size - 2, 0, -2))]
+    blocks = [kept, *exchange([block] * size, "space", size, (size - 2, *range(2, size - 2, 2)))]
     twins = [twin for b in blocks for twin in exchange([b, b], "space", size, (1,))]
     return blocks + twins[:2], twins[2:]
 

time: 43.4 us -> 43.4 us (level)
  transfers between devices with their start and end apart: 16 -> 16, of which waited for: 12 -> 11; matrix products, arithmetic and copies ran while one was open for 0% -> 0% of each run, Pallas kernels for 8% -> 8%
where the time goes in v8:
time: 43.4 us; the launch traced here: 43.3 us
  starting transfers between devices  17.8 us (41%)
  waiting for transfers between devices  17 us (39%)
  Pallas kernels  8.31 us (19%)
    ppermute x16, starting transfers between devices, exchange(): lax.ppermute(parts[k], axis, [(i, i ^ k) for i in range(size)])  17.8 us
    ppermute x16, waiting for transfers between devices, exchange(): lax.ppermute(parts[k], axis, [(i, i ^ k) for i in range(size)])  17 us
    pallas_call x11, Pallas kernels, call(): pl.pallas_call(kernel, out_shape=out_shapes, in_specs=in_specs, out_specs...  8.31 us
  transfers between devices with their start and end apart: 16, of which 11 were waited for; matrix products, arithmetic and copies ran while one was open for 0% of the time, Pallas kernels for 8%

profile of v8, /device:TPU:0, one launch (start us, length us, event | category | flops | bytes accessed | tf_op | source)
XLA Modules:
  0.0 43.3 jit_solution(17726482811045272275)
XLA Ops:
  0.0 2.0 %shard_map.82 = (bf16[4,4,32,1024]{3,2,1,0:T(8,128)(2,1)S(1)}, bf16[1024,1024]{1,0:T(8,128)(2,1)S(1)}, bf16[4,4,32,128]{3,2,1,0:T(8,128)(2,1)S(1)}, bf16[4,32,128]{2,1,0:T(8,128)(2,1)S(1)}) custom-call(bf16[4,4,32,1024]{3,2,1,0:T(8,128)(2,1)} %bitcast.4, bf16[16,1024]{1,0:T(8,128)(2,1)} %bitcast.5, bf16[1024,1024]{1,0:T(8,128)(2,1)} %wv_hbm.1), custom_call_target="tpu_custom_call" | custom-call | flops 134217728 | bytes 6488064 | tf_op jit(solution)/shard_map/pallas_call | solution.py:180
  2.0 0.5 %shard_map.83 = bf16[32,1152]{1,0:T(8,128)(2,1)S(1)} custom-call(bf16[4,4,32,1024]{3,2,1,0:T(8,128)(2,1)S(1)} %get-tuple-element.23.x_ref, bf16[1024,1024]{1,0:T(8,128)(2,1)S(1)} %get-tuple-element.24.wv_ref, bf16[4,4,32,128]{3,2,1,0:T(8,128)(2,1)S(1)} %get-tuple-element.25.share_ref, bf16[4,32,128]{2,1,0:T(8,128)(2,1)S(1)} %get-tuple-element.26.stats_ref), custom_call_target="tpu_custom_call" | custom-call | flops 268435456 | bytes 3383296 | tf_op jit(solution)/shard_map/pallas_call | solution.py:180
  2.5 5.1 %collective-permute-start = (bf16[32,1152]{1,0:T(8,128)(2,1)S(1)}, bf16[32,1152]{1,0:T(8,128)(2,1)S(1)}, u32[]{:S(2)}, u32[]{:S(2)}) collective-permute-start(bf16[32,1152]{1,0:T(8,128)(2,1)S(1)} %shard_map.83), channel_id=1, source_target_pairs={{0,3},{1,2},{2,1},{3,0},{4,7},{5,6},{6,5},{7,4},{8,11},{9,10},{10,... | collective-permute-start | bytes 221192 | tf_op jit(solution)/shard_map/ppermute | solution.py:193
  7.6 0.5 %shard_map.84 = bf16[32,1152]{1,0:T(8,128)(2,1)S(1)} custom-call(bf16[4,4,32,1024]{3,2,1,0:T(8,128)(2,1)S(1)} %get-tuple-element.23.x_ref, bf16[1024,1024]{1,0:T(8,128)(2,1)S(1)} %get-tuple-element.24.wv_ref, bf16[4,4,32,128]{3,2,1,0:T(8,128)(2,1)S(1)} %get-tuple-element.25.share_ref, bf16[4,32,128]{2,1,0:T(8,128)(2,1)S(1)} %get-tuple-element.26.stats_ref), custom_call_target="tpu_custom_call" | custom-call | flops 268435456 | bytes 3383296 | tf_op jit(solution)/shard_map/pallas_call | solution.py:180
  8.1 0.0 copy-start.4
  8.1 0.1 collective-permute-start.1
  8.2 0.0 copy-start.2
  8.2 0.5 %shard_map.85 = bf16[32,1152]{1,0:T(8,128)(2,1)S(1)} custom-call(bf16[4,4,32,1024]{3,2,1,0:T(8,128)(2,1)S(1)} %get-tuple-element.23.x_ref, bf16[1024,1024]{1,0:T(8,128)(2,1)S(1)} %get-tuple-element.24.wv_ref, bf16[4,4,32,128]{3,2,1,0:T(8,128)(2,1)S(1)} %get-tuple-element.25.share_ref, bf16[4,32,128]{2,1,0:T(8,128)(2,1)S(1)} %get-tuple-element.26.stats_ref), custom_call_target="tpu_custom_call" | custom-call | flops 268435456 | bytes 3383296 | tf_op jit(solution)/shard_map/pallas_call | solution.py:180
  8.7 0.6 %collective-permute-start.2 = (bf16[32,1152]{1,0:T(8,128)(2,1)S(1)}, bf16[32,1152]{1,0:T(8,128)(2,1)S(1)}, u32[]{:S(2)}, u32[]{:S(2)}) collective-permute-start(bf16[32,1152]{1,0:T(8,128)(2,1)S(1)} %shard_map.85), channel_id=1, source_target_pairs={{0,1},{1,0},{2,3},{3,2},{4,5},{5,4},{6,7},{7,6},{8,9},{9,8},{10,11... | collective-permute-start | bytes 221192 | tf_op jit(solution)/shard_map/ppermute | solution.py:193
  9.3 0.0 copy-done.4
  9.3 0.0 copy-start
  9.3 0.0 copy-start.1
  9.4 0.5 %shard_map.86.refs_3_ = bf16[32,1152]{1,0:T(8,128)(2,1)S(1)} custom-call(bf16[4,4,32,1024]{3,2,1,0:T(8,128)(2,1)S(1)} %get-tuple-element.23.x_ref, bf16[1024,1024]{1,0:T(8,128)(2,1)S(1)} %get-tuple-element.24.wv_ref, bf16[4,4,32,128]{3,2,1,0:T(8,128)(2,1)S(1)} %get-tuple-element.25.share_ref, bf16[4,32,128]{2,1,0:T(8,128)(2,1)S(1)} %get-tuple-element.26.stats_ref), custom_call_target="tpu_custom_call" | custom-call | flops 268435456 | bytes 3383296 | tf_op jit(solution)/shard_map/pallas_call | solution.py:180
  9.8 0.4 %collective-permute-done.refs_0_ = bf16[32,1152]{1,0:T(8,128)(2,1)S(1)} collective-permute-done((bf16[32,1152]{1,0:T(8,128)(2,1)S(1)}, bf16[32,1152]{1,0:T(8,128)(2,1)S(1)}, u32[]{:S(2)}, u32[]{:S(2)}) %collective-permute-start) | collective-permute-done | bytes 73760 | tf_op jit(solution)/shard_map/ppermute | solution.py:193
  10.3 3.7 %collective-permute-done.1.refs_1_ = bf16[32,1152]{1,0:T(8,128)(2,1)S(1)} collective-permute-done((bf16[32,1152]{1,0:T(8,128)(2,1)S(1)}, bf16[32,1152]{1,0:T(8,128)(2,1)S(1)}, u32[]{:S(2)}, u32[]{:S(2)}) %collective-permute-start.1) | collective-permute-done | bytes 73760 | tf_op jit(solution)/shard_map/ppermute | solution.py:193
  14.0 0.5 %collective-permute-done.2.refs_2_ = bf16[32,1152]{1,0:T(8,128)(2,1)S(1)} collective-permute-done((bf16[32,1152]{1,0:T(8,128)(2,1)S(1)}, bf16[32,1152]{1,0:T(8,128)(2,1)S(1)}, u32[]{:S(2)}, u32[]{:S(2)}) %collective-permute-start.2) | collective-permute-done | bytes 73760 | tf_op jit(solution)/shard_map/ppermute | solution.py:193
  14.5 0.6 %shard_map.87 = (bf16[32,1024]{1,0:T(8,128)(2,1)S(1)}, bf16[32,1024]{1,0:T(8,128)(2,1)S(1)}) custom-call(bf16[1,1024]{1,0:T(2,128)(2,1)S(1)} %reshape.6.gain_ref, bf16[32,1152]{1,0:T(8,128)(2,1)S(1)} %collective-permute-done.refs_0_, bf16[32,1152]{1,0:T(8,128)(2,1)S(1)} %collective-permute-done.1.refs_1_, ...), custom_call_target="tpu_custom_call" | custom-call | bytes 428032 | tf_op jit(solution)/shard_map/pallas_call | solution.py:180
  15.0 1.6 %collective-permute-start.5 = (bf16[32,1024]{1,0:T(8,128)(2,1)S(1)}, bf16[32,1024]{1,0:T(8,128)(2,1)S(1)}, u32[]{:S(2)}, u32[]{:S(2)}) collective-permute-start(bf16[32,1024]{1,0:T(8,128)(2,1)S(1)} %get-tuple-element.28.refs_3_), channel_id=1, source_target_pairs={{0,2},{1,3},{2,0},{3,1},{4,6},{5,7},{6,4},{7,5},{8,10},{9,11},{10,... | collective-permute-start | bytes 196616 | tf_op jit(solution)/shard_map/ppermute | solution.py:193
  16.7 1.2 %collective-permute-start.4 = (bf16[32,1024]{1,0:T(8,128)(2,1)S(1)}, bf16[32,1024]{1,0:T(8,128)(2,1)S(1)}, u32[]{:S(2)}, u32[]{:S(2)}) collective-permute-start(bf16[32,1024]{1,0:T(8,128)(2,1)S(1)} %get-tuple-element.28.refs_3_), channel_id=1, source_target_pairs={{0,3},{1,2},{2,1},{3,0},{4,7},{5,6},{6,5},{7,4},{8,11},{9,10},{10,... | collective-permute-start | bytes 196616 | tf_op jit(solution)/shard_map/ppermute | solution.py:193
  17.8 0.8 %collective-permute-start.3 = (bf16[32,1024]{1,0:T(8,128)(2,1)S(1)}, bf16[32,1024]{1,0:T(8,128)(2,1)S(1)}, u32[]{:S(2)}, u32[]{:S(2)}) collective-permute-start(bf16[32,1024]{1,0:T(8,128)(2,1)S(1)} %get-tuple-element.28.refs_3_), channel_id=1, source_target_pairs={{0,1},{1,0},{2,3},{3,2},{4,5},{5,4},{6,7},{7,6},{8,9},{9,8},{10,11... | collective-permute-start | bytes 196616 | tf_op jit(solution)/shard_map/ppermute | solution.py:193
  18.6 3.4 %collective-permute-done.5.refs_2_ = bf16[32,1024]{1,0:T(8,128)(2,1)S(1)} collective-permute-done((bf16[32,1024]{1,0:T(8,128)(2,1)S(1)}, bf16[32,1024]{1,0:T(8,128)(2,1)S(1)}, u32[]{:S(2)}, u32[]{:S(2)}) %collective-permute-start.5) | collective-permute-done | bytes 65568 | tf_op jit(solution)/shard_map/ppermute | solution.py:193
  22.0 0.9 %collective-permute-done.4.refs_1_ = bf16[32,1024]{1,0:T(8,128)(2,1)S(1)} collective-permute-done((bf16[32,1024]{1,0:T(8,128)(2,1)S(1)}, bf16[32,1024]{1,0:T(8,128)(2,1)S(1)}, u32[]{:S(2)}, u32[]{:S(2)}) %collective-permute-start.4) | collective-permute-done | bytes 65568 | tf_op jit(solution)/shard_map/ppermute | solution.py:193
  22.9 0.2 collective-permute-done.3.refs_0_
  23.1 0.0 copy-done.2
  23.1 0.4 shard_map.88
  23.5 2.5 %collective-permute-start.6 = (bf16[128,512]{1,0:T(8,128)(2,1)S(1)}, bf16[128,512]{1,0:T(8,128)(2,1)S(1)}, u32[]{:S(2)}, u32[]{:S(2)}) collective-permute-start(bf16[128,512]{1,0:T(8,128)(2,1)S(1)} %get-tuple-element.33), channel_id=1, source_target_pairs={{0,24},{4,28},{8,16},{12,20},{16,8},{20,12},{24,0},{28,4},{1,25},{... | collective-permute-start | bytes 393224 | tf_op jit(solution)/shard_map/ppermute | solution.py:193
  26.0 0.5 %collective-permute-start.8 = (bf16[128,512]{1,0:T(8,128)(2,1)S(1)}, bf16[128,512]{1,0:T(8,128)(2,1)S(1)}, u32[]{:S(2)}, u32[]{:S(2)}) collective-permute-start(bf16[128,512]{1,0:T(8,128)(2,1)S(1)} %get-tuple-element.33), channel_id=1, source_target_pairs={{0,16},{4,20},{8,24},{12,28},{16,0},{20,4},{24,8},{28,12},{1,17},{... | collective-permute-start | bytes 393224 | tf_op jit(solution)/shard_map/ppermute | solution.py:193
  26.5 0.5 %collective-permute-start.7 = (bf16[128,512]{1,0:T(8,128)(2,1)S(1)}, bf16[128,512]{1,0:T(8,128)(2,1)S(1)}, u32[]{:S(2)}, u32[]{:S(2)}) collective-permute-start(bf16[128,512]{1,0:T(8,128)(2,1)S(1)} %get-tuple-element.33), channel_id=1, source_target_pairs={{0,8},{4,12},{8,0},{12,4},{16,24},{20,28},{24,16},{28,20},{1,9},{5... | collective-permute-start | bytes 393224 | tf_op jit(solution)/shard_map/ppermute | solution.py:193
  27.1 0.0 copy-done
  27.1 0.0 copy-done.1
  27.1 0.0 copy-start.3
  27.1 0.8 %shard_map.89 = (f32[128,1024]{1,0:T(8,128)S(1)}, bf16[128,512]{1,0:T(8,128)(2,1)S(1)}) custom-call(bf16[1024,1024]{1,0:T(8,128)(2,1)S(1)} %copy-done, bf16[1024,1024]{1,0:T(8,128)(2,1)S(1)} %copy-done.1, bf16[32,1024]{1,0:T(8,128)(2,1)S(1)} %collective-permute-done.3.refs_0_, ...), custom_call_target="tpu_custom_call", output_to_operand_aliasing={{1}: (6, {})} | custom-call | flops 536870912 | bytes 5242880 | tf_op jit(solution)/shard_map/pallas_call | solution.py:180
  27.9 0.1 collective-permute-start.9
  28.0 2.0 %collective-permute-done.6.refs_1_ = bf16[128,512]{1,0:T(8,128)(2,1)S(1)} collective-permute-done((bf16[128,512]{1,0:T(8,128)(2,1)S(1)}, bf16[128,512]{1,0:T(8,128)(2,1)S(1)}, u32[]{:S(2)}, u32[]{:S(2)}) %collective-permute-start.6) | collective-permute-done | bytes 131104 | tf_op jit(solution)/shard_map/ppermute | solution.py:193
  30.0 0.0 collective-permute-start.10
  30.0 1.4 %collective-permute-done.8.refs_3_ = bf16[128,512]{1,0:T(8,128)(2,1)S(1)} collective-permute-done((bf16[128,512]{1,0:T(8,128)(2,1)S(1)}, bf16[128,512]{1,0:T(8,128)(2,1)S(1)}, u32[]{:S(2)}, u32[]{:S(2)}) %collective-permute-start.8) | collective-permute-done | bytes 131104 | tf_op jit(solution)/shard_map/ppermute | solution.py:193
  31.4 0.0 collective-permute-start.12
  31.4 0.1 collective-permute-done.7.refs_2_
  31.5 0.4 collective-permute-start.11
  31.9 0.0 collective-permute-done.9.refs_4_
  31.9 0.0 collective-permute-done.10.refs_5_
  31.9 1.2 %shard_map.90 = (f32[128,256]{1,0:T(8,128)S(1)}, f32[128,256]{1,0:T(8,128)S(1)}, f32[128,256]{1,0:T(8,128)S(1)}) custom-call(bf16[128,256]{1,0:T(8,128)(2,1)S(1)} %get-tuple-element.29.q_ref, bf16[128,512]{1,0:T(8,128)(2,1)S(1)} %get-tuple-element.32.refs_0_, bf16[128,512]{1,0:T(8,128)(2,1)S(1)} %collective-permute-done.6.refs_1_, ...), custom_call_target="tpu_custom_call" | custom-call | flops 402653184 | bytes 1245184 | tf_op jit(solution)/shard_map/pallas_call | solution.py:180
  33.1 0.0 collective-permute-done.12.refs_1_
  33.1 0.0 collective-permute-done.11.refs_0_
  33.1 0.0 copy-done.3
  33.1 0.7 %shard_map.91 = (bf16[32,1024]{1,0:T(8,128)(2,1)S(1)}, bf16[32,1024]{1,0:T(8,128)(2,1)S(1)}, bf16[32,1024]{1,0:T(8,128)(2,1)S(1)}, bf16[32,1024]{1,0:T(8,128)(2,1)S(1)}) custom-call(bf16[128,256]{1,0:T(8,128)(2,1)S(1)} %get-tuple-element.29.q_ref, f32[128,1024]{1,0:T(8,128)S(1)} %get-tuple-element.31.ffn_ref, bf16[256,1024]{1,0:T(8,128)(2,1)S(1)} %copy-done.3, ...), custom_call_target="tpu_custom_call" | custom-call | flops 134217728 | bytes 2031616 | tf_op jit(solution)/shard_map/pallas_call | solution.py:180
  33.8 1.6 %collective-permute-start.13 = (bf16[32,1024]{1,0:T(8,128)(2,1)S(1)}, bf16[32,1024]{1,0:T(8,128)(2,1)S(1)}, u32[]{:S(2)}, u32[]{:S(2)}) collective-permute-start(bf16[32,1024]{1,0:T(8,128)(2,1)S(1)} %get-tuple-element.37), channel_id=1, source_target_pairs={{0,2},{1,3},{2,0},{3,1},{4,6},{5,7},{6,4},{7,5},{8,10},{9,11},{10,... | collective-permute-start | bytes 196616 | tf_op jit(solution)/shard_map/ppermute | solution.py:193
  35.4 1.0 %collective-permute-start.14 = (bf16[32,1024]{1,0:T(8,128)(2,1)S(1)}, bf16[32,1024]{1,0:T(8,128)(2,1)S(1)}, u32[]{:S(2)}, u32[]{:S(2)}) collective-permute-start(bf16[32,1024]{1,0:T(8,128)(2,1)S(1)} %get-tuple-element.38), channel_id=1, source_target_pairs={{0,1},{1,0},{2,3},{3,2},{4,5},{5,4},{6,7},{7,6},{8,9},{9,8},{10,11... | collective-permute-start | bytes 196616 | tf_op jit(solution)/shard_map/ppermute | solution.py:193
  36.5 1.8 %collective-permute-start.15 = (bf16[32,1024]{1,0:T(8,128)(2,1)S(1)}, bf16[32,1024]{1,0:T(8,128)(2,1)S(1)}, u32[]{:S(2)}, u32[]{:S(2)}) collective-permute-start(bf16[32,1024]{1,0:T(8,128)(2,1)S(1)} %get-tuple-element.39), channel_id=1, source_target_pairs={{0,3},{1,2},{2,1},{3,0},{4,7},{5,6},{6,5},{7,4},{8,11},{9,10},{10,... | collective-permute-start | bytes 196616 | tf_op jit(solution)/shard_map/ppermute | solution.py:193
  38.3 2.8 %collective-permute-done.13.refs_1_ = bf16[32,1024]{1,0:T(8,128)(2,1)S(1)} collective-permute-done((bf16[32,1024]{1,0:T(8,128)(2,1)S(1)}, bf16[32,1024]{1,0:T(8,128)(2,1)S(1)}, u32[]{:S(2)}, u32[]{:S(2)}) %collective-permute-start.13) | collective-permute-done | bytes 65568 | tf_op jit(solution)/shard_map/ppermute | solution.py:193
  41.1 0.0 collective-permute-done.14.refs_2_
  41.1 1.5 %collective-permute-done.15.refs_3_ = bf16[32,1024]{1,0:T(8,128)(2,1)S(1)} collective-permute-done((bf16[32,1024]{1,0:T(8,128)(2,1)S(1)}, bf16[32,1024]{1,0:T(8,128)(2,1)S(1)}, u32[]{:S(2)}, u32[]{:S(2)}) %collective-permute-start.15) | collective-permute-done | bytes 65568 | tf_op jit(solution)/shard_map/ppermute | solution.py:193
  42.6 0.7 %shard_map.92 = bf16[32,1024]{1,0:T(8,128)(2,1)} custom-call(bf16[32,1024]{1,0:T(8,128)(2,1)S(1)} %get-tuple-element.27.refs_0_, bf16[32,1024]{1,0:T(8,128)(2,1)S(1)} %collective-permute-done.13.refs_1_, bf16[32,1024]{1,0:T(8,128)(2,1)S(1)} %collective-permute-done.14.refs_2_, bf16[32,1024]{1,0:T(8,128)(2,1)S(1)} %collective-permute-done.15.refs_3_, ...), custom_call_target="tpu_custom_call" | custom-call | bytes 393216 | tf_op jit(solution)/shard_map/pallas_call | solution.py:180
  (1 shorter events, 0.0 us)
Async XLA Ops:
  2.5 7.8 %collective-permute-start = (bf16[32,1152]{1,0:T(8,128)(2,1)S(1)}, bf16[32,1152]{1,0:T(8,128)(2,1)S(1)}, u32[]{:S(2)}, u32[]{:S(2)}) collective-permute-start(bf16[32,1152]{1,0:T(8,128)(2,1)S(1)} %shard_map.83), channel_id=1, source_target_pairs={{0,3},{1,2},{2,1},{3,0},{4,7},{5,6},{6,5},{7,4},{8,11},{9,10},{10,... | collective-permute-start | bytes 221192 | tf_op jit(solution)/shard_map/ppermute | solution.py:193
  8.1 1.2 %copy-start.4 = (bf16[1024]{0:T(1024)(128)(2,1)S(1)}, bf16[1024]{0:T(1024)(128)(2,1)}, u32[]{:S(2)}) copy-start(bf16[1024]{0:T(1024)(128)(2,1)} %param.15) | copy-start | bytes 6148
  8.1 5.8 %collective-permute-start.1 = (bf16[32,1152]{1,0:T(8,128)(2,1)S(1)}, bf16[32,1152]{1,0:T(8,128)(2,1)S(1)}, u32[]{:S(2)}, u32[]{:S(2)}) collective-permute-start(bf16[32,1152]{1,0:T(8,128)(2,1)S(1)} %shard_map.84), channel_id=1, source_target_pairs={{0,2},{1,3},{2,0},{3,1},{4,6},{5,7},{6,4},{7,5},{8,10},{9,11},{10,... | collective-permute-start | bytes 221192 | tf_op jit(solution)/shard_map/ppermute | solution.py:193
  8.2 14.9 %copy-start.2 = (bf16[1024,3,256]{2,0,1:T(8,128)(2,1)S(1)}, bf16[1024,3,256]{2,0,1:T(8,128)(2,1)}, u32[]{:S(2)}) copy-start(bf16[1024,3,256]{2,0,1:T(8,128)(2,1)} %param.11) | copy-start | bytes 4718596
  8.7 5.7 %collective-permute-start.2 = (bf16[32,1152]{1,0:T(8,128)(2,1)S(1)}, bf16[32,1152]{1,0:T(8,128)(2,1)S(1)}, u32[]{:S(2)}, u32[]{:S(2)}) collective-permute-start(bf16[32,1152]{1,0:T(8,128)(2,1)S(1)} %shard_map.85), channel_id=1, source_target_pairs={{0,1},{1,0},{2,3},{3,2},{4,5},{5,4},{6,7},{7,6},{8,9},{9,8},{10,11... | collective-permute-start | bytes 221192 | tf_op jit(solution)/shard_map/ppermute | solution.py:193
  9.3 17.7 %copy-start = (bf16[1024,1024]{1,0:T(8,128)(2,1)S(1)}, bf16[1024,1024]{1,0:T(8,128)(2,1)}, u32[]{:S(2)}) copy-start(bf16[1024,1024]{1,0:T(8,128)(2,1)} %up_ref.1) | copy-start | bytes 6291460
  9.3 17.7 %copy-start.1 = (bf16[1024,1024]{1,0:T(8,128)(2,1)S(1)}, bf16[1024,1024]{1,0:T(8,128)(2,1)}, u32[]{:S(2)}) copy-start(bf16[1024,1024]{1,0:T(8,128)(2,1)} %down_ref.1) | copy-start | bytes 6291460
  15.0 7.0 %collective-permute-start.5 = (bf16[32,1024]{1,0:T(8,128)(2,1)S(1)}, bf16[32,1024]{1,0:T(8,128)(2,1)S(1)}, u32[]{:S(2)}, u32[]{:S(2)}) collective-permute-start(bf16[32,1024]{1,0:T(8,128)(2,1)S(1)} %get-tuple-element.28.refs_3_), channel_id=1, source_target_pairs={{0,2},{1,3},{2,0},{3,1},{4,6},{5,7},{6,4},{7,5},{8,10},{9,11},{10,... | collective-permute-start | bytes 196616 | tf_op jit(solution)/shard_map/ppermute | solution.py:193
  16.7 6.2 %collective-permute-start.4 = (bf16[32,1024]{1,0:T(8,128)(2,1)S(1)}, bf16[32,1024]{1,0:T(8,128)(2,1)S(1)}, u32[]{:S(2)}, u32[]{:S(2)}) collective-permute-start(bf16[32,1024]{1,0:T(8,128)(2,1)S(1)} %get-tuple-element.28.refs_3_), channel_id=1, source_target_pairs={{0,3},{1,2},{2,1},{3,0},{4,7},{5,6},{6,5},{7,4},{8,11},{9,10},{10,... | collective-permute-start | bytes 196616 | tf_op jit(solution)/shard_map/ppermute | solution.py:193
  17.8 5.3 %collective-permute-start.3 = (bf16[32,1024]{1,0:T(8,128)(2,1)S(1)}, bf16[32,1024]{1,0:T(8,128)(2,1)S(1)}, u32[]{:S(2)}, u32[]{:S(2)}) collective-permute-start(bf16[32,1024]{1,0:T(8,128)(2,1)S(1)} %get-tuple-element.28.refs_3_), channel_id=1, source_target_pairs={{0,1},{1,0},{2,3},{3,2},{4,5},{5,4},{6,7},{7,6},{8,9},{9,8},{10,11... | collective-permute-start | bytes 196616 | tf_op jit(solution)/shard_map/ppermute | solution.py:193
  23.5 6.5 %collective-permute-start.6 = (bf16[128,512]{1,0:T(8,128)(2,1)S(1)}, bf16[128,512]{1,0:T(8,128)(2,1)S(1)}, u32[]{:S(2)}, u32[]{:S(2)}) collective-permute-start(bf16[128,512]{1,0:T(8,128)(2,1)S(1)} %get-tuple-element.33), channel_id=1, source_target_pairs={{0,24},{4,28},{8,16},{12,20},{16,8},{20,12},{24,0},{28,4},{1,25},{... | collective-permute-start | bytes 393224 | tf_op jit(solution)/shard_map/ppermute | solution.py:193
  26.0 5.4 %collective-permute-start.8 = (bf16[128,512]{1,0:T(8,128)(2,1)S(1)}, bf16[128,512]{1,0:T(8,128)(2,1)S(1)}, u32[]{:S(2)}, u32[]{:S(2)}) collective-permute-start(bf16[128,512]{1,0:T(8,128)(2,1)S(1)} %get-tuple-element.33), channel_id=1, source_target_pairs={{0,16},{4,20},{8,24},{12,28},{16,0},{20,4},{24,8},{28,12},{1,17},{... | collective-permute-start | bytes 393224 | tf_op jit(solution)/shard_map/ppermute | solution.py:193
  26.5 5.0 %collective-permute-start.7 = (bf16[128,512]{1,0:T(8,128)(2,1)S(1)}, bf16[128,512]{1,0:T(8,128)(2,1)S(1)}, u32[]{:S(2)}, u32[]{:S(2)}) collective-permute-start(bf16[128,512]{1,0:T(8,128)(2,1)S(1)} %get-tuple-element.33), channel_id=1, source_target_pairs={{0,8},{4,12},{8,0},{12,4},{16,24},{20,28},{24,16},{28,20},{1,9},{5... | collective-permute-start | bytes 393224 | tf_op jit(solution)/shard_map/ppermute | solution.py:193
  27.1 6.0 %copy-start.3 = (bf16[256,1024]{1,0:T(8,128)(2,1)S(1)}, bf16[256,1024]{1,0:T(8,128)(2,1)}, u32[]{:S(2)}) copy-start(bf16[256,1024]{1,0:T(8,128)(2,1)} %wo_ref.1) | copy-start | bytes 1572868
  27.9 4.0 %collective-permute-start.9 = (bf16[128,512]{1,0:T(8,128)(2,1)S(1)}, bf16[128,512]{1,0:T(8,128)(2,1)S(1)}, u32[]{:S(2)}, u32[]{:S(2)}) collective-permute-start(bf16[128,512]{1,0:T(8,128)(2,1)S(1)} %get-tuple-element.32.refs_0_), channel_id=1, source_target_pairs={{0,4},{4,0},{8,12},{12,8},{16,20},{20,16},{24,28},{28,24},{1,5},{5... | collective-permute-start | bytes 393224 | tf_op jit(solution)/shard_map/ppermute | solution.py:193
  30.0 1.9 %collective-permute-start.10 = (bf16[128,512]{1,0:T(8,128)(2,1)S(1)}, bf16[128,512]{1,0:T(8,128)(2,1)S(1)}, u32[]{:S(2)}, u32[]{:S(2)}) collective-permute-start(bf16[128,512]{1,0:T(8,128)(2,1)S(1)} %collective-permute-done.6.refs_1_), channel_id=1, source_target_pairs={{0,4},{4,0},{8,12},{12,8},{16,20},{20,16},{24,28},{28,24},{1,5},{5... | collective-permute-start | bytes 393224 | tf_op jit(solution)/shard_map/ppermute | solution.py:193
  31.4 1.7 %collective-permute-start.12 = (bf16[128,512]{1,0:T(8,128)(2,1)S(1)}, bf16[128,512]{1,0:T(8,128)(2,1)S(1)}, u32[]{:S(2)}, u32[]{:S(2)}) collective-permute-start(bf16[128,512]{1,0:T(8,128)(2,1)S(1)} %collective-permute-done.8.refs_3_), channel_id=1, source_target_pairs={{0,4},{4,0},{8,12},{12,8},{16,20},{20,16},{24,28},{28,24},{1,5},{5... | collective-permute-start | bytes 393224 | tf_op jit(solution)/shard_map/ppermute | solution.py:193
  31.5 1.6 %collective-permute-start.11 = (bf16[128,512]{1,0:T(8,128)(2,1)S(1)}, bf16[128,512]{1,0:T(8,128)(2,1)S(1)}, u32[]{:S(2)}, u32[]{:S(2)}) collective-permute-start(bf16[128,512]{1,0:T(8,128)(2,1)S(1)} %collective-permute-done.7.refs_2_), channel_id=1, source_target_pairs={{0,4},{4,0},{8,12},{12,8},{16,20},{20,16},{24,28},{28,24},{1,5},{5... | collective-permute-start | bytes 393224 | tf_op jit(solution)/shard_map/ppermute | solution.py:193
  33.8 7.2 %collective-permute-start.13 = (bf16[32,1024]{1,0:T(8,128)(2,1)S(1)}, bf16[32,1024]{1,0:T(8,128)(2,1)S(1)}, u32[]{:S(2)}, u32[]{:S(2)}) collective-permute-start(bf16[32,1024]{1,0:T(8,128)(2,1)S(1)} %get-tuple-element.37), channel_id=1, source_target_pairs={{0,2},{1,3},{2,0},{3,1},{4,6},{5,7},{6,4},{7,5},{8,10},{9,11},{10,... | collective-permute-start | bytes 196616 | tf_op jit(solution)/shard_map/ppermute | solution.py:193
  35.4 5.6 %collective-permute-start.14 = (bf16[32,1024]{1,0:T(8,128)(2,1)S(1)}, bf16[32,1024]{1,0:T(8,128)(2,1)S(1)}, u32[]{:S(2)}, u32[]{:S(2)}) collective-permute-start(bf16[32,1024]{1,0:T(8,128)(2,1)S(1)} %get-tuple-element.38), channel_id=1, source_target_pairs={{0,1},{1,0},{2,3},{3,2},{4,5},{5,4},{6,7},{7,6},{8,9},{9,8},{10,11... | collective-permute-start | bytes 196616 | tf_op jit(solution)/shard_map/ppermute | solution.py:193
  36.5 6.1 %collective-permute-start.15 = (bf16[32,1024]{1,0:T(8,128)(2,1)S(1)}, bf16[32,1024]{1,0:T(8,128)(2,1)S(1)}, u32[]{:S(2)}, u32[]{:S(2)}) collective-permute-start(bf16[32,1024]{1,0:T(8,128)(2,1)S(1)} %get-tuple-element.39), channel_id=1, source_target_pairs={{0,3},{1,2},{2,1},{3,0},{4,7},{5,6},{6,5},{7,4},{8,11},{9,10},{10,... | collective-permute-start | bytes 196616 | tf_op jit(solution)/shard_map/ppermute | solution.py:193
